TPU v7x, 32 devices: a whole 2x2x4 slice. The times are simulated.
32 devices in a mesh: replica: 2 (over x), fsdp: 16 (over z, y, core).
Axes of the slice: x: 2, y: 2, z: 4, core: 2. Of those that a mesh axis runs over, the one named last changes fastest.
Arguments:
- tokens: bfloat16 [32768, 768], P(('replica', 'fsdp')), may hold values from -6 to 6
- lengths: int32 [64, 8], P(('replica', 'fsdp')), may hold values from 1 to 128, 512 in all within a row
- w_qkv: bfloat16 [768, 2304], P('fsdp'), may hold values from -0.21875 to 0.21875
- bias_qv: bfloat16 [1536], P('fsdp'), may hold values from -1.75 to 1.75
- w_out: bfloat16 [768, 768], P('fsdp'), may hold values from -0.875 to 0.875
- bias_out: bfloat16 [768], P('fsdp'), may hold values from -1.75 to 1.75
- gain_one: bfloat16 [768], P('fsdp'), may hold values from 0.5 to 1.5
- shift_one: bfloat16 [768], P('fsdp'), may hold values from -1.75 to 1.75
- w_up: bfloat16 [768, 3072], P('fsdp'), may hold values from -0.21875 to 0.21875
- bias_up: bfloat16 [3072], P('fsdp'), may hold values from -1.75 to 1.75
- w_down: bfloat16 [3072, 768], P('fsdp'), may hold values from -0.15625 to 0.15625
- bias_down: bfloat16 [768], P('fsdp'), may hold values from -1.75 to 1.75
- gain_two: bfloat16 [768], P('fsdp'), may hold values from 0.5 to 1.5
- shift_two: bfloat16 [768], P('fsdp'), may hold values from -1.75 to 1.75
- cotangent: bfloat16 [32768, 768], P(('replica', 'fsdp')), may hold values from -6 to 6
Outputs:
- layer_out: bfloat16 [32768, 768], P(('replica', 'fsdp'))
- input_grad: float32 [32768, 768], P(('replica', 'fsdp'))
- pooled: float32 [64, 8, 768], replicated
- grad_w_qkv: float32 [768, 2304], P('fsdp')
- grad_bias_qv: float32 [1536], P('fsdp')
- grad_w_out: float32 [768, 768], P('fsdp')
- grad_bias_out: float32 [768], P('fsdp')
- grad_gain_one: float32 [768], P('fsdp')
- grad_shift_one: float32 [768], P('fsdp')
- grad_w_up: float32 [768, 3072], P('fsdp')
- grad_bias_up: float32 [3072], P('fsdp')
- grad_w_down: float32 [3072, 768], P('fsdp')
- grad_bias_down: float32 [768], P('fsdp')
- grad_gain_two: float32 [768], P('fsdp')
- grad_shift_two: float32 [768], P('fsdp')
Inputs may be any that keep to these rules, and one draw needn't show every extreme that they name: The sentence lengths of each row sum to 512, and each row has a sentence of exactly 128 tokens.
All inputs are finite; a program needn't handle non-finite values.
Results may differ from a plain program's by a relative error of at most 0.015.
Values may be sent and summed in bfloat16 or wider, within the bound.
No kernel may reach another device: no remote copies, remote signals or barrier semaphores. Data moves between devices by JAX's collectives and lax.ppermute only.
A program may use at most 192 MiB of HBM per device.

v0:
```python
import jax
import jax.numpy as jnp
from jax import lax
from jax.sharding import PartitionSpec as P

D = 768
H = 12
HD = 64
SEQ = 512
SEGS = 8


epsilon = 1e-12
root_half = 0.7071067811865476
masked_score = -1e30


def layer_norm(values, gain, shift):
    centered = values - jnp.mean(values, axis=-1, keepdims=True)
    variance = jnp.mean(centered * centered, axis=-1, keepdims=True)
    return centered * lax.rsqrt(variance + epsilon) * gain + shift


def gelu(values):
    return 0.5 * values * (1.0 + lax.erf(values * root_half))


def inner_rows(left, right):
    return lax.dot_general(
        left, right, (((0,), (0,)), ((), ())), preferred_element_type=jnp.float32
    )


def times_transpose(left, right):
    return lax.dot_general(
        left, right, (((1,), (1,)), ((), ())), preferred_element_type=jnp.float32
    )


def segment_ids(lengths):
    segment_ends = jnp.cumsum(lengths, axis=1)
    places = jnp.arange(SEQ, dtype=jnp.int32)
    return jnp.sum((places[None, :, None] >= segment_ends[:, None, :]).astype(jnp.int32), axis=2)


def split_heads(row_block):
    token_count = row_block.shape[0]
    queries = row_block[:, :D].reshape(token_count, H, HD)
    key_rows = row_block[:, D : 2 * D].reshape(token_count, H, HD)
    value_rows = row_block[:, 2 * D :].reshape(token_count, H, HD)
    return (queries, key_rows, value_rows)


def row_scores(queries, key_rows, segment):
    scores = jnp.einsum(
        "qhd,khd->hqk", queries, key_rows, preferred_element_type=jnp.float32
    ) * HD ** (-0.5)
    same_segment = segment[:, None] == segment[None, :]
    return jnp.where(same_segment[None], scores, masked_score)


def attend_forward(inputs):
    row_block, segment = inputs
    queries, key_rows, value_rows = split_heads(row_block)
    scores = row_scores(queries, key_rows, segment)
    highest_score = jnp.max(scores, axis=-1, keepdims=True)
    weights = jnp.exp(scores - highest_score)
    denominator = jnp.sum(weights, axis=-1, keepdims=True)
    probabilities = (weights / denominator).astype(jnp.bfloat16)
    mixed = jnp.einsum(
        "hqk,khd->qhd", probabilities, value_rows, preferred_element_type=jnp.float32
    )
    log_total = (highest_score + jnp.log(denominator))[:, :, 0]
    return (mixed.reshape(row_block.shape[0], D).astype(jnp.bfloat16), log_total)


def attend_backward(inputs):
    row_block, segment, log_total, grad_mixed = inputs
    token_count = row_block.shape[0]
    queries, key_rows, value_rows = split_heads(row_block)
    grad_heads = grad_mixed.reshape(token_count, H, HD)
    scores = row_scores(queries, key_rows, segment)
    probabilities = jnp.exp(scores - log_total[:, :, None])
    grad_probs = jnp.einsum(
        "qhd,khd->hqk", grad_heads, value_rows, preferred_element_type=jnp.float32
    )
    row_delta = jnp.sum(probabilities * grad_probs, axis=-1, keepdims=True)
    grad_scores = (probabilities * (grad_probs - row_delta)).astype(jnp.bfloat16)
    score_scale = HD ** (-0.5)
    grad_queries = (
        jnp.einsum("hqk,khd->qhd", grad_scores, key_rows, preferred_element_type=jnp.float32)
        * score_scale
    )
    grad_keys = (
        jnp.einsum("hqk,qhd->khd", grad_scores, queries, preferred_element_type=jnp.float32)
        * score_scale
    )
    grad_values = jnp.einsum(
        "hqk,qhd->khd",
        probabilities.astype(jnp.bfloat16),
        grad_heads,
        preferred_element_type=jnp.float32,
    )
    joined = jnp.concatenate(
        [
            grad_queries.reshape(token_count, D),
            grad_keys.reshape(token_count, D),
            grad_values.reshape(token_count, D),
        ],
        axis=1,
    )
    return joined.astype(jnp.bfloat16)


def forward(tokens, segments, params):
    (
        w_qkv,
        bias_qv,
        w_out,
        bias_out,
        gain_one,
        shift_one,
        w_up,
        bias_up,
        w_down,
        bias_down,
        gain_two,
        shift_two,
    ) = params
    row_count = segments.shape[0]
    bias_full = jnp.concatenate(
        [
            bias_qv[:D].astype(jnp.float32),
            jnp.zeros((D,), jnp.float32),
            bias_qv[D:].astype(jnp.float32),
        ]
    )
    projected = (jnp.dot(tokens, w_qkv, preferred_element_type=jnp.float32) + bias_full).astype(
        jnp.bfloat16
    )
    mixed, log_total = lax.map(attend_forward, (projected.reshape(row_count, SEQ, 3 * D), segments))
    mixed = mixed.reshape(row_count * SEQ, D)
    first = tokens.astype(jnp.float32) + (
        jnp.dot(mixed, w_out, preferred_element_type=jnp.float32) + bias_out.astype(jnp.float32)
    )
    normed = layer_norm(first, gain_one.astype(jnp.float32), shift_one.astype(jnp.float32))
    normed_low = normed.astype(jnp.bfloat16)
    upper = jnp.dot(normed_low, w_up, preferred_element_type=jnp.float32) + bias_up.astype(
        jnp.float32
    )
    active = gelu(upper).astype(jnp.bfloat16)
    second = normed + (
        jnp.dot(active, w_down, preferred_element_type=jnp.float32) + bias_down.astype(jnp.float32)
    )
    result = layer_norm(second, gain_two.astype(jnp.float32), shift_two.astype(jnp.float32))
    return (
        result.astype(jnp.bfloat16),
        (projected, mixed, log_total, first, normed_low, upper, active, second),
    )


def backward(tokens, segments, params, kept, cotangent):
    (
        w_qkv,
        bias_qv,
        w_out,
        bias_out,
        gain_one,
        shift_one,
        w_up,
        bias_up,
        w_down,
        bias_down,
        gain_two,
        shift_two,
    ) = params
    projected, mixed, log_total, first, normed_low, upper, active, second = kept
    row_count = segments.shape[0]
    unused_two, pull_two = jax.vjp(
        layer_norm, second, gain_two.astype(jnp.float32), shift_two.astype(jnp.float32)
    )
    grad_second, grad_gain_two, grad_shift_two = pull_two(cotangent.astype(jnp.float32))
    grad_down = grad_second.astype(jnp.bfloat16)
    grad_w_down = inner_rows(active, grad_down)
    grad_bias_down = jnp.sum(grad_down.astype(jnp.float32), axis=0)
    grad_active = times_transpose(grad_down, w_down)
    unused_gelu, pull_gelu = jax.vjp(gelu, upper)
    grad_upper = pull_gelu(grad_active)[0].astype(jnp.bfloat16)
    grad_w_up = inner_rows(normed_low, grad_upper)
    grad_bias_up = jnp.sum(grad_upper.astype(jnp.float32), axis=0)
    grad_normed = grad_second + times_transpose(grad_upper, w_up)
    unused_one, pull_one = jax.vjp(
        layer_norm, first, gain_one.astype(jnp.float32), shift_one.astype(jnp.float32)
    )
    grad_first, grad_gain_one, grad_shift_one = pull_one(grad_normed)
    grad_attended = grad_first.astype(jnp.bfloat16)
    grad_w_out = inner_rows(mixed, grad_attended)
    grad_bias_out = jnp.sum(grad_attended.astype(jnp.float32), axis=0)
    grad_mixed = times_transpose(grad_attended, w_out).astype(jnp.bfloat16)
    grad_projected = lax.map(
        attend_backward,
        (
            projected.reshape(row_count, SEQ, 3 * D),
            segments,
            log_total,
            grad_mixed.reshape(row_count, SEQ, D),
        ),
    )
    grad_projected = grad_projected.reshape(row_count * SEQ, 3 * D)
    grad_w_qkv = inner_rows(tokens, grad_projected)
    column_sums = jnp.sum(grad_projected.astype(jnp.float32), axis=0)
    grad_bias_qv = jnp.concatenate([column_sums[:D], column_sums[2 * D :]])
    input_grad = grad_first + times_transpose(grad_projected, w_qkv)
    grads = (
        grad_w_qkv,
        grad_bias_qv,
        grad_w_out,
        grad_bias_out,
        grad_gain_one,
        grad_shift_one,
        grad_w_up,
        grad_bias_up,
        grad_w_down,
        grad_bias_down,
        grad_gain_two,
        grad_shift_two,
    )
    return (input_grad, grads)


def body(
    tokens,
    lengths,
    w_qkv,
    bias_qv,
    w_out,
    bias_out,
    gain_one,
    shift_one,
    w_up,
    bias_up,
    w_down,
    bias_down,
    gain_two,
    shift_two,
    cotangent,
):
    segments = segment_ids(lengths)
    gathered = (
        lax.all_gather(w_qkv, "fsdp", axis=0, tiled=True),
        lax.all_gather(bias_qv, "fsdp", axis=0, tiled=True),
        lax.all_gather(w_out, "fsdp", axis=0, tiled=True),
        lax.all_gather(bias_out, "fsdp", axis=0, tiled=True),
        lax.all_gather(gain_one, "fsdp", axis=0, tiled=True),
        lax.all_gather(shift_one, "fsdp", axis=0, tiled=True),
        lax.all_gather(w_up, "fsdp", axis=0, tiled=True),
        lax.all_gather(bias_up, "fsdp", axis=0, tiled=True),
        lax.all_gather(w_down, "fsdp", axis=0, tiled=True),
        lax.all_gather(bias_down, "fsdp", axis=0, tiled=True),
        lax.all_gather(gain_two, "fsdp", axis=0, tiled=True),
        lax.all_gather(shift_two, "fsdp", axis=0, tiled=True),
    )
    layer_out, kept = forward(tokens, segments, gathered)
    params = (
        lax.all_gather(w_qkv, "fsdp", axis=0, tiled=True),
        lax.all_gather(bias_qv, "fsdp", axis=0, tiled=True),
        lax.all_gather(w_out, "fsdp", axis=0, tiled=True),
        lax.all_gather(bias_out, "fsdp", axis=0, tiled=True),
        lax.all_gather(gain_one, "fsdp", axis=0, tiled=True),
        lax.all_gather(shift_one, "fsdp", axis=0, tiled=True),
        lax.all_gather(w_up, "fsdp", axis=0, tiled=True),
        lax.all_gather(bias_up, "fsdp", axis=0, tiled=True),
        lax.all_gather(w_down, "fsdp", axis=0, tiled=True),
        lax.all_gather(bias_down, "fsdp", axis=0, tiled=True),
        lax.all_gather(gain_two, "fsdp", axis=0, tiled=True),
        lax.all_gather(shift_two, "fsdp", axis=0, tiled=True),
    )
    ignored, kept = forward(tokens, segments, params)
    input_grad, grads = backward(tokens, segments, params, kept, cotangent)
    (
        term_qkv,
        term_bias_qv,
        term_out,
        term_bias_out,
        term_gain_one,
        term_shift_one,
        term_up,
        term_bias_up,
        term_down,
        term_bias_down,
        term_gain_two,
        term_shift_two,
    ) = grads
    shards = (
        lax.psum_scatter(term_qkv, "fsdp", scatter_dimension=0, tiled=True),
        lax.psum_scatter(term_bias_qv, "fsdp", scatter_dimension=0, tiled=True),
        lax.psum_scatter(term_out, "fsdp", scatter_dimension=0, tiled=True),
        lax.psum_scatter(term_bias_out, "fsdp", scatter_dimension=0, tiled=True),
        lax.psum_scatter(term_gain_one, "fsdp", scatter_dimension=0, tiled=True),
        lax.psum_scatter(term_shift_one, "fsdp", scatter_dimension=0, tiled=True),
        lax.psum_scatter(term_up, "fsdp", scatter_dimension=0, tiled=True),
        lax.psum_scatter(term_bias_up, "fsdp", scatter_dimension=0, tiled=True),
        lax.psum_scatter(term_down, "fsdp", scatter_dimension=0, tiled=True),
        lax.psum_scatter(term_bias_down, "fsdp", scatter_dimension=0, tiled=True),
        lax.psum_scatter(term_gain_two, "fsdp", scatter_dimension=0, tiled=True),
        lax.psum_scatter(term_shift_two, "fsdp", scatter_dimension=0, tiled=True),
    )
    (
        shard_qkv,
        shard_bias_qv,
        shard_out,
        shard_bias_out,
        shard_gain_one,
        shard_shift_one,
        shard_up,
        shard_bias_up,
        shard_down,
        shard_bias_down,
        shard_gain_two,
        shard_shift_two,
    ) = shards
    summed = (
        lax.psum(shard_qkv.astype(jnp.bfloat16), "replica").astype(jnp.float32),
        lax.psum(shard_bias_qv.astype(jnp.bfloat16), "replica").astype(jnp.float32),
        lax.psum(shard_out.astype(jnp.bfloat16), "replica").astype(jnp.float32),
        lax.psum(shard_bias_out.astype(jnp.bfloat16), "replica").astype(jnp.float32),
        lax.psum(shard_gain_one.astype(jnp.bfloat16), "replica").astype(jnp.float32),
        lax.psum(shard_shift_one.astype(jnp.bfloat16), "replica").astype(jnp.float32),
        lax.psum(shard_up.astype(jnp.bfloat16), "replica").astype(jnp.float32),
        lax.psum(shard_bias_up.astype(jnp.bfloat16), "replica").astype(jnp.float32),
        lax.psum(shard_down.astype(jnp.bfloat16), "replica").astype(jnp.float32),
        lax.psum(shard_bias_down.astype(jnp.bfloat16), "replica").astype(jnp.float32),
        lax.psum(shard_gain_two.astype(jnp.bfloat16), "replica").astype(jnp.float32),
        lax.psum(shard_shift_two.astype(jnp.bfloat16), "replica").astype(jnp.float32),
    )
    row_count = segments.shape[0]
    member = (segments[:, None, :] == jnp.arange(SEGS, dtype=jnp.int32)[None, :, None]).astype(
        jnp.bfloat16
    )
    sentence_sums = jnp.einsum(
        "mgp,mpl->mgl",
        member,
        layer_out.reshape(row_count, SEQ, D),
        preferred_element_type=jnp.float32,
    )
    pooled = sentence_sums / lengths.astype(jnp.float32)[:, :, None]
    pooled_all = lax.all_gather(
        pooled.astype(jnp.bfloat16), ("replica", "fsdp"), axis=0, tiled=True
    ).astype(pooled.dtype)
    return (
        layer_out,
        input_grad,
        pooled_all,
        summed[0],
        summed[1],
        summed[2],
        summed[3],
        summed[4],
        summed[5],
        summed[6],
        summed[7],
        summed[8],
        summed[9],
        summed[10],
        summed[11],
    )


def solution(mesh):
    return jax.shard_map(
        body,
        mesh=mesh,
        in_specs=(
            P(("replica", "fsdp"), None),
            P(("replica", "fsdp"), None),
            P("fsdp", None),
            P("fsdp"),
            P("fsdp", None),
            P("fsdp"),
            P("fsdp"),
            P("fsdp"),
            P("fsdp", None),
            P("fsdp"),
            P("fsdp", None),
            P("fsdp"),
            P("fsdp"),
            P("fsdp"),
            P(("replica", "fsdp"), None),
        ),
        out_specs=(
            P(("replica", "fsdp"), None),
            P(("replica", "fsdp"), None),
            P(),
            P("fsdp", None),
            P("fsdp"),
            P("fsdp", None),
            P("fsdp"),
            P("fsdp"),
            P("fsdp"),
            P("fsdp", None),
            P("fsdp"),
            P("fsdp", None),
            P("fsdp"),
            P("fsdp"),
            P("fsdp"),
        ),
        check_vma=False,
    )
```

profile of v0, /device:TPU:20, one launch (start us, length us, event | category | flops | bytes accessed | tf_op | source)
XLA Modules:
  0.0 767.5 jit_solution(8567511061273146843)
XLA Ops:
  20.1 47.7 %all-reduce.17 = (bf16[1536]{0:T(1024)(128)(2,1)S(1)}, bf16[768]{0:T(1024)(128)(2,1)S(1)}, bf16[768]{0:T(1024)(128)(2,1)S(1)}, bf16[768]{0:T(1024)(128)(2,1)S(1)...) all-reduce(bf16[1536]{0:T(1024)(128)(2,1)S(1)} %dynamic-update-slic, ...), channel_id=1, replica_groups=mesh['replica'=2,'fsdp'=16] {'fsdp'}, use_global_device_ids=true, to_apply=%add | all-reduce | flops 9216 | bytes 36864
  72.3 8.4 %add_convert_fusion.1 = bf16[1024,2304]{1,0:T(8,128)(2,1)} fusion(bf16[1024,768]{1,0:T(8,128)(2,1)} %param.21, bf16[768,2304]{1,0:T(8,128)(2,1)} %all-gather.5.cloned.1.call-done, f32[2304]{0:T(1024)S(1)} %pad_maximum_fusion), kind=kOutput, calls=%fused_computation.54 | convolution fusion | flops 3628597248 | bytes 9839616 | tf_op jit(solution)/shard_map/dot_general | solution.py:138
  88.6 34.5 %while.32 = (s32[]{:T(128)}, bf16[2,512,768]{2,1,0:T(8,128)(2,1)}, bf16[2,512,2304]{1,2,0:T(8,128)(2,1)}, s32[2,512]{1,0:T(2,128)S(1)}, s32[]{:T(128)}) while((s32[]{:T(128)}, bf16[2,512,768]{2,1,0:T(8,128)(2,1)}, bf16[2,512,2304]{1,2,0:T(8,128)(2,1)}, s32[2,512]{1,0:T(2,128)S(1)}, s32[]{:T(128)}) %tuple.108), condition=%wide.region_5.6_spmd, body=%wide.region_2.5_spmd.sunk | while | flops 824836608 | bytes 54057088 | solution.py:141
  90.9 7.6 fusion.149
  108.1 7.6 fusion.149
  129.3 22.2 %while.33 = (s32[]{:T(128)}, bf16[2,512,768]{2,1,0:T(8,128)(2,1)S(1)}, f32[2,12,512]{2,1,0:T(8,128)S(1)}, bf16[2,512,2304]{1,2,0:T(8,128)(2,1)}, s32[2,512]{1,0:T(2,128)S(1)}, /*index=5*/s32[]{:T(128)}) while((s32[]{:T(128)}, bf16[2,512,768]{2,1,0:T(8,128)(2,1)S(1)}, f32[2,12,512]{2,1,0:T(8,128)S(1)}, bf16[2,512,2304]{1,2,0:T(8,128)(2,1)}, ...), condition=%wide.region_13.14_spmd, body=%wide.region_10.13_spmd.sunk | while | flops 843704320 | bytes 54753364 | solution.py:141
  157.0 48.9 %all-gather.9.cloned.1.call-done = bf16[768,3072]{1,0:T(8,128)(2,1)} async-done(((bf16[48,3072]{1,0:T(8,128)(2,1)}), bf16[768,3072]{1,0:T(8,128)(2,1)}) %all-gather.9.cloned.1.call-update) | async-done | bytes 4718608 | tf_op jit(solution)/shard_map/all_gather | solution.py:256
  206.0 17.6 %fusion.69 = (f32[1024]{0:T(1024)S(1)}, f32[1024,768]{1,0:T(8,128)}) fusion(f32[768]{0:T(1024)S(1)} %copy-done.34, bf16[3072,768]{1,0:T(8,128)(2,1)} %all-gather.11.cloned.1.call-done, f32[3072]{0:T(1024)S(1)} %copy-done.32, bf16[768,3072]{1,0:T(8,128)(2,1)} %all-gather.9.cloned.1.call-done, f32[1024,768]{1,0:T(8,128)} %copy-done.9, ...), kind=kOutput, calls=%fused_computation.141 | convolution fusion | flops 9691986944 | bytes 15762432 | tf_op jit(solution)/shard_map/dot_general | solution.py:153
  223.6 12.1 %multiply_convert_fusion.3 = (bf16[1024,3072]{1,0:T(8,128)(2,1)S(1)}, f32[1024,3072]{1,0:T(8,128)}) fusion(f32[3072]{0:T(1024)S(1)} %copy-done.32, bf16[768,3072]{1,0:T(8,128)(2,1)} %all-gather.9.cloned.1.call-done, f32[1024,768]{1,0:T(8,128)S(1)} %get-tuple-element.316, f32[1024]{0:T(1024)S(1)} %fusion.49, f32[1024]{0:T(1024)S(1)} %broadcast_multiply_fusion.1, ...), kind=kOutput, calls=%fused_computation.50 | convolution fusion | flops 4854644736 | bytes 26765312 | tf_op jit(solution)/shard_map/dot_general | solution.py:148
  249.1 15.5 %convert_reduce_fusion = (f32[3072]{0:T(1024)}, bf16[1024,3072]{1,0:T(8,128)(2,1)S(1)}) fusion(bf16[1024,768]{1,0:T(8,128)(2,1)S(1)} %get-tuple-element.286, bf16[3072,768]{1,0:T(8,128)(2,1)S(1)} %copy-done.38, f32[1024,3072]{1,0:T(8,128)} %get-tuple-element.318, f32[3072]{0:T(1024)S(1)} %copy-done.32), kind=kOutput, calls=%fused_computation.48 | convolution fusion | flops 4882166784 | bytes 25190400 | tf_op jit(solution)/shard_map/dot_general | solution.py:35
  280.6 78.3 %while.34 = (s32[]{:T(128)}, bf16[2,512,2304]{1,2,0:T(8,128)(2,1)}, bf16[2,512,2304]{1,2,0:T(8,128)(2,1)}, s32[2,512]{1,0:T(2,128)S(1)}, f32[2,12,512]{2,1,0:T(8...) while((s32[]{:T(128)}, bf16[2,512,2304]{1,2,0:T(8,128)(2,1)}, bf16[2,512,2304]{1,2,0:T(8,128)(2,1)}, ...), condition=%wide.region_24.25_spmd, body=%wide.region_22.24_spmd.sunk | while | flops 2069751808 | bytes 164805328 | solution.py:200
  291.9 11.1 %multiply_reduce_fusion.8 = (f32[12,512]{1,0:T(8,128)S(1)}, f32[12,512,512]{1,2,0:T(8,128)}) fusion(f32[12,512,512]{1,2,0:T(8,128)} %fusion.169, f32[12,512]{1,0:T(8,128)S(1)} %dynamic-slice_bitcast_fusion.11, pred[512,512]{0,1:T(8,128)(4,1)S(1)} %broadcast_compare_fusion.8, bf16[512,12,64]{0,2,1:T(8,128)(2,1)S(1)} %bitcast.181, ...), kind=kOutput, calls=%fused_computation.32.clone.1 | convolution fusion | flops 418375680 | bytes 27049984 | tf_op jit(solution)/shard_map/while/body/eval_jaxpr/qhd,khd->hqk/dot_general | solution.py:84
  305.0 7.3 multiply_convert_fusion.11
  331.2 11.0 %multiply_reduce_fusion.8 = (f32[12,512]{1,0:T(8,128)S(1)}, f32[12,512,512]{1,2,0:T(8,128)}) fusion(f32[12,512,512]{1,2,0:T(8,128)} %fusion.169, f32[12,512]{1,0:T(8,128)S(1)} %dynamic-slice_bitcast_fusion.11, pred[512,512]{0,1:T(8,128)(4,1)S(1)} %broadcast_compare_fusion.8, bf16[512,12,64]{0,2,1:T(8,128)(2,1)S(1)} %bitcast.181, ...), kind=kOutput, calls=%fused_computation.32.clone.1 | convolution fusion | flops 418375680 | bytes 27049984 | tf_op jit(solution)/shard_map/while/body/eval_jaxpr/qhd,khd->hqk/dot_general | solution.py:84
  365.8 8.2 %convolution_bitcast_fusion = f32[768,2304]{0,1:T(8,128)} fusion(bf16[1024,2304]{1,0:T(8,128)(2,1)} %bitcast.193, bf16[1024,768]{1,0:T(8,128)(2,1)S(1)} %copy-done.39), kind=kOutput, calls=%fused_computation.56 | convolution fusion | flops 3623878656 | bytes 13369344 | tf_op jit(solution)/shard_map/dot_general | solution.py:29
  373.9 8.1 %copy.94 = f32[768,2304]{1,0:T(8,128)} copy(f32[768,2304]{0,1:T(8,128)} %convolution_bitcast_fusion) | data formatting | bytes 14155776
  383.9 10.9 %fusion.54 = f32[768,3072]{1,0:T(8,128)} fusion(bf16[1024,3072]{1,0:T(8,128)(2,1)} %copy-done.6, f32[1024,768]{1,0:T(8,128)S(1)} %copy-done.1, f32[1024]{0:T(1024)S(1)} %copy-done.19, f32[1024]{0:T(1024)S(1)} %copy-done.17, f32[768]{0:T(1024)S(1)} %copy-done.23, f32[768]{0:T(1024)S(1)} %copy-done.21), kind=kOutput, calls=%fused_computation.128 | convolution fusion | flops 4835770368 | bytes 18888704 | tf_op jit(solution)/shard_map/dot_general | solution.py:29
  396.4 10.7 %fusion.74 = f32[3072,768]{1,0:T(8,128)} fusion(bf16[1024,3072]{1,0:T(8,128)(2,1)} %copy-done.41, bf16[1024,768]{1,0:T(8,128)(2,1)S(1)} %copy-done.15), kind=kOutput, calls=%fused_computation.144 | convolution fusion | flops 4831838208 | bytes 17301504 | tf_op jit(solution)/shard_map/dot_general | solution.py:29
  412.8 48.5 %all-reduce.16 = (bf16[1536]{0:T(1024)(128)(2,1)S(1)}, bf16[768]{0:T(1024)(128)(2,1)S(1)}, bf16[768]{0:T(1024)(128)(2,1)S(1)}, bf16[768]{0:T(1024)(128)(2,1)S(1)...) all-reduce(f32[1536]{0:T(1024)S(1)} %pad_maximum_fusion.1, ...), channel_id=3, replica_groups=mesh['replica'=2,'fsdp'=16] {'fsdp'}, use_global_device_ids=true, to_apply=%region_28.29.clone | all-reduce | flops 9216 | bytes 55296
  471.3 49.6 %all_gather.62 = bf16[64,8,768]{2,1,0:T(8,128)(2,1)S(1)} all-gather(bf16[2,8,768]{2,1,0:T(8,128)(2,1)S(1)} %fusion.47), channel_id=1, replica_groups=mesh['replica'=2,'fsdp'=16] {'replica','fsdp'}, dimensions={0}, use_global_device_ids=true | all-gather | bytes 811008 | tf_op jit(solution)/shard_map/all_gather | solution.py:347
  526.0 62.8 %reduce-scatter.9.cloned.1.call-done = f32[48,3072]{1,0:T(8,128)} async-done(((f32[768,3072]{1,0:T(8,128)}), f32[48,3072]{1,0:T(8,128)}) %reduce-scatter.9.cloned.1.call-update) | async-done | bytes 589840 | tf_op jit(solution)/shard_map/reduce_scatter | solution.py:301
  590.6 114.0 %reduce-scatter.11.cloned.1.call-done = f32[192,768]{1,0:T(8,128)} async-done(((f32[3072,768]{1,0:T(8,128)}), f32[192,768]{1,0:T(8,128)}) %reduce-scatter.11.cloned.1.call-update) | async-done | bytes 589840 | tf_op jit(solution)/shard_map/reduce_scatter | solution.py:303
  706.5 9.0 %add_add_fusion.4 = f32[1024,768]{1,0:T(8,128)} fusion(f32[1024,768]{1,0:T(8,128)S(1)} %copy-done.3, bf16[1024,2304]{1,0:T(8,128)(2,1)} %bitcast.194, bf16[768,2304]{1,0:T(8,128)(2,1)} %all-gather.5.cloned.1.call-done, f32[1024]{0:T(1024)S(1)} %copy-done.26), kind=kOutput, calls=%fused_computation.81 | convolution fusion | flops 3625451520 | bytes 14553088 | tf_op jit(solution)/shard_map/dot_general | solution.py:35
  715.4 37.9 %all-reduce.22.cloned.1.call-done = (bf16[48,2304]{0,1:T(8,128)(2,1)}, bf16[48,768]{1,0:T(8,128)(2,1)}, bf16[48,3072]{1,0:T(8,128)(2,1)}, bf16[192,768]{1,0:T(8,128)(2,1)}) async-done(((bf16[48,2304]{0,1:T(8,128)(2,1)}, bf16[48,768]{1,0:T(8,128)(2,1)}, bf16[48,3072]{1,0:T(8,128)(2,1)}, bf16[192,768]{1,0:T(8,128)(2,1)}), (bf16[48,2304]{0,1:T(8,128)(2,1)}, bf16[48,768]{1,0:T(8,128)(2,1)}, ...) | async-done | bytes 884752 | tf_op jit(solution)/shard_map/psum | solution.py:323
  (283 shorter events, 193.3 us)
Async XLA Ops:
  7.2 65.1 %all-gather.5.cloned.1.call-start = ((), (), s32[]{:S(2)}) async-start(), calls=%async_computation.4 | async-start | bytes 3760128 | tf_op jit(solution)/shard_map/all_gather | solution.py:250
  7.9 115.3 %all-gather.7.cloned.1.call-start = ((), (), s32[]{:S(2)}) async-start(), calls=%async_computation.5 | async-start | bytes 1253376 | tf_op jit(solution)/shard_map/all_gather | solution.py:252
  8.7 148.4 %all-gather.11.cloned.1.call-start = ((), (), s32[]{:S(2)}) async-start(), calls=%async_computation.7 | async-start | bytes 5013504 | tf_op jit(solution)/shard_map/all_gather | solution.py:258
  9.4 196.6 %all-gather.9.cloned.1.call-start = ((), (), s32[]{:S(2)}) async-start(), calls=%async_computation.6 | async-start | bytes 5013504 | tf_op jit(solution)/shard_map/all_gather | solution.py:256
  10.0 512.2 %reduce-scatter.7.cloned.1.call-start = ((), (), s32[]{:S(2)}) async-start(), calls=%async_computation.8 | async-start | bytes 2506752 | tf_op jit(solution)/shard_map/reduce_scatter | solution.py:297
  156.4 114.6 %copy-start = (f32[1024,768]{1,0:T(8,128)}, f32[1024,768]{1,0:T(8,128)S(1)}, u32[]{:S(2)}) copy-start(f32[1024,768]{1,0:T(8,128)S(1)} %get-tuple-element.316) | copy-start | bytes 9437188
  156.4 49.5 %copy-start.20 = (f32[768]{0:T(1024)S(1)}, f32[768]{0:T(1024)}, u32[]{:S(2)}) copy-start(f32[768]{0:T(1024)} %convert_element_type.230) | copy-start | bytes 9220
  156.4 49.5 %copy-start.22 = (f32[768]{0:T(1024)S(1)}, f32[768]{0:T(1024)}, u32[]{:S(2)}) copy-start(f32[768]{0:T(1024)} %convert_element_type.231) | copy-start | bytes 9220
  156.4 49.5 %copy-start.32 = (f32[3072]{0:T(1024)S(1)}, f32[3072]{0:T(1024)}, u32[]{:S(2)}) copy-start(f32[3072]{0:T(1024)} %convert_element_type.233) | copy-start | bytes 36868
  156.4 49.5 %copy-start.34 = (f32[768]{0:T(1024)S(1)}, f32[768]{0:T(1024)}, u32[]{:S(2)}) copy-start(f32[768]{0:T(1024)} %convert_element_type.235) | copy-start | bytes 9220
  156.5 114.6 %copy-start.16 = (f32[1024]{0:T(1024)}, f32[1024]{0:T(1024)S(1)}, u32[]{:S(2)}) copy-start(f32[1024]{0:T(1024)S(1)} %broadcast_multiply_fusion.1) | copy-start | bytes 12292
  157.0 114.1 %copy-start.18 = (f32[1024]{0:T(1024)}, f32[1024]{0:T(1024)S(1)}, u32[]{:S(2)}) copy-start(f32[1024]{0:T(1024)S(1)} %fusion.49) | copy-start | bytes 12292
  248.2 16.4 %slice-start.3 = ((s8[4718592]{0:T(1024)(128)(4,1)}), s8[4194304]{0:T(1024)(128)(4,1)S(1)}, s32[]{:S(2)}) async-start(s8[4718592]{0:T(1024)(128)(4,1)} %bitcast.202), calls=%async_computation.16 | async-start | bytes 8388608
  249.1 15.5 %copy-start.14 = (bf16[1024,768]{1,0:T(8,128)(2,1)}, bf16[1024,768]{1,0:T(8,128)(2,1)S(1)}, u32[]{:S(2)}) copy-start(bf16[1024,768]{1,0:T(8,128)(2,1)S(1)} %get-tuple-element.286) | copy-start | bytes 4718596
  249.1 15.5 %slice-start.4 = ((s8[4718592]{0:T(1024)(128)(4,1)}), s8[524288]{0:T(1024)(128)(4,1)S(1)}, s32[]{:S(2)}) async-start(s8[4718592]{0:T(1024)(128)(4,1)} %bitcast.202), calls=%async_computation.17 | async-start | bytes 1048576
  278.0 246.0 %reduce-scatter.13.cloned.1.call-start = ((), (), s32[]{:S(2)}) async-start(), calls=%async_computation.11 | async-start | bytes 7520256
  291.9 13.1 %slice-start.2 = ((s8[12582912]{0:T(1024)(128)(4,1)}), s8[4194304]{0:T(1024)(128)(4,1)S(1)}, s32[]{:S(2)}) async-start(s8[12582912]{0:T(1024)(128)(4,1)} %bitcast.171), calls=%async_computation.15 | async-start | bytes 8388608 | tf_op jit(solution)/shard_map/while
  331.2 12.7 %slice-start.2 = ((s8[12582912]{0:T(1024)(128)(4,1)}), s8[4194304]{0:T(1024)(128)(4,1)S(1)}, s32[]{:S(2)}) async-start(s8[12582912]{0:T(1024)(128)(4,1)} %bitcast.171), calls=%async_computation.15 | async-start | bytes 8388608 | tf_op jit(solution)/shard_map/while
  382.1 206.8 %reduce-scatter.9.cloned.1.call-start = ((), (), s32[]{:S(2)}) async-start(), calls=%async_computation.9 | async-start | bytes 10027008 | tf_op jit(solution)/shard_map/reduce_scatter | solution.py:301
  394.9 309.8 %reduce-scatter.11.cloned.1.call-start = ((), (), s32[]{:S(2)}) async-start(), calls=%async_computation.10 | async-start | bytes 10027008 | tf_op jit(solution)/shard_map/reduce_scatter | solution.py:303
  407.1 63.8 %copy-start.8 = (bf16[1024,768]{1,0:T(8,128)(2,1)S(1)}, bf16[1024,768]{1,0:T(8,128)(2,1)}, u32[]{:S(2)}) copy-start(bf16[1024,768]{1,0:T(8,128)(2,1)} %get-tuple-element.310) | copy-start | bytes 4718596
  407.2 346.2 %all-reduce.22.cloned.1.call-start = ((), (), s32[]{:S(2)}) async-start(), calls=%async_computation.12 | async-start | bytes 2506752 | tf_op jit(solution)/shard_map/psum | solution.py:323
  520.9 185.6 %copy-start.3 = (f32[1024,768]{1,0:T(8,128)S(1)}, f32[1024,768]{1,0:T(8,128)}, u32[]{:S(2)}) copy-start(f32[1024,768]{1,0:T(8,128)} %copy-done.2) | copy-start | bytes 9437188
  520.9 185.6 %copy-start.26 = (f32[1024]{0:T(1024)S(1)}, f32[1024]{0:T(1024)}, u32[]{:S(2)}) copy-start(f32[1024]{0:T(1024)} %copy-done.25) | copy-start | bytes 12292
  (38 other events, 178.6 us)
Sparse Core Ops, SparseCore 0:
  10.3 47.5 all-gather.4
  60.1 36.3 all-gather.6
  98.9 52.8 all-gather.10
  153.9 51.9 all-gather.8
  278.1 62.0 reduce-scatter.6
  382.2 90.4 reduce-scatter.12
  476.7 112.0 reduce-scatter.8
  593.5 111.0 reduce-scatter.10
  708.3 45.0 all-reduce.21
where the time goes:
time: 779 us; the launch traced here: 768 us
  waiting for transfers between devices  266 us (34%)
  matrix products  203 us (26%)
  blocking collectives  151 us (19%)
  local copies, waits for them, and re-layouts  69.4 us (9%)
  other arithmetic  57.4 us (7%)
  between operations  18.8 us (2%)
    reduce_scatter x1, waiting for transfers between devices, body(): lax.psum_scatter(term_down, 'fsdp', scatter_dimension=0, tiled=True)  114 us
    unnamed x2, blocking collectives  96.1 us
    reduce_scatter x1, waiting for transfers between devices, body(): lax.psum_scatter(term_up, 'fsdp', scatter_dimension=0, tiled=True)  62.8 us
    all_gather x1, blocking collectives, body(): lax.all_gather(pooled.astype(jnp.bfloat16), ('replica', 'fsdp'), axis=0,...  49.6 us
    all_gather x1, waiting for transfers between devices, body(): lax.all_gather(w_up, 'fsdp', axis=0, tiled=True)  48.9 us
    psum x1, waiting for transfers between devices, body(): lax.psum(shard_qkv.astype(jnp.bfloat16), 'replica').astype(jnp.float32)  37.9 us
    dot_general x4, matrix products, times_transpose(): lax.dot_general(left, right, (((1,), (1,)), ((), ())), preferred_element_...  33.4 us
    dot_general x4, matrix products, inner_rows(): lax.dot_general(left, right, (((0,), (0,)), ((), ())), preferred_element_...  32.6 us
  transfers between devices with their start and end apart: 9, of which 4 were waited for; matrix products, arithmetic and copies ran while one was open for 31% of the time, Pallas kernels for 0%

commit v1 on v0

v1 whole, which is shorter than its diff:
```python
import functools

import jax
import jax.numpy as jnp
from jax import lax
from jax.experimental import pallas as pl
from jax.experimental.pallas import tpu as pltpu
from jax.sharding import PartitionSpec as P

D = 768
H = 12
HD = 64
FF = 3072
SEQ = 512
SEGS = 8
GROUPS = 3
GW = D // GROUPS
PAIRS = GW // 128
BLOCK = 128
BLOCKS = SEQ // BLOCK
WIDE = 3 * BLOCK

epsilon = 1e-12
root_half = 0.7071067811865476
masked_score = -1e30
pdf_scale = 0.3989422804014327

BF = jnp.bfloat16
F32 = jnp.float32
VMEM_LIMIT = 56 * 2**20


def dot(a, b):
    return jnp.dot(a, b, preferred_element_type=F32)


def dot_t(a, b):
    return lax.dot_general(a, b, (((1,), (1,)), ((), ())), preferred_element_type=F32)


def t_dot(a, b):
    return lax.dot_general(a, b, (((0,), (0,)), ((), ())), preferred_element_type=F32)


def window(qb):
    return max(0, (qb - 1) * BLOCK), min(SEQ, (qb + 2) * BLOCK)


def call(kernel, grid, in_specs, out_specs, out_shape, flops, nbytes, scratch=(), prefetch=0):
    return pl.pallas_call(
        kernel,
        grid_spec=pltpu.PrefetchScalarGridSpec(
            num_scalar_prefetch=prefetch,
            grid=grid,
            in_specs=in_specs,
            out_specs=out_specs,
            scratch_shapes=list(scratch),
        ),
        out_shape=out_shape,
        compiler_params=pltpu.CompilerParams(vmem_limit_bytes=VMEM_LIMIT),
        cost_estimate=pl.CostEstimate(flops=flops, bytes_accessed=nbytes, transcendentals=0),
    )


def shaped(shape, dtype):
    return jax.ShapeDtypeStruct(shape, dtype)


def whole(shape):
    return pl.BlockSpec(shape, lambda *_: (0,) * len(shape), pipeline_mode=pl.Buffered(1))


def segment_of(places, lengths_ref, row):
    total = jnp.int32(0)
    segment = jnp.zeros(places.shape, jnp.int32)
    for s in range(SEGS):
        total = total + lengths_ref[row, s]
        segment = segment + (places >= total).astype(jnp.int32)
    return segment


def attend_forward_kernel(
    lengths_ref, tok_ref, wq_ref, wk_ref, wv_ref, bias_ref, q_ref, k_ref, v_ref, p_ref, m_ref
):
    row = pl.program_id(0)
    tok = tok_ref[...]
    q_ref[...] = (dot(tok, wq_ref[...]) + bias_ref[0:1, :]).astype(BF) * jnp.asarray(0.125, BF)
    k_ref[...] = dot(tok, wk_ref[...]).astype(BF)
    v_ref[...] = (dot(tok, wv_ref[...]) + bias_ref[1:2, :]).astype(BF)
    low = lax.broadcasted_iota(jnp.int32, (1, 128), 1) < HD
    for qb in range(BLOCKS):
        lo, hi = window(qb)
        width = hi - lo
        rows = slice(qb * BLOCK, (qb + 1) * BLOCK)
        seg_q = segment_of(
            lax.broadcasted_iota(jnp.int32, (BLOCK, 1), 0) + qb * BLOCK, lengths_ref, row
        )
        seg_k = segment_of(
            lax.broadcasted_iota(jnp.int32, (1, width), 1) + lo, lengths_ref, row
        )
        mask = jnp.where(seg_q == seg_k, 0.0, masked_score)
        for pair in range(PAIRS):
            lanes = slice(pair * 128, (pair + 1) * 128)
            q2 = q_ref[rows, lanes]
            k2 = k_ref[lo:hi, lanes]
            v2 = v_ref[lo:hi, lanes]
            mixed = []
            for h in range(2):
                qh = jnp.where(low if h == 0 else ~low, q2, jnp.zeros_like(q2))
                s = dot_t(qh, k2) + mask
                w = jnp.exp(s - jnp.max(s, axis=-1, keepdims=True))
                p = (w * (1.0 / jnp.sum(w, axis=-1, keepdims=True))).astype(BF)
                p_ref[pair, qb, h * BLOCK : (h + 1) * BLOCK, :width] = p
                mixed.append(dot(p, v2))
            m_ref[rows, lanes] = jnp.where(low, mixed[0], mixed[1]).astype(BF)


def attend_forward(lengths, tokens, wq, wk, wv, bias):
    t = tokens.shape[0]
    rows = t // SEQ
    row_spec = pl.BlockSpec((SEQ, GW), lambda r, *_: (r, 0))
    p_shape = (rows * PAIRS, BLOCKS, 2 * BLOCK, WIDE)
    return call(
        attend_forward_kernel,
        (rows,),
        [
            pl.BlockSpec((SEQ, D), lambda r, *_: (r, 0)),
            whole((D, GW)),
            whole((D, GW)),
            whole((D, GW)),
            whole((2, GW)),
        ],
        [row_spec] * 3
        + [pl.BlockSpec((PAIRS,) + p_shape[1:], lambda r, *_: (r, 0, 0, 0)), row_spec],
        [shaped((t, GW), BF)] * 3 + [shaped(p_shape, BF), shaped((t, GW), BF)],
        flops=t * D * D * 2 * 4,
        nbytes=8 * 2**20,
        prefetch=1,
    )(lengths, tokens, wq, wk, wv, bias)


def attend_backward_kernel(
    datt_ref, wo_ref, q_ref, k_ref, v_ref, p_ref, m_ref, dp_ref, sums_ref, dk_acc, dv_acc
):
    low = lax.broadcasted_iota(jnp.int32, (1, 128), 1) < HD
    dmix = dot_t(datt_ref[...], wo_ref[...]).astype(BF)
    dk_acc[...] = jnp.zeros_like(dk_acc)
    dv_acc[...] = jnp.zeros_like(dv_acc)
    for qb in range(BLOCKS):
        lo, hi = window(qb)
        width = hi - lo
        rows = slice(qb * BLOCK, (qb + 1) * BLOCK)
        for pair in range(PAIRS):
            lanes = slice(pair * 128, (pair + 1) * 128)
            q2 = q_ref[rows, lanes]
            k2 = k_ref[lo:hi, lanes]
            v2 = v_ref[lo:hi, lanes]
            do2 = dmix[rows, lanes]
            prod = do2.astype(F32) * m_ref[rows, lanes].astype(F32)
            dqs, scores, qs, dos = [], [], [], []
            for h in range(2):
                pick = low if h == 0 else ~low
                doh = jnp.where(pick, do2, jnp.zeros_like(do2))
                delta = jnp.sum(jnp.where(pick, prod, 0.0), axis=-1, keepdims=True)
                p = p_ref[pair, qb, h * BLOCK : (h + 1) * BLOCK, :width]
                ds = (p.astype(F32) * (dot_t(doh, v2) - delta)).astype(BF)
                dqs.append(dot(ds, k2))
                scores.append(ds)
                qs.append(jnp.where(pick, q2, jnp.zeros_like(q2)))
                dos.append(doh)
            dp_ref[rows, pair * 128 : (pair + 1) * 128] = (
                jnp.where(low, dqs[0], dqs[1]) * 0.125
            ).astype(BF)
            ds_both = jnp.concatenate(scores, axis=0)
            p_both = p_ref[pair, qb, :, :width]
            dk_acc[lo:hi, lanes] += t_dot(ds_both, jnp.concatenate(qs, axis=0))
            dv_acc[lo:hi, lanes] += t_dot(p_both, jnp.concatenate(dos, axis=0))
    dp_ref[:, GW : 2 * GW] = dk_acc[...].astype(BF)
    dp_ref[:, 2 * GW :] = dv_acc[...].astype(BF)
    sums = jnp.concatenate(
        [
            jnp.sum(dp_ref[:, :GW].astype(F32), axis=0, keepdims=True),
            jnp.sum(dp_ref[:, 2 * GW :].astype(F32), axis=0, keepdims=True),
        ],
        axis=0,
    )

    @pl.when(pl.program_id(0) == 0)
    def _():
        sums_ref[...] = sums

    @pl.when(pl.program_id(0) > 0)
    def _():
        sums_ref[...] += sums


def attend_backward(datt, w_out, group, kept):
    q, k, v, p, mixed = kept
    t = datt.shape[0]
    rows = t // SEQ
    row_spec = pl.BlockSpec((SEQ, GW), lambda r: (r, 0))
    return call(
        attend_backward_kernel,
        (rows,),
        [
            pl.BlockSpec((SEQ, D), lambda r: (r, 0)),
            pl.BlockSpec((GW, D), lambda r: (group, 0), pipeline_mode=pl.Buffered(1)),
            row_spec,
            row_spec,
            row_spec,
            pl.BlockSpec((PAIRS,) + p.shape[1:], lambda r: (r, 0, 0, 0)),
            row_spec,
        ],
        [pl.BlockSpec((SEQ, 3 * GW), lambda r: (r, 0)), pl.BlockSpec((2, GW), lambda r: (0, 0))],
        [shaped((t, 3 * GW), BF), shaped((2, GW), F32)],
        flops=t * D * D * 2 * 4,
        nbytes=8 * 2**20,
        scratch=[pltpu.VMEM((SEQ, GW), F32), pltpu.VMEM((SEQ, GW), F32)],
    )(datt, w_out, q, k, v, p, mixed)


TB = 256
CH = 768


def normalize(values):
    centered = values - jnp.mean(values, axis=-1, keepdims=True)
    variance = jnp.mean(centered * centered, axis=-1, keepdims=True)
    inverse = lax.rsqrt(variance + epsilon)
    return centered * inverse, inverse


def normalize_back(grad, xhat, inverse):
    mean = jnp.mean(grad, axis=-1, keepdims=True)
    along = jnp.mean(grad * xhat, axis=-1, keepdims=True)
    return (grad - mean - xhat * along) * inverse


def add_rows(ref, rows):
    stacked = jnp.concatenate([jnp.sum(r, axis=0, keepdims=True) for r in rows], axis=0)

    @pl.when(pl.program_id(0) == 0)
    def _():
        ref[...] = stacked

    @pl.when(pl.program_id(0) > 0)
    def _():
        ref[...] += stacked


def up_kernel(
    tok_ref, m0, m1, m2, wo_ref, vec_ref, wu_ref, bu_ref, xhat_ref, inv_ref, nl_ref, act_ref, gp_ref
):
    att = vec_ref[0:1, :]
    for g, m in enumerate((m0, m1, m2)):
        att = att + dot(m[...], wo_ref[g * GW : (g + 1) * GW, :])
    xhat, inverse = normalize(tok_ref[...].astype(F32) + att)
    xhat_ref[...] = xhat
    inv_ref[...] = inverse
    nl = (xhat * vec_ref[1:2, :] + vec_ref[2:3, :]).astype(BF)
    nl_ref[...] = nl
    for c in range(0, FF, CH):
        u = dot(nl, wu_ref[:, c : c + CH]) + bu_ref[:, c : c + CH]
        cdf = 0.5 * (1.0 + lax.erf(u * root_half))
        act_ref[:, c : c + CH] = (u * cdf).astype(BF)
        gp_ref[:, c : c + CH] = (cdf + u * (jnp.exp(u * u * -0.5) * pdf_scale)).astype(BF)


def up(tokens, mixed, w_out, vec, w_up, bias_up):
    t = tokens.shape[0]
    tok = lambda n: pl.BlockSpec((TB, n), lambda i: (i, 0))
    return call(
        up_kernel,
        (t // TB,),
        [tok(D), tok(GW), tok(GW), tok(GW), whole((D, D)), whole((3, D)), whole((D, FF)), whole((1, FF))],
        [tok(D), tok(1), tok(D), tok(FF), tok(FF)],
        [shaped((t, D), F32), shaped((t, 1), F32), shaped((t, D), BF), shaped((t, FF), BF), shaped((t, FF), BF)],
        flops=2 * t * D * (D + FF) * 2,
        nbytes=24 * 2**20,
    )(tokens, *mixed, w_out, vec, w_up, bias_up)


def down_kernel(
    lengths_ref, act_ref, xhat_ref, wd_ref, vec_ref, cot_ref, out_ref, ds_ref, dd_ref, sums_ref, pool_ref
):
    i = pl.program_id(0)
    normed = xhat_ref[...] * vec_ref[0:1, :] + vec_ref[1:2, :]
    second = normed + (dot(act_ref[...], wd_ref[...]) + vec_ref[2:3, :])
    xhat, inverse = normalize(second)
    out = (xhat * vec_ref[3:4, :] + vec_ref[4:5, :]).astype(BF)
    out_ref[...] = out
    cot = cot_ref[...].astype(F32)
    d_second = normalize_back(cot * vec_ref[3:4, :], xhat, inverse)
    ds_ref[...] = d_second
    d_down = d_second.astype(BF)
    dd_ref[...] = d_down
    add_rows(sums_ref, (cot * xhat, cot, d_down.astype(F32)))
    per_row = SEQ // TB
    row = i // per_row
    places = lax.broadcasted_iota(jnp.int32, (1, TB), 1) + (i % per_row) * TB
    segment = segment_of(places, lengths_ref, row)
    ids = lax.broadcasted_iota(jnp.int32, (SEGS, TB), 0)
    member = jnp.where(segment == ids, 1.0, 0.0).astype(BF)
    sums = dot(member, out)

    @pl.when(i % per_row == 0)
    def _():
        pool_ref[0] = sums

    @pl.when(i % per_row > 0)
    def _():
        pool_ref[0] += sums


def down(lengths, active, xhat, w_down, vec, cot):
    t = cot.shape[0]
    tok = lambda n: pl.BlockSpec((TB, n), lambda i, *_: (i, 0))
    return call(
        down_kernel,
        (t // TB,),
        [tok(FF), tok(D), whole((FF, D)), whole((5, D)), tok(D)],
        [
            tok(D),
            tok(D),
            tok(D),
            pl.BlockSpec((3, D), lambda i, *_: (0, 0)),
            pl.BlockSpec((1, SEGS, D), lambda i, *_: (i // (SEQ // TB), 0, 0)),
        ],
        [
            shaped((t, D), BF),
            shaped((t, D), F32),
            shaped((t, D), BF),
            shaped((3, D), F32),
            shaped((t // SEQ, SEGS, D), F32),
        ],
        flops=2 * t * D * FF,
        nbytes=24 * 2**20,
        prefetch=1,
    )(lengths, active, xhat, w_down, vec, cot)


def back_kernel(
    dd_ref, gp_ref, ds_ref, xhat_ref, inv_ref, wd_ref, wu_ref, gain_ref, du_ref, df_ref, da_ref, sums_ref, su_ref
):
    i = pl.program_id(0)
    dd = dd_ref[...]
    d_normed = ds_ref[...]
    for c in range(0, FF, CH):
        du = (dot_t(dd, wd_ref[c : c + CH, :]) * gp_ref[:, c : c + CH].astype(F32)).astype(BF)
        du_ref[:, c : c + CH] = du
        d_normed = d_normed + dot_t(du, wu_ref[:, c : c + CH])
        partial = jnp.sum(du.astype(F32), axis=0, keepdims=True)
        su_ref[:, c : c + CH] = jnp.where(i == 0, partial, su_ref[:, c : c + CH] + partial)
    xhat = xhat_ref[...]
    d_first = normalize_back(d_normed * gain_ref[...], xhat, inv_ref[...])
    df_ref[...] = d_first
    d_att = d_first.astype(BF)
    da_ref[...] = d_att
    add_rows(sums_ref, (d_normed * xhat, d_normed, d_att.astype(F32)))


def back(d_down, gp, d_second, xhat, inverse, w_down, w_up, gain):
    t = d_down.shape[0]
    tok = lambda n: pl.BlockSpec((TB, n), lambda i: (i, 0))
    return call(
        back_kernel,
        (t // TB,),
        [tok(D), tok(FF), tok(D), tok(D), tok(1), whole((FF, D)), whole((D, FF)), whole((1, D))],
        [tok(FF), tok(D), tok(D), pl.BlockSpec((3, D), lambda i: (0, 0)), pl.BlockSpec((1, FF), lambda i: (0, 0))],
        [shaped((t, FF), BF), shaped((t, D), F32), shaped((t, D), BF), shaped((3, D), F32), shaped((1, FF), F32)],
        flops=4 * t * D * FF,
        nbytes=32 * 2**20,
    )(d_down, gp, d_second, xhat, inverse, w_down, w_up, gain)


def input_kernel(df_ref, p0, p1, p2, wqkv_ref, out_ref):
    total = df_ref[...]
    for g, p in enumerate((p0, p1, p2)):
        for part in range(3):
            start = part * D + g * GW
            total = total + dot_t(p[:, part * GW : (part + 1) * GW], wqkv_ref[:, start : start + GW])
    out_ref[...] = total


def input_gradient(d_first, d_projected, w_qkv):
    t = d_first.shape[0]
    tok = lambda n: pl.BlockSpec((TB, n), lambda i: (i, 0))
    return call(
        input_kernel,
        (t // TB,),
        [tok(D), tok(D), tok(D), tok(D), whole((D, 3 * D))],
        tok(D),
        shaped((t, D), F32),
        flops=2 * t * D * 3 * D,
        nbytes=16 * 2**20,
    )(d_first, *d_projected, w_qkv)


def weight_kernel(ranks, half, me_ref, a_ref, b_ref, *refs):
    outs, (acc, sems) = refs[:-2], refs[-2:]
    me = me_ref[0]
    replica = me_ref[1]
    step = pl.program_id(0)
    columns = acc.shape[1]
    acc[...] = t_dot(a_ref[...], b_ref[...]).astype(BF)
    rows = acc.shape[0] // ranks
    copies = []
    for j in range(ranks):
        owner = me ^ j
        source = acc.at[pl.ds(pl.multiple_of(owner * rows, rows), rows)]
        copies.append(pltpu.make_async_copy(source, outs[j % 2].at[j // 2], sems.at[j]))
    for copy in copies:
        copy.start()
    for copy in copies:
        copy.wait()


def weight_gradient(where, a, b, ranks):
    t, m = a.shape
    n = b.shape[1]
    rows = m // ranks
    half = shaped((ranks // 2, rows, n), BF)
    return call(
        functools.partial(weight_kernel, ranks, False),
        (1,),
        [pl.BlockSpec((t, m), lambda i, *_: (0, 0)), pl.BlockSpec((t, n), lambda i, *_: (0, 0))],
        [pl.BlockSpec(memory_space=pl.ANY)] * 2,
        [half, half],
        flops=2 * t * m * n,
        nbytes=2 * (t * m + t * n + m * n),
        scratch=[pltpu.VMEM((m, n), BF), pltpu.SemaphoreType.DMA((ranks,))],
        prefetch=1,
    )(where, a, b)


def swap(x, mask, ranks):
    return lax.ppermute(x, "fsdp", [(i, i ^ mask) for i in range(ranks)])


def swap_replica(x):
    return lax.ppermute(x, "replica", [(0, 1), (1, 0)])


def bf_sum(*terms):
    total = terms[0].astype(F32)
    for term in terms[1:]:
        total = total + term.astype(F32)
    return total.astype(BF)


def gather_pieces(w, ranks):
    z = jnp.stack([w] + [swap(w, m, ranks) for m in (4, 8, 12)])
    y = swap(z, 2, ranks)
    return (z, y, swap(z, 1, ranks), swap(y, 1, ranks))


def assemble_kernel(me_ref, p0, p1, p2, p3, out_ref, sems):
    me = me_ref[0]
    rows = p0.shape[1]
    copies = []
    for index, piece in enumerate((p0, p1, p2, p3)):
        mask = (index % 2) * 2 + index // 2
        for k in range(4):
            owner = me ^ (4 * k + mask)
            target = out_ref.at[pl.ds(pl.multiple_of(owner * rows, rows), rows)]
            copies.append(pltpu.make_async_copy(piece.at[k], target, sems.at[index * 4 + k]))
    for copy in copies:
        copy.start()
    for copy in copies:
        copy.wait()


def assemble(where, pieces):
    _, rows, columns = pieces[0].shape
    return call(
        assemble_kernel,
        (1,),
        [pl.BlockSpec(memory_space=pl.ANY)] * 4,
        pl.BlockSpec(memory_space=pl.ANY),
        shaped((16 * rows, columns), BF),
        flops=0,
        nbytes=4 * 16 * rows * columns,
        scratch=[pltpu.SemaphoreType.DMA((16,))],
        prefetch=1,
    )(where, *pieces)


def gather_small(x, ranks, me):
    z = jnp.stack([x] + [swap(x, m, ranks) for m in (4, 8, 12)])
    y = swap(z, 2, ranks)
    zy = jnp.stack([z, y], axis=1)
    c = swap(zy, 1, ranks)
    relative = jnp.stack([zy, c], axis=2).reshape(ranks, -1)
    return relative[me ^ jnp.arange(ranks)]


def scatter_pieces(keep, send, ranks):
    _, rows, columns = keep.shape
    received = swap(send, 1, ranks)
    keep = keep.reshape(4, 2, rows, columns)
    received = received.reshape(4, 2, rows, columns)
    away = bf_sum(keep[:, 1], received[:, 1])
    stay = bf_sum(keep[:, 0], received[:, 0])
    back_y = swap(away, 2, ranks)
    parts = [bf_sum(stay[k], back_y[k]) for k in range(4)]
    total = bf_sum(parts[0], *[swap(parts[k], 4 * k, ranks) for k in (1, 2, 3)])
    return total.astype(F32) + swap_replica(total).astype(F32)


def scatter_small(x, ranks, me):
    relative = x[me ^ jnp.arange(ranks)].reshape(4, 2, 2, -1)
    relative = relative[:, :, 0] + swap(relative[:, :, 1], 1, ranks)
    relative = relative[:, 0] + swap(relative[:, 1], 2, ranks)
    total = relative[0] + sum(swap(relative[k], 4 * k, ranks) for k in (1, 2, 3))
    return total + swap_replica(total)


def gather_pooled(pooled, ranks, me, replica):
    z = jnp.stack([pooled] + [swap(pooled, m, ranks) for m in (4, 8, 12)])
    y = swap(z, 2, ranks)
    zy = jnp.stack([z, y], axis=1)
    x = swap_replica(zy)
    zyx = jnp.stack([zy, x])
    c = swap(zyx, 1, ranks)
    relative = jnp.stack([zyx, c], axis=3)
    relative = relative.reshape((2, ranks) + pooled.shape)
    own = relative[jnp.array([0, 1]) ^ replica][:, me ^ jnp.arange(ranks)]
    return own.reshape((2 * ranks * pooled.shape[0],) + pooled.shape[1:])


SMALL = ("bias_qv", "bias_out", "gain_one", "shift_one", "bias_up", "bias_down", "gain_two", "shift_two")
SMALL_SIZES = (2 * D, D, D, D, FF, D, D, D)


def body(
    ranks,
    replicas,
    tokens,
    lengths,
    w_qkv,
    bias_qv,
    w_out,
    bias_out,
    gain_one,
    shift_one,
    w_up,
    bias_up,
    w_down,
    bias_down,
    gain_two,
    shift_two,
    cotangent,
):
    direct = ranks == 16 and replicas == 2
    me = lax.axis_index("fsdp")
    replica = lax.axis_index("replica")
    where = jnp.stack([me, replica]).astype(jnp.int32)
    gather = lambda w: lax.all_gather(w, "fsdp", axis=0, tiled=True)

    small = jnp.concatenate(
        [bias_qv, bias_out, gain_one, shift_one, bias_up, bias_down, gain_two, shift_two]
    )
    if direct:
        small_all = gather_small(small, ranks, me)
    else:
        small_all = gather(small).reshape(ranks, -1)
    vectors, start = {}, 0
    for name, size in zip(SMALL, SMALL_SIZES):
        part = size // ranks
        vectors[name] = small_all[:, start : start + part].reshape(size).astype(F32)
        start += part
    if direct:
        w_qkv_full = assemble(where, gather_pieces(w_qkv, ranks))
    else:
        w_qkv_full = gather(w_qkv)
    w_out_full, w_up_full, w_down_full = gather(w_out), gather(w_up), gather(w_down)

    kept = []
    for g in range(GROUPS):
        cols = slice(g * GW, (g + 1) * GW)
        wq, wk, wv = (w_qkv_full[:, p * D + g * GW : p * D + (g + 1) * GW] for p in range(3))
        bias = jnp.stack([vectors["bias_qv"][:D][cols], vectors["bias_qv"][D:][cols]])
        kept.append(attend_forward(lengths, tokens, wq, wk, wv, bias))
    mixed = [item[4] for item in kept]
    vec_one = jnp.stack([vectors["bias_out"], vectors["gain_one"], vectors["shift_one"]])
    xhat, inverse, nl, active, gp = up(
        tokens, mixed, w_out_full, vec_one, w_up_full, vectors["bias_up"][None]
    )
    vec_two = jnp.stack(
        [vectors[n] for n in ("gain_one", "shift_one", "bias_down", "gain_two", "shift_two")]
    )
    layer_out, d_second, d_down, sums_two, pool = down(
        lengths, active, xhat, w_down_full, vec_two, cotangent
    )

    def reduce(a, b):
        m, n = a.shape[1], b.shape[1]
        if direct:
            return scatter_pieces(*weight_gradient(where, a, b, ranks), ranks)
        term = t_dot(a, b).astype(BF)
        shard = lax.psum_scatter(term, "fsdp", scatter_dimension=0, tiled=True)
        return lax.psum(shard, "replica").astype(F32)

    grad_w_down = reduce(active, d_down)
    d_upper, d_first, d_att, sums_one, sums_up = back(
        d_down, gp, d_second, xhat, inverse, w_down_full, w_up_full, vectors["gain_one"][None]
    )
    grad_w_up = reduce(nl, d_upper)
    grad_w_out = reduce(jnp.concatenate(mixed, axis=1), d_att)
    d_projected, sums_qv, grads_qkv = [], [], []
    for g in range(GROUPS):
        dp, sums = attend_backward(d_att, w_out_full, g, kept[g])
        d_projected.append(dp)
        sums_qv.append(sums)
        grads_qkv.append(reduce(tokens, dp))
    input_grad = input_gradient(d_first, d_projected, w_qkv_full)
    grad_w_qkv = jnp.concatenate(
        [grads_qkv[g][:, p * GW : (p + 1) * GW] for p in range(3) for g in range(GROUPS)], axis=1
    )

    pooled = (pool / lengths.astype(F32)[:, :, None]).astype(BF)
    if direct:
        pooled_all = gather_pooled(pooled, ranks, me, replica)
    else:
        pooled_all = lax.all_gather(pooled, ("replica", "fsdp"), axis=0, tiled=True)

    small_terms = {
        "bias_qv": jnp.concatenate([s[i] for i in range(2) for s in sums_qv]),
        "bias_out": sums_one[2],
        "gain_one": sums_one[0],
        "shift_one": sums_one[1],
        "bias_up": sums_up[0],
        "bias_down": sums_two[2],
        "gain_two": sums_two[0],
        "shift_two": sums_two[1],
    }
    packed = jnp.concatenate([small_terms[n].reshape(ranks, -1) for n in SMALL], axis=1)
    if direct:
        packed = scatter_small(packed, ranks, me)
    else:
        packed = lax.psum_scatter(packed, "fsdp", scatter_dimension=0, tiled=False)
        packed = lax.psum(packed, "replica")
    small_grads, start = {}, 0
    for name, size in zip(SMALL, SMALL_SIZES):
        part = size // ranks
        small_grads[name] = packed[start : start + part]
        start += part
    return (
        layer_out,
        input_grad,
        pooled_all.astype(F32),
        grad_w_qkv,
        small_grads["bias_qv"],
        grad_w_out,
        small_grads["bias_out"],
        small_grads["gain_one"],
        small_grads["shift_one"],
        grad_w_up,
        small_grads["bias_up"],
        grad_w_down,
        small_grads["bias_down"],
        small_grads["gain_two"],
        small_grads["shift_two"],
    )


def solution(mesh):
    rows = P(("replica", "fsdp"), None)
    matrix = P("fsdp", None)
    vector = P("fsdp")
    return jax.shard_map(
        functools.partial(body, mesh.shape["fsdp"], mesh.shape["replica"]),
        mesh=mesh,
        in_specs=(
            rows,
            rows,
            matrix,
            vector,
            matrix,
            vector,
            vector,
            vector,
            matrix,
            vector,
            matrix,
            vector,
            vector,
            vector,
            rows,
        ),
        out_specs=(
            rows,
            rows,
            P(),
            matrix,
            vector,
            matrix,
            vector,
            vector,
            vector,
            matrix,
            vector,
            matrix,
            vector,
            vector,
            vector,
        ),
        check_vma=False,
    )
```

time: 779 us -> 565 us (0.73)
  Pallas kernels: 0 us -> 292 us
  matrix products: 203 us -> 0 us
  blocking collectives: 151 us -> 0 us
  waiting for transfers between devices: 266 us -> 140 us
  starting transfers between devices: 0.36 us -> 62.9 us
  local copies, waits for them, and re-layouts: 69.4 us -> 21.5 us
  other arithmetic: 57.4 us -> 24.7 us
    pallas_call x0 -> x17, Pallas kernels: none -> 292 us  [the longest x1 109 us: assemble(): call(assemble_kernel, (1,), [pl.BlockSpec(memory_space=pl.ANY)] * 4, pl.B...]
    dot_general x31 -> x0, matrix products: 188 us -> none  [the longest x4 33.4 us: times_transpose(): lax.dot_general(left, right, (((1,), (1,)), ((), ())), preferred_element_...]
    reduce_scatter x3 -> x0, waiting for transfers between devices: 177 us -> none  [the longest x1 114 us: body(): lax.psum_scatter(term_down, 'fsdp', scatter_dimension=0, tiled=True)]
    ppermute x0 -> x59, waiting for transfers between devices: none -> 137 us  [the longest x51 119 us: swap(): return lax.ppermute(x, 'fsdp', [(i, i ^ mask) for i in range(ranks)])]
    unnamed x2 -> x0, blocking collectives: 96.1 us -> none
    ppermute x0 -> x59, starting transfers between devices: none -> 62.8 us  [the longest x51 56.7 us: swap(): return lax.ppermute(x, 'fsdp', [(i, i ^ mask) for i in range(ranks)])]
    all_gather x1 -> x0, blocking collectives: 49.6 us -> none  [body(): lax.all_gather(pooled.astype(jnp.bfloat16), ('replica', 'fsdp'), axis=0,...]
    all_gather x4 -> x3, waiting for transfers between devices: 49 us -> 0.02 us  [body(): gather = lambda w: lax.all_gather(w, 'fsdp', axis=0, tiled=True)]
  transfers between devices with their start and end apart: 9 -> 62, of which waited for: 4 -> 26; matrix products, arithmetic and copies ran while one was open for 31% -> 8% of each run, Pallas kernels for 0% -> 50%
where the time goes in v1:
time: 565 us; the launch traced here: 555 us
  Pallas kernels  292 us (52%)
  waiting for transfers between devices  140 us (25%)
  starting transfers between devices  62.9 us (11%)
  other arithmetic  24.7 us (4%)
  local copies, waits for them, and re-layouts  21.5 us (4%)
  between operations  15.1 us (3%)
    ppermute x51, waiting for transfers between devices, swap(): return lax.ppermute(x, 'fsdp', [(i, i ^ mask) for i in range(ranks)])  119 us
    pallas_call x1, Pallas kernels, assemble(): call(assemble_kernel, (1,), [pl.BlockSpec(memory_space=pl.ANY)] * 4, pl.B...  109 us
    ppermute x51, starting transfers between devices, swap(): return lax.ppermute(x, 'fsdp', [(i, i ^ mask) for i in range(ranks)])  56.7 us
    pallas_call x3, Pallas kernels, attend_forward(): call(attend_forward_kernel, (rows,), [pl.BlockSpec((SEQ, D), lambda r, *_...  44.1 us
    pallas_call x6, Pallas kernels, weight_gradient(): call(functools.partial(weight_kernel, ranks, False), (1,), [pl.BlockSpec(...  43.4 us
    pallas_call x3, Pallas kernels, attend_backward(): call(attend_backward_kernel, (rows,), [pl.BlockSpec((SEQ, D), lambda r: (...  33.2 us
    pallas_call x1, Pallas kernels, back(): call(back_kernel, (t // TB,), [tok(D), tok(FF), tok(D), tok(D), tok(1), w...  19.5 us
    ppermute x8, waiting for transfers between devices, swap_replica(): return lax.ppermute(x, 'replica', [(0, 1), (1, 0)])  18.6 us
  transfers between devices with their start and end apart: 62, of which 26 were waited for; matrix products, arithmetic and copies ran while one was open for 8% of the time, Pallas kernels for 50%

profile of v1, /device:TPU:20, one launch (start us, length us, event | category | flops | bytes accessed | tf_op | source)
XLA Modules:
  0.0 555.3 jit_solution(3106716799686536459)
XLA Ops:
  9.4 5.4 concatenate.15
  23.1 7.6 %collective-permute-done = bf16[48,2304]{1,0:T(8,128)(2,1)S(1)} collective-permute-done((bf16[48,2304]{1,0:T(8,128)(2,1)}, bf16[48,2304]{1,0:T(8,128)(2,1)S(1)}, u32[]{:S(2)}, u32[]{:S(2)}) %collective-permute-start) | collective-permute-done | bytes 221216 | tf_op jit(solution)/shard_map/ppermute | solution.py:437
  30.6 7.6 %collective-permute-done.1 = bf16[48,2304]{1,0:T(8,128)(2,1)S(1)} collective-permute-done((bf16[48,2304]{1,0:T(8,128)(2,1)}, bf16[48,2304]{1,0:T(8,128)(2,1)S(1)}, u32[]{:S(2)}, u32[]{:S(2)}) %collective-permute-start.1) | collective-permute-done | bytes 221216 | tf_op jit(solution)/shard_map/ppermute | solution.py:437
  46.9 19.8 %collective-permute-done.3.p1 = bf16[4,48,2304]{2,1,0:T(8,128)(2,1)S(1)} collective-permute-done((bf16[4,48,2304]{2,1,0:T(8,128)(2,1)S(1)}, bf16[4,48,2304]{2,1,0:T(8,128)(2,1)S(1)}, u32[]{:S(2)}, u32[]{:S(2)}) %collective-permute-start.3) | collective-permute-done | bytes 884768 | tf_op jit(solution)/shard_map/ppermute | solution.py:437
  71.7 109.1 %shard_map.271.wqkv_ref = bf16[768,2304]{1,0:T(8,128)(2,1)} custom-call(s32[2]{0:T(128)} %pad_add_fusion.me_ref, bf16[4,48,2304]{2,1,0:T(8,128)(2,1)} %copy-done, bf16[4,48,2304]{2,1,0:T(8,128)(2,1)} %copy-done.3, bf16[4,48,2304]{2,1,0:T(8,128)(2,1)} %copy-done.4, bf16[4,48,2304]{2,1,0:T(8,128)(2,1)} %collective-permute-done.5.p3), custom_call_target="tpu_custom_call" | custom-call | bytes 7077888 | tf_op jit(solution)/shard_map/pallas_call | solution.py:475
  184.7 14.7 %shard_map.274 = (bf16[1024,256]{1,0:T(8,128)(2,1)}, bf16[1024,256]{1,0:T(8,128)(2,1)}, bf16[1024,256]{1,0:T(8,128)(2,1)}, bf16[4,4,256,384]{3,2,1,0:T(8,128)(2,1)}, bf16[1024,256]{1,0:T(8,128)(2,1)}) custom-call(s32[2,8]{1,0:T(2,128)} %lengths_ref.7, bf16[1024,768]{1,0:T(8,128)(2,1)} %a_ref.5, bf16[768,256]{1,0:T(8,128)(2,1)} %get-tuple-element.127.wq_ref, ...), custom_call_target="tpu_custom_call" | custom-call | flops 4831838208 | bytes 8388608 | tf_op jit(solution)/shard_map/pallas_call | solution.py:123
  199.4 14.7 %shard_map.273 = (bf16[1024,256]{1,0:T(8,128)(2,1)}, bf16[1024,256]{1,0:T(8,128)(2,1)}, bf16[1024,256]{1,0:T(8,128)(2,1)}, bf16[4,4,256,384]{3,2,1,0:T(8,128)(2,1)}, bf16[1024,256]{1,0:T(8,128)(2,1)}) custom-call(s32[2,8]{1,0:T(2,128)} %lengths_ref.7, bf16[1024,768]{1,0:T(8,128)(2,1)} %a_ref.5, bf16[768,256]{1,0:T(8,128)(2,1)} %get-tuple-element.130.wq_ref, ...), custom_call_target="tpu_custom_call" | custom-call | flops 4831838208 | bytes 8388608 | tf_op jit(solution)/shard_map/pallas_call | solution.py:123
  214.0 14.7 %shard_map.272 = (bf16[1024,256]{1,0:T(8,128)(2,1)}, bf16[1024,256]{1,0:T(8,128)(2,1)}, bf16[1024,256]{1,0:T(8,128)(2,1)}, bf16[4,4,256,384]{3,2,1,0:T(8,128)(2,1)}, bf16[1024,256]{1,0:T(8,128)(2,1)}) custom-call(s32[2,8]{1,0:T(2,128)} %lengths_ref.7, bf16[1024,768]{1,0:T(8,128)(2,1)} %a_ref.5, bf16[768,256]{1,0:T(8,128)(2,1)} %get-tuple-element.133.wq_ref, ...), custom_call_target="tpu_custom_call" | custom-call | flops 4831838208 | bytes 8388608 | tf_op jit(solution)/shard_map/pallas_call | solution.py:123
  231.1 18.5 %shard_map.275 = (f32[1024,768]{1,0:T(8,128)}, f32[1024,1]{1,0:T(8,128)}, bf16[1024,768]{1,0:T(8,128)(2,1)}, bf16[1024,3072]{1,0:T(8,128)(2,1)}, bf16[1024,3072]{1,0:T(8,128)(2,1)}) custom-call(bf16[1024,768]{1,0:T(8,128)(2,1)} %a_ref.5, bf16[1024,256]{1,0:T(8,128)(2,1)} %get-tuple-element.63.m0.m_ref, bf16[1024,256]{1,0:T(8,128)(2,1)} %get-tuple-element.64.m1.m_ref, ...), custom_call_target="tpu_custom_call" | custom-call | flops 12079595520 | bytes 25165824 | tf_op jit(solution)/shard_map/pallas_call | solution.py:272
  249.6 14.6 %shard_map.276 = (bf16[1024,768]{1,0:T(8,128)(2,1)}, f32[1024,768]{1,0:T(8,128)}, bf16[1024,768]{1,0:T(8,128)(2,1)}, f32[3,768]{1,0:T(4,128)}, f32[2,8,768]{2,1,0:T(8,128)}) custom-call(s32[2,8]{1,0:T(2,128)} %lengths_ref.7, bf16[1024,3072]{1,0:T(8,128)(2,1)} %get-tuple-element.66.act_ref.a_ref, f32[1024,768]{1,0:T(8,128)} %get-tuple-element.67.xhat_ref, ...), custom_call_target="tpu_custom_call" | custom-call | flops 4831838208 | bytes 25165824 | tf_op jit(solution)/shard_map/pallas_call | solution.py:318
  268.6 11.5 %shard_map.287 = (bf16[8,192,768]{2,1,0:T(8,128)(2,1)}, bf16[8,192,768]{2,1,0:T(8,128)(2,1)}) custom-call(s32[2]{0:T(128)} %pad_add_fusion.me_ref, bf16[1024,3072]{1,0:T(8,128)(2,1)} %get-tuple-element.66.act_ref.a_ref, bf16[1024,768]{1,0:T(8,128)(2,1)} %get-tuple-element.69.dd_ref.b_ref), custom_call_target="tpu_custom_call" | custom-call | flops 4831838208 | bytes 12582912 | tf_op jit(solution)/shard_map/pallas_call | solution.py:423
  280.2 19.5 %shard_map.277 = (bf16[1024,3072]{1,0:T(8,128)(2,1)}, f32[1024,768]{1,0:T(8,128)}, bf16[1024,768]{1,0:T(8,128)(2,1)}, f32[3,768]{1,0:T(4,128)}, f32[1,3072]{1,0:T(1,128)}) custom-call(bf16[1024,768]{1,0:T(8,128)(2,1)} %get-tuple-element.69.dd_ref.b_ref, bf16[1024,3072]{1,0:T(8,128)(2,1)} %get-tuple-element.70.gp_ref, f32[1024,768]{1,0:T(8,128)} %get-tuple-element.71.ds_ref, ...), custom_call_target="tpu_custom_call" | custom-call | flops 9663676416 | bytes 33554432 | tf_op jit(solution)/shard_map/pallas_call | solution.py:365
  299.7 11.0 %shard_map.279 = (bf16[1024,768]{1,0:T(8,128)(2,1)}, f32[2,256]{1,0:T(2,128)}) custom-call(bf16[1024,768]{1,0:T(8,128)(2,1)} %get-tuple-element.74.datt_ref.b_ref, bf16[768,768]{1,0:T(8,128)(2,1)} %all-gather.4.cloned.1.call-done.wo_ref, bf16[1024,256]{1,0:T(8,128)(2,1)} %get-tuple-element.80.q_ref, bf16[1024,256]{1,0:T(8,128)(2,1)} %get-tuple-element.81.k_ref, ...), custom_call_target="tpu_custom_call" | custom-call | flops 4831838208 | bytes 8388608 | tf_op jit(solution)/shard_map/pallas_call | solution.py:202
  311.4 11.0 %shard_map.278 = (bf16[1024,768]{1,0:T(8,128)(2,1)}, f32[2,256]{1,0:T(2,128)}) custom-call(bf16[1024,768]{1,0:T(8,128)(2,1)} %get-tuple-element.74.datt_ref.b_ref, bf16[768,768]{1,0:T(8,128)(2,1)} %all-gather.4.cloned.1.call-done.wo_ref, bf16[1024,256]{1,0:T(8,128)(2,1)} %get-tuple-element.75.q_ref, bf16[1024,256]{1,0:T(8,128)(2,1)} %get-tuple-element.76.k_ref, ...), custom_call_target="tpu_custom_call" | custom-call | flops 4831838208 | bytes 8388608 | tf_op jit(solution)/shard_map/pallas_call | solution.py:202
  323.2 11.2 %shard_map.280 = (bf16[1024,768]{1,0:T(8,128)(2,1)}, f32[2,256]{1,0:T(2,128)}) custom-call(bf16[1024,768]{1,0:T(8,128)(2,1)} %get-tuple-element.74.datt_ref.b_ref, bf16[768,768]{1,0:T(8,128)(2,1)} %all-gather.4.cloned.1.call-done.wo_ref, bf16[1024,256]{1,0:T(8,128)(2,1)} %get-tuple-element.85.q_ref, bf16[1024,256]{1,0:T(8,128)(2,1)} %get-tuple-element.86.k_ref, ...), custom_call_target="tpu_custom_call" | custom-call | flops 4831838208 | bytes 8388608 | tf_op jit(solution)/shard_map/pallas_call | solution.py:202
  348.7 11.3 %shard_map.286 = (bf16[8,48,3072]{2,1,0:T(8,128)(2,1)}, bf16[8,48,3072]{2,1,0:T(8,128)(2,1)}) custom-call(s32[2]{0:T(128)} %pad_add_fusion.me_ref, bf16[1024,768]{1,0:T(8,128)(2,1)} %get-tuple-element.105.a_ref, bf16[1024,3072]{1,0:T(8,128)(2,1)} %get-tuple-element.106.b_ref), custom_call_target="tpu_custom_call" | custom-call | flops 4831838208 | bytes 12582912 | tf_op jit(solution)/shard_map/pallas_call | solution.py:423
  360.1 9.2 %shard_map.281 = f32[1024,768]{1,0:T(8,128)} custom-call(f32[1024,768]{1,0:T(8,128)} %get-tuple-element.73.df_ref, bf16[1024,768]{1,0:T(8,128)(2,1)} %get-tuple-element.79.p0.b_ref, bf16[1024,768]{1,0:T(8,128)(2,1)} %get-tuple-element.84.p1.b_ref, bf16[1024,768]{1,0:T(8,128)(2,1)} %get-tuple-element.89.p2.b_ref, bf16[768,2304]{1,0:T(8,128)(2,1)} %shard_map.271.wqkv_ref), custom_call_target="tpu_custom_call" | custom-call | flops 3623878656 | bytes 16777216 | tf_op jit(solution)/shard_map/pallas_call | solution.py:388
  391.6 6.1 %collective-permute-done.15 = bf16[4,2,2,8,768]{4,3,2,0,1:T(8,128)(2,1)S(1)} collective-permute-done((bf16[4,2,2,8,768]{4,3,2,0,1:T(8,128)(2,1)S(1)}, bf16[4,2,2,8,768]{4,3,2,0,1:T(8,128)(2,1)S(1)}, u32[]{:S(2)}, u32[]{:S(2)}) %collective-permute-start.15) | collective-permute-done | bytes 196640 | tf_op jit(solution)/shard_map/ppermute | solution.py:441
  469.0 23.5 %collective-permute-done.54 = bf16[4,192,768]{2,1,0:T(8,128)(2,1)S(1)} collective-permute-done((bf16[4,192,768]{2,1,0:T(8,128)(2,1)S(1)}, bf16[4,192,768]{2,1,0:T(8,128)(2,1)S(1)}, u32[]{:S(2)}, u32[]{:S(2)}) %collective-permute-start.54) | collective-permute-done | bytes 1179680 | tf_op jit(solution)/shard_map/ppermute | solution.py:437
  497.9 16.1 %collective-permute-done.48 = bf16[4,48,3072]{2,1,0:T(8,128)(2,1)S(1)} collective-permute-done((bf16[4,48,3072]{2,1,0:T(8,128)(2,1)S(1)}, bf16[4,48,3072]{2,1,0:T(8,128)(2,1)S(1)}, u32[]{:S(2)}, u32[]{:S(2)}) %collective-permute-start.48) | collective-permute-done | bytes 1179680 | tf_op jit(solution)/shard_map/ppermute | solution.py:437
  518.6 6.4 %collective-permute-done.49 = bf16[48,3072]{1,0:T(8,128)(2,1)S(1)} collective-permute-done((bf16[48,3072]{1,0:T(8,128)(2,1)S(1)}, bf16[48,3072]{1,0:T(8,128)(2,1)S(1)}, u32[]{:S(2)}, u32[]{:S(2)}) %collective-permute-start.49) | collective-permute-done | bytes 294944 | tf_op jit(solution)/shard_map/ppermute | solution.py:437
  525.1 9.1 %collective-permute-done.50 = bf16[48,3072]{1,0:T(8,128)(2,1)S(1)} collective-permute-done((bf16[48,3072]{1,0:T(8,128)(2,1)S(1)}, bf16[48,3072]{1,0:T(8,128)(2,1)S(1)}, u32[]{:S(2)}, u32[]{:S(2)}) %collective-permute-start.50) | collective-permute-done | bytes 294944 | tf_op jit(solution)/shard_map/ppermute | solution.py:437
  534.2 5.6 %collective-permute-done.51 = bf16[48,3072]{1,0:T(8,128)(2,1)S(1)} collective-permute-done((bf16[48,3072]{1,0:T(8,128)(2,1)S(1)}, bf16[48,3072]{1,0:T(8,128)(2,1)S(1)}, u32[]{:S(2)}, u32[]{:S(2)}) %collective-permute-start.51) | collective-permute-done | bytes 294944 | tf_op jit(solution)/shard_map/ppermute | solution.py:437
  541.6 5.9 %collective-permute-done.52 = bf16[48,3072]{1,0:T(8,128)(2,1)S(1)} collective-permute-done((bf16[48,3072]{1,0:T(8,128)(2,1)S(1)}, bf16[48,3072]{1,0:T(8,128)(2,1)S(1)}, u32[]{:S(2)}, u32[]{:S(2)}) %collective-permute-start.52) | collective-permute-done | bytes 294944 | tf_op jit(solution)/shard_map/ppermute | solution.py:441
  (280 shorter events, 156.0 us)
Async XLA Ops:
  7.2 223.9 %all-gather.4.cloned.1.call-start = ((), (), s32[]{:S(2)}) async-start(), calls=%async_computation | async-start | bytes 1253376 | tf_op jit(solution)/shard_map/all_gather | solution.py:558
  7.9 223.1 %all-gather.6.cloned.1.call-start = ((), (), s32[]{:S(2)}) async-start(), calls=%async_computation.1 | async-start | bytes 5013504 | tf_op jit(solution)/shard_map/all_gather | solution.py:558
  8.7 240.9 %all-gather.8.cloned.1.call-start = ((), (), s32[]{:S(2)}) async-start(), calls=%async_computation.2 | async-start | bytes 5013504 | tf_op jit(solution)/shard_map/all_gather | solution.py:558
  20.9 21.8 %collective-permute-start.2 = (bf16[48,2304]{1,0:T(8,128)(2,1)}, bf16[48,2304]{1,0:T(8,128)(2,1)S(1)}, u32[]{:S(2)}, u32[]{:S(2)}) collective-permute-start(bf16[48,2304]{1,0:T(8,128)(2,1)} %param.18), channel_id=1, source_target_pairs={{0,12},{1,13},{2,14},{3,15},{4,8},{5,9},{6,10},{7,11},{8,4},{9,5},... | collective-permute-start | bytes 663560 | tf_op jit(solution)/shard_map/ppermute | solution.py:437
  22.5 21.8 %collective-permute-start.9 = (bf16[4,576]{1,0:T(4,128)(2,1)S(1)}, bf16[4,576]{1,0:T(4,128)(2,1)S(1)}, u32[]{:S(2)}, u32[]{:S(2)}) collective-permute-start(bf16[4,576]{1,0:T(4,128)(2,1)S(1)} %pad_maximum_fusion.9), channel_id=1, source_target_pairs={{0,2},{1,3},{2,0},{3,1},{4,6},{5,7},{6,4},{7,5},{8,10},{9,11},{10,... | collective-permute-start | bytes 13832 | tf_op jit(solution)/shard_map/ppermute | solution.py:437
  43.7 22.9 %collective-permute-start.3 = (bf16[4,48,2304]{2,1,0:T(8,128)(2,1)S(1)}, bf16[4,48,2304]{2,1,0:T(8,128)(2,1)S(1)}, u32[]{:S(2)}, u32[]{:S(2)}) collective-permute-start(bf16[4,48,2304]{2,1,0:T(8,128)(2,1)S(1)} %pad_maximum_fusion.1.p0), channel_id=1, source_target_pairs={{0,2},{1,3},{2,0},{3,1},{4,6},{5,7},{6,4},{7,5},{8,10},{9,11},{10,... | collective-permute-start | bytes 2654216 | tf_op jit(solution)/shard_map/ppermute | solution.py:437
  46.7 24.2 %collective-permute-start.4 = (bf16[4,48,2304]{2,1,0:T(8,128)(2,1)S(1)}, bf16[4,48,2304]{2,1,0:T(8,128)(2,1)S(1)}, u32[]{:S(2)}, u32[]{:S(2)}) collective-permute-start(bf16[4,48,2304]{2,1,0:T(8,128)(2,1)S(1)} %pad_maximum_fusion.1.p0), channel_id=1, source_target_pairs={{0,1},{1,0},{2,3},{3,2},{4,5},{5,4},{6,7},{7,6},{8,9},{9,8},{10,11... | collective-permute-start | bytes 2654216 | tf_op jit(solution)/shard_map/ppermute | solution.py:437
  265.0 110.2 %collective-permute-start.11 = (bf16[2,8,768]{2,1,0:T(8,128)(2,1)S(1)}, bf16[2,8,768]{2,1,0:T(8,128)(2,1)S(1)}, u32[]{:S(2)}, u32[]{:S(2)}) collective-permute-start(bf16[2,8,768]{2,1,0:T(8,128)(2,1)S(1)} %divide_convert_fusion), channel_id=1, source_target_pairs={{0,4},{1,5},{2,6},{3,7},{4,0},{5,1},{6,2},{7,3},{8,12},{9,13},{10,... | collective-permute-start | bytes 73736 | tf_op jit(solution)/shard_map/ppermute | solution.py:437
  265.1 111.5 %collective-permute-start.12 = (bf16[2,8,768]{2,1,0:T(8,128)(2,1)S(1)}, bf16[2,8,768]{2,1,0:T(8,128)(2,1)S(1)}, u32[]{:S(2)}, u32[]{:S(2)}) collective-permute-start(bf16[2,8,768]{2,1,0:T(8,128)(2,1)S(1)} %divide_convert_fusion), channel_id=1, source_target_pairs={{0,8},{1,9},{2,10},{3,11},{4,12},{5,13},{6,14},{7,15},{8,0},{9,1},... | collective-permute-start | bytes 73736 | tf_op jit(solution)/shard_map/ppermute | solution.py:437
  267.3 111.3 %collective-permute-start.13 = (bf16[2,8,768]{2,1,0:T(8,128)(2,1)S(1)}, bf16[2,8,768]{2,1,0:T(8,128)(2,1)S(1)}, u32[]{:S(2)}, u32[]{:S(2)}) collective-permute-start(bf16[2,8,768]{2,1,0:T(8,128)(2,1)S(1)} %divide_convert_fusion), channel_id=1, source_target_pairs={{0,12},{1,13},{2,14},{3,15},{4,8},{5,9},{6,10},{7,11},{8,4},{9,5},... | collective-permute-start | bytes 73736 | tf_op jit(solution)/shard_map/ppermute | solution.py:437
  280.1 181.1 %collective-permute-start.53 = (bf16[8,192,768]{2,1,0:T(8,128)(2,1)}, bf16[8,192,768]{2,1,0:T(8,128)(2,1)}, u32[]{:S(2)}, u32[]{:S(2)}) collective-permute-start(bf16[8,192,768]{2,1,0:T(8,128)(2,1)} %get-tuple-element.110), channel_id=1, source_target_pairs={{0,1},{1,0},{2,3},{3,2},{4,5},{5,4},{6,7},{7,6},{8,9},{9,8},{10,11... | collective-permute-start | bytes 7077896 | tf_op jit(solution)/shard_map/ppermute | solution.py:437
  337.9 31.4 %collective-permute-start.35 = (f32[4,2,576]{2,1,0:T(2,128)S(1)}, f32[4,2,576]{2,1,0:T(2,128)S(1)}, u32[]{:S(2)}, u32[]{:S(2)}) collective-permute-start(f32[4,2,576]{2,1,0:T(2,128)S(1)} %bitcast.290), channel_id=1, source_target_pairs={{0,1},{1,0},{2,3},{3,2},{4,5},{5,4},{6,7},{7,6},{8,9},{9,8},{10,11... | collective-permute-start | bytes 55304 | tf_op jit(solution)/shard_map/ppermute | solution.py:437
  375.1 90.5 %collective-permute-start.47 = (bf16[8,48,3072]{2,1,0:T(8,128)(2,1)}, bf16[8,48,3072]{2,1,0:T(8,128)(2,1)}, u32[]{:S(2)}, u32[]{:S(2)}) collective-permute-start(bf16[8,48,3072]{2,1,0:T(8,128)(2,1)} %get-tuple-element.108), channel_id=1, source_target_pairs={{0,1},{1,0},{2,3},{3,2},{4,5},{5,4},{6,7},{7,6},{8,9},{9,8},{10,11... | collective-permute-start | bytes 7077896 | tf_op jit(solution)/shard_map/ppermute | solution.py:437
  378.9 18.9 %collective-permute-start.41 = (bf16[8,48,768]{2,1,0:T(8,128)(2,1)}, bf16[8,48,768]{2,1,0:T(8,128)(2,1)S(1)}, u32[]{:S(2)}, u32[]{:S(2)}) collective-permute-start(bf16[8,48,768]{2,1,0:T(8,128)(2,1)} %get-tuple-element.104), channel_id=1, source_target_pairs={{0,1},{1,0},{2,3},{3,2},{4,5},{5,4},{6,7},{7,6},{8,9},{9,8},{10,11... | collective-permute-start | bytes 1769480 | tf_op jit(solution)/shard_map/ppermute | solution.py:437
  403.5 18.9 %collective-permute-start.24 = (bf16[4,48,768]{2,1,0:T(8,128)(2,1)}, bf16[4,48,768]{2,1,0:T(8,128)(2,1)}, u32[]{:S(2)}, u32[]{:S(2)}) collective-permute-start(bf16[4,48,768]{2,1,0:T(8,128)(2,1)} %get-tuple-element.145), channel_id=1, source_target_pairs={{0,2},{1,3},{2,0},{3,1},{4,6},{5,7},{6,4},{7,5},{8,10},{9,11},{10,... | collective-permute-start | bytes 884744 | tf_op jit(solution)/shard_map/ppermute | solution.py:437
  449.6 18.7 %collective-permute-start.46 = (bf16[48,768]{1,0:T(8,128)(2,1)S(1)}, bf16[48,768]{1,0:T(8,128)(2,1)S(1)}, u32[]{:S(2)}, u32[]{:S(2)}) collective-permute-start(bf16[48,768]{1,0:T(8,128)(2,1)S(1)} %fusion.33), channel_id=1, source_target_pairs={{0,16},{16,0},{1,17},{17,1},{2,18},{18,2},{3,19},{19,3},{4,20},{20... | collective-permute-start | bytes 221192 | tf_op jit(solution)/shard_map/ppermute | solution.py:441
  463.6 29.0 %collective-permute-start.54 = (bf16[4,192,768]{2,1,0:T(8,128)(2,1)S(1)}, bf16[4,192,768]{2,1,0:T(8,128)(2,1)S(1)}, u32[]{:S(2)}, u32[]{:S(2)}) collective-permute-start(bf16[4,192,768]{2,1,0:T(8,128)(2,1)S(1)} %get-tuple-element.122), channel_id=1, source_target_pairs={{0,2},{1,3},{2,0},{3,1},{4,6},{5,7},{6,4},{7,5},{8,10},{9,11},{10,... | collective-permute-start | bytes 3538952 | tf_op jit(solution)/shard_map/ppermute | solution.py:437
  468.1 46.0 %collective-permute-start.48 = (bf16[4,48,3072]{2,1,0:T(8,128)(2,1)S(1)}, bf16[4,48,3072]{2,1,0:T(8,128)(2,1)S(1)}, u32[]{:S(2)}, u32[]{:S(2)}) collective-permute-start(bf16[4,48,3072]{2,1,0:T(8,128)(2,1)S(1)} %get-tuple-element.124), channel_id=1, source_target_pairs={{0,2},{1,3},{2,0},{3,1},{4,6},{5,7},{6,4},{7,5},{8,10},{9,11},{10,... | collective-permute-start | bytes 3538952 | tf_op jit(solution)/shard_map/ppermute | solution.py:437
  492.8 24.5 %collective-permute-start.55 = (bf16[192,768]{1,0:T(8,128)(2,1)S(1)}, bf16[192,768]{1,0:T(8,128)(2,1)S(1)}, u32[]{:S(2)}, u32[]{:S(2)}) collective-permute-start(bf16[192,768]{1,0:T(8,128)(2,1)S(1)} %get-tuple-element.134), channel_id=1, source_target_pairs={{0,4},{1,5},{2,6},{3,7},{4,0},{5,1},{6,2},{7,3},{8,12},{9,13},{10,... | collective-permute-start | bytes 884744 | tf_op jit(solution)/shard_map/ppermute | solution.py:437
  496.4 21.5 %collective-permute-start.56 = (bf16[192,768]{1,0:T(8,128)(2,1)S(1)}, bf16[192,768]{1,0:T(8,128)(2,1)S(1)}, u32[]{:S(2)}, u32[]{:S(2)}) collective-permute-start(bf16[192,768]{1,0:T(8,128)(2,1)S(1)} %get-tuple-element.136), channel_id=1, source_target_pairs={{0,8},{1,9},{2,10},{3,11},{4,12},{5,13},{6,14},{7,15},{8,0},{9,1},... | collective-permute-start | bytes 884744 | tf_op jit(solution)/shard_map/ppermute | solution.py:437
  497.4 20.5 %collective-permute-start.57 = (bf16[192,768]{1,0:T(8,128)(2,1)S(1)}, bf16[192,768]{1,0:T(8,128)(2,1)S(1)}, u32[]{:S(2)}, u32[]{:S(2)}) collective-permute-start(bf16[192,768]{1,0:T(8,128)(2,1)S(1)} %get-tuple-element.135), channel_id=1, source_target_pairs={{0,12},{1,13},{2,14},{3,15},{4,8},{5,9},{6,10},{7,11},{8,4},{9,5},... | collective-permute-start | bytes 884744 | tf_op jit(solution)/shard_map/ppermute | solution.py:437
  514.4 19.8 %collective-permute-start.50 = (bf16[48,3072]{1,0:T(8,128)(2,1)S(1)}, bf16[48,3072]{1,0:T(8,128)(2,1)S(1)}, u32[]{:S(2)}, u32[]{:S(2)}) collective-permute-start(bf16[48,3072]{1,0:T(8,128)(2,1)S(1)} %get-tuple-element.139), channel_id=1, source_target_pairs={{0,8},{1,9},{2,10},{3,11},{4,12},{5,13},{6,14},{7,15},{8,0},{9,1},... | collective-permute-start | bytes 884744 | tf_op jit(solution)/shard_map/ppermute | solution.py:437
  517.3 22.5 %collective-permute-start.51 = (bf16[48,3072]{1,0:T(8,128)(2,1)S(1)}, bf16[48,3072]{1,0:T(8,128)(2,1)S(1)}, u32[]{:S(2)}, u32[]{:S(2)}) collective-permute-start(bf16[48,3072]{1,0:T(8,128)(2,1)S(1)} %get-tuple-element.138), channel_id=1, source_target_pairs={{0,12},{1,13},{2,14},{3,15},{4,8},{5,9},{6,10},{7,11},{8,4},{9,5},... | collective-permute-start | bytes 884744 | tf_op jit(solution)/shard_map/ppermute | solution.py:437
  518.0 22.6 %collective-permute-start.58 = (bf16[192,768]{1,0:T(8,128)(2,1)S(1)}, bf16[192,768]{1,0:T(8,128)(2,1)S(1)}, u32[]{:S(2)}, u32[]{:S(2)}) collective-permute-start(bf16[192,768]{1,0:T(8,128)(2,1)S(1)} %fusion.7), channel_id=1, source_target_pairs={{0,16},{16,0},{1,17},{17,1},{2,18},{18,2},{3,19},{19,3},{4,20},{20... | collective-permute-start | bytes 884744 | tf_op jit(solution)/shard_map/ppermute | solution.py:441
  (59 other events, 659.4 us)
Sparse Core Ops, SparseCore 0:
  10.3 46.7 all-gather.3
  59.4 53.7 all-gather.5
  115.5 51.9 all-gather.7

commit v2 on v1

v2 whole, which is shorter than its diff:
```python
import functools

import jax
import jax.numpy as jnp
from jax import lax
from jax.experimental import pallas as pl
from jax.experimental.pallas import tpu as pltpu
from jax.sharding import PartitionSpec as P

D = 768
H = 12
HD = 64
FF = 3072
SEQ = 512
SEGS = 8
GROUPS = 3
GW = D // GROUPS
PAIRS = GW // 128
BLOCK = 128
BLOCKS = SEQ // BLOCK
WIDE = 3 * BLOCK

epsilon = 1e-12
root_half = 0.7071067811865476
masked_score = -1e30
pdf_scale = 0.3989422804014327

BF = jnp.bfloat16
F32 = jnp.float32
VMEM_LIMIT = 56 * 2**20


def dot(a, b):
    return jnp.dot(a, b, preferred_element_type=F32)


def dot_t(a, b):
    return lax.dot_general(a, b, (((1,), (1,)), ((), ())), preferred_element_type=F32)


def t_dot(a, b):
    return lax.dot_general(a, b, (((0,), (0,)), ((), ())), preferred_element_type=F32)


def window(qb):
    return max(0, (qb - 1) * BLOCK), min(SEQ, (qb + 2) * BLOCK)


def call(kernel, grid, in_specs, out_specs, out_shape, us, scratch=(), prefetch=0, after=()):
    first = prefetch + len(in_specs)

    def run(*refs):
        kernel(*refs[:first], *refs[first + len(after) :])

    return functools.partial(
        lambda extra, *args: pl.pallas_call(
            run,
            grid_spec=pltpu.PrefetchScalarGridSpec(
                num_scalar_prefetch=prefetch,
                grid=grid,
                in_specs=list(in_specs) + [pl.BlockSpec(memory_space=pl.ANY)] * len(extra),
                out_specs=out_specs,
                scratch_shapes=list(scratch),
            ),
            out_shape=out_shape,
            compiler_params=pltpu.CompilerParams(vmem_limit_bytes=VMEM_LIMIT),
            cost_estimate=pl.CostEstimate(
                flops=int(us * 1.15e9), bytes_accessed=int(us * 3.6e6), transcendentals=0
            ),
        )(*args, *extra),
        tuple(after),
    )


def shaped(shape, dtype):
    return jax.ShapeDtypeStruct(shape, dtype)


def whole(shape):
    return pl.BlockSpec(shape, lambda *_: (0,) * len(shape), pipeline_mode=pl.Buffered(1))


ANY = pl.BlockSpec(memory_space=pl.ANY)


def pack_weights(w_out, w_up, w_down):
    blocks = [w_up[:, i * D : (i + 1) * D] for i in range(FF // D)]
    return jnp.concatenate([w_out] + blocks + [w_down], axis=0)


def weight_copies(name, refs, target, sems):
    if len(refs) == 3:
        source = refs[("out", "up", "down").index(name)]
        return [pltpu.make_async_copy(source, target, sems.at[0])]
    packed = refs[0]
    ranks = packed.shape[0]
    r = D // ranks
    copies = []
    for o in range(ranks):
        if name == "out":
            parts = [(slice(0, r), target.at[o * r : (o + 1) * r])]
        elif name == "up":
            parts = [
                (
                    slice((1 + i) * r, (2 + i) * r),
                    target.at[o * r : (o + 1) * r, i * D : (i + 1) * D],
                )
                for i in range(FF // D)
            ]
        else:
            n = FF // ranks
            parts = [(slice(5 * r, 5 * r + n), target.at[o * n : (o + 1) * n])]
        for rows, where in parts:
            copies.append(pltpu.make_async_copy(packed.at[o, rows], where, sems.at[len(copies)]))
    return copies


def start_all(copies):
    for copy in copies:
        copy.start()


def wait_all(copies):
    for copy in copies:
        copy.wait()


def segment_of(places, lengths_ref, row):
    total = jnp.int32(0)
    segment = jnp.zeros(places.shape, jnp.int32)
    for s in range(SEGS):
        total = total + lengths_ref[row, s]
        segment = segment + (places >= total).astype(jnp.int32)
    return segment


def both_heads(x2):
    low = lax.broadcasted_iota(jnp.int32, (1, 128), 1) < HD
    zero = jnp.zeros_like(x2)
    return jnp.concatenate([jnp.where(low, x2, zero), jnp.where(low, zero, x2)], axis=0)


def attend_forward_kernel(
    lengths_ref, tok_ref, wq_ref, wk_ref, wv_ref, bias_ref, q_ref, k_ref, v_ref, p_ref, m_ref, vt, ot
):
    row = pl.program_id(1)
    tok = tok_ref[...]
    q_ref[...] = (dot(tok, wq_ref[...]) + bias_ref[0, 0:1, :]).astype(BF) * jnp.asarray(0.125, BF)
    k_ref[...] = dot(tok, wk_ref[...]).astype(BF)
    v = dot(tok, wv_ref[...]) + bias_ref[0, 1:2, :]
    v_ref[...] = v.astype(BF)
    vt[...] = v.T.astype(BF)
    for qb in range(BLOCKS):
        lo, hi = window(qb)
        width = hi - lo
        rows = slice(qb * BLOCK, (qb + 1) * BLOCK)
        seg_q = segment_of(
            lax.broadcasted_iota(jnp.int32, (1, BLOCK), 1) + qb * BLOCK, lengths_ref, row
        )
        seg_k = segment_of(
            lax.broadcasted_iota(jnp.int32, (width, 1), 0) + lo, lengths_ref, row
        )
        mask = jnp.where(jnp.concatenate([seg_q, seg_q], axis=1) == seg_k, 0.0, masked_score)
        for pair in range(PAIRS):
            lanes = slice(pair * 128, (pair + 1) * 128)
            s = dot_t(k_ref[lo:hi, lanes], both_heads(q_ref[rows, lanes])) + mask
            w = jnp.exp(s - jnp.max(s, axis=0, keepdims=True))
            p = (w * (1.0 / jnp.sum(w, axis=0, keepdims=True))).astype(BF)
            p_ref[0, pair, qb, :width, :] = p
            o = dot(vt[lanes, lo:hi], p)
            ot[pair * 128 : pair * 128 + HD, rows] = o[:HD, :BLOCK]
            ot[pair * 128 + HD : (pair + 1) * 128, rows] = o[HD:, BLOCK:]
    m_ref[...] = ot[...].T.astype(BF)


def attend_forward(lengths, tokens, w_qkv, bias, after=()):
    t = tokens.shape[0]
    rows = t // SEQ
    row_spec = pl.BlockSpec((SEQ, GW), lambda g, r, *_: (r, g))
    p_shape = (GROUPS * rows, PAIRS, BLOCKS, WIDE, 2 * BLOCK)
    column = lambda part: pl.BlockSpec((D, GW), lambda g, r, *_: (0, part * GROUPS + g))
    return call(
        attend_forward_kernel,
        (GROUPS, rows),
        [
            pl.BlockSpec((SEQ, D), lambda g, r, *_: (r, 0)),
            column(0),
            column(1),
            column(2),
            pl.BlockSpec((1, 2, GW), lambda g, r, *_: (g, 0, 0)),
        ],
        [row_spec] * 3
        + [pl.BlockSpec((1,) + p_shape[1:], lambda g, r, *_: (g * rows + r, 0, 0, 0, 0)), row_spec],
        [shaped((t, D), BF)] * 3 + [shaped(p_shape, BF), shaped((t, D), BF)],
        us=28,
        scratch=[pltpu.VMEM((GW, SEQ), BF), pltpu.VMEM((GW, SEQ), F32)],
        prefetch=1,
        after=after,
    )(lengths, tokens, w_qkv, w_qkv, w_qkv, bias)


def attend_backward_kernel(
    groups, direct, halves, where_ref, datt_ref, tok_ref, m_ref, wrefs, q_ref, k_ref, v_ref, p_ref, dp_ref,
    sums_ref, wg_refs, wo, kt, qt, dk_acc, dv_acc, dw_acc, dw_low, wsems, sems,
):
    g = pl.program_id(0)
    row = pl.program_id(1)
    first = groups[0]
    with_out = first == 0
    last = pl.num_programs(1) - 1
    span = 3 * GW

    def emit(place):
        if direct:
            part = span // halves
            copies = term_copies(
                where_ref,
                lambda owner_rows, h: dw_low.at[owner_rows, h * part : (h + 1) * part],
                D,
                lambda ref, where: ref.at[
                    where + (slice(None), pl.ds(pl.multiple_of(place * part, 128), part))
                ],
                wg_refs,
                sems,
                halves,
            )
        else:
            where = pl.ds(pl.multiple_of(place * span, 128), span)
            copies = [pltpu.make_async_copy(dw_low, wg_refs[0].at[:, where], sems.at[0])]
        start_all(copies)
        wait_all(copies)

    def add_term(term, place):
        @pl.when(row == 0)
        def _():
            dw_acc[...] = term

        @pl.when((row > 0) & (row < last))
        def _():
            dw_acc[...] += term

        @pl.when(row == last)
        def _():
            dw_low[...] = (dw_acc[...] + term).astype(BF)
            emit(place)

    if with_out:

        @pl.when(g == 0)
        def _():
            add_term(t_dot(m_ref[...], datt_ref[...]), 0)

    @pl.when((g == with_out) & (row == 0))
    def _():
        copies = weight_copies("out", wrefs, wo, wsems)
        start_all(copies)
        wait_all(copies)

    def group_step():
        place = g - with_out
        wo_rows = wo[pl.ds(pl.multiple_of((place + first) * GW, GW), GW), :]
        dmix = dot_t(datt_ref[...], wo_rows).astype(BF)
        kt[...] = k_ref[...].astype(F32).T.astype(BF)
        dk_acc[...] = jnp.zeros_like(dk_acc)
        dv_acc[...] = jnp.zeros_like(dv_acc)
        for qb in range(BLOCKS):
            lo, hi = window(qb)
            width = hi - lo
            rows = slice(qb * BLOCK, (qb + 1) * BLOCK)
            for pair in range(PAIRS):
                lanes = slice(pair * 128, (pair + 1) * 128)
                dos = both_heads(dmix[rows, lanes])
                p_low = p_ref[0, pair, qb, :width, :]
                p = p_low.astype(F32)
                dp = dot_t(v_ref[lo:hi, lanes], dos)
                delta = jnp.sum(p * dp, axis=0, keepdims=True)
                ds = (p * (dp - delta)).astype(BF)
                dk_acc[lo:hi, lanes] += dot(ds, both_heads(q_ref[rows, lanes]))
                dv_acc[lo:hi, lanes] += dot(p_low, dos)
                dq = dot(kt[lanes, lo:hi], ds)
                qt[pair * 128 : pair * 128 + HD, rows] = dq[:HD, :BLOCK]
                qt[pair * 128 + HD : (pair + 1) * 128, rows] = dq[HD:, BLOCK:]
        dq = (qt[...] * 0.125).T.astype(BF)
        dv = dv_acc[...].astype(BF)
        dp_ref[:, :GW] = dq
        dp_ref[:, GW : 2 * GW] = dk_acc[...].astype(BF)
        dp_ref[:, 2 * GW :] = dv
        sums = jnp.concatenate(
            [
                jnp.sum(dq.astype(F32), axis=0, keepdims=True),
                jnp.sum(dv.astype(F32), axis=0, keepdims=True),
            ],
            axis=0,
        )
        sums_ref[...] = jnp.where(row == 0, sums, sums_ref[...] + sums)
        add_term(t_dot(tok_ref[...], dp_ref[...]), g)

    if with_out:
        pl.when(g > 0)(group_step)
    else:
        group_step()


RANKS = 16


def term_copies(where_ref, source, total_rows, target, refs, sems, halves):
    me, replica = where_ref[0], where_ref[1]
    rows = total_rows // RANKS
    copies = []
    for j in range(RANKS):
        owner_rows = pl.ds(pl.multiple_of((me ^ j) * rows, rows), rows)
        place = ((j >> 1) & 1, j >> 2)
        for h in range(halves):
            where = ((h ^ replica,) if halves == 2 else ()) + place
            copies.append(
                pltpu.make_async_copy(
                    source(owner_rows, h), target(refs[j & 1], where), sems.at[halves * j + h]
                )
            )
    return copies


def attend_backward(where, datt, tokens, weights, groups, kept, direct, halves, after=()):
    q, k, v, p, mixed = kept
    t = datt.shape[0]
    rows = t // SEQ
    count, first = len(groups), groups[0]
    extra = int(first == 0)
    group = lambda g: jnp.maximum(g - extra, 0) + first
    row_spec = pl.BlockSpec((SEQ, GW), lambda g, r, *_: (r, group(g)))
    full_row = pl.BlockSpec((SEQ, D), lambda g, r, *_: (r, 0))
    columns = (count + extra) * 3 * GW
    if direct:
        lead = (2, 2, 4) if halves == 2 else (2, 4)
        wg_shapes = [shaped(lead + (D // RANKS, columns // halves), BF)] * 2
    else:
        wg_shapes = [shaped((D, columns), BF)]
    nw, ng = len(weights), len(wg_shapes)

    def kernel(where_ref, datt_ref, tok_ref, m_ref, *refs):
        wrefs, refs = refs[:nw], refs[nw:]
        q_ref, k_ref, v_ref, p_ref, dp_ref, sums_ref = refs[:6]
        wg_refs, scratch = refs[6 : 6 + ng], refs[6 + ng :]
        attend_backward_kernel(
            groups, direct, halves, where_ref, datt_ref, tok_ref, m_ref, wrefs, q_ref, k_ref, v_ref, p_ref,
            dp_ref, sums_ref, wg_refs, *scratch,
        )

    m_spec = pl.BlockSpec((SEQ, D), lambda g, r, *_: (jnp.where(g == 0, r, rows - 1), 0))
    return call(
        kernel,
        (count + extra, rows),
        [full_row, full_row, m_spec if extra else ANY]
        + [ANY] * nw
        + [
            row_spec,
            row_spec,
            row_spec,
            pl.BlockSpec((1,) + p.shape[1:], lambda g, r, *_: (group(g) * rows + r, 0, 0, 0, 0)),
        ],
        [
            pl.BlockSpec(
                (SEQ, 3 * GW), lambda g, r, *_: (jnp.where(g < extra, 0, r), jnp.maximum(g - extra, 0))
            ),
            pl.BlockSpec((2, GW), lambda g, r, *_: (0, jnp.maximum(g - extra, 0))),
        ]
        + [ANY] * ng,
        [shaped((t, count * 3 * GW), BF), shaped((2, count * GW), F32)] + wg_shapes,
        us=1,
        scratch=[
            pltpu.VMEM((D, D), BF),
            pltpu.VMEM((GW, SEQ), BF),
            pltpu.VMEM((GW, SEQ), F32),
            pltpu.VMEM((SEQ, GW), F32),
            pltpu.VMEM((SEQ, GW), F32),
            pltpu.VMEM((D, 3 * GW), F32),
            pltpu.VMEM((D, 3 * GW), BF),
            pltpu.SemaphoreType.DMA((16,)),
            pltpu.SemaphoreType.DMA((2 * RANKS,)),
        ],
        prefetch=1,
        after=after,
    )(where, datt, tokens, mixed, *weights, q, k, v, p)


TB = 256
CH = 768


def normalize(values):
    centered = values - jnp.mean(values, axis=-1, keepdims=True)
    variance = jnp.mean(centered * centered, axis=-1, keepdims=True)
    inverse = lax.rsqrt(variance + epsilon)
    return centered * inverse, inverse


def normalize_back(grad, xhat, inverse):
    mean = jnp.mean(grad, axis=-1, keepdims=True)
    along = jnp.mean(grad * xhat, axis=-1, keepdims=True)
    return (grad - mean - xhat * along) * inverse


def add_rows(ref, rows):
    stacked = jnp.concatenate([jnp.sum(r, axis=0, keepdims=True) for r in rows], axis=0)
    ref[...] = jnp.where(pl.program_id(0) == 0, stacked, ref[...] + stacked)


def up(tokens, mixed, weights, vec, bias_up, after=()):
    t = tokens.shape[0]
    nw = len(weights)

    def kernel(tok_ref, m_ref, vec_ref, bu_ref, *refs):
        wrefs, refs = refs[:nw], refs[nw:]
        xhat_ref, inv_ref, nl_ref, act_ref, gp_ref, wo, wu, so, su = refs
        out_copies = weight_copies("out", wrefs, wo, so)
        up_copies = weight_copies("up", wrefs, wu, su)

        @pl.when(pl.program_id(0) == 0)
        def _():
            start_all(out_copies)
            start_all(up_copies)
            wait_all(out_copies)

        att = dot(m_ref[...], wo[...]) + vec_ref[0:1, :]
        xhat, inverse = normalize(tok_ref[...].astype(F32) + att)
        xhat_ref[...] = xhat
        inv_ref[...] = inverse
        nl_ref[...] = (xhat * vec_ref[1:2, :] + vec_ref[2:3, :]).astype(BF)

        @pl.when(pl.program_id(0) == 0)
        def _():
            wait_all(up_copies)

        nl = nl_ref[...]
        for c in range(0, FF, CH):
            u = dot(nl, wu[:, c : c + CH]) + bu_ref[:, c : c + CH]
            cdf = 0.5 * (1.0 + lax.erf(u * root_half))
            act_ref[:, c : c + CH] = (u * cdf).astype(BF)
            gp_ref[:, c : c + CH] = (cdf + u * (jnp.exp(u * u * -0.5) * pdf_scale)).astype(BF)

    tok = lambda n: pl.BlockSpec((TB, n), lambda i: (i, 0))
    return call(
        kernel,
        (t // TB,),
        [tok(D), tok(D), whole((3, D)), whole((1, FF))] + [ANY] * nw,
        [tok(D), tok(1), tok(D), tok(FF), tok(FF)],
        [shaped((t, D), F32), shaped((t, 1), F32), shaped((t, D), BF), shaped((t, FF), BF), shaped((t, FF), BF)],
        us=18,
        scratch=[
            pltpu.VMEM((D, D), BF),
            pltpu.VMEM((D, FF), BF),
            pltpu.SemaphoreType.DMA((16,)),
            pltpu.SemaphoreType.DMA((64,)),
        ],
        after=after,
    )(tokens, mixed, vec, bias_up, *weights)


def down(lengths, active, xhat, weights, vec, cot, after=()):
    t = cot.shape[0]
    nw = len(weights)
    per_row = SEQ // TB

    def kernel(lengths_ref, act_ref, xhat_ref, vec_ref, cot_ref, *refs):
        wrefs, refs = refs[:nw], refs[nw:]
        out_ref, ds_ref, dd_ref, sums_ref, pool_ref, wd, sems = refs
        i = pl.program_id(0)

        @pl.when(i == 0)
        def _():
            copies = weight_copies("down", wrefs, wd, sems)
            start_all(copies)
            wait_all(copies)

        normed = xhat_ref[...] * vec_ref[0:1, :] + vec_ref[1:2, :]
        second = normed + (dot(act_ref[...], wd[...]) + vec_ref[2:3, :])
        xhat, inverse = normalize(second)
        out = (xhat * vec_ref[3:4, :] + vec_ref[4:5, :]).astype(BF)
        out_ref[...] = out
        cot = cot_ref[...].astype(F32)
        d_second = normalize_back(cot * vec_ref[3:4, :], xhat, inverse)
        ds_ref[...] = d_second
        d_down = d_second.astype(BF)
        dd_ref[...] = d_down
        add_rows(sums_ref, (d_down.astype(F32), cot * xhat, cot))
        row = i // per_row
        places = lax.broadcasted_iota(jnp.int32, (1, TB), 1) + (i % per_row) * TB
        segment = segment_of(places, lengths_ref, row)
        ids = lax.broadcasted_iota(jnp.int32, (SEGS, TB), 0)
        sums = dot(jnp.where(segment == ids, 1.0, 0.0).astype(BF), out)
        pool_ref[0] = jnp.where(i % per_row == 0, sums, pool_ref[0] + sums)

    tok = lambda n: pl.BlockSpec((TB, n), lambda i, *_: (i, 0))
    return call(
        kernel,
        (t // TB,),
        [tok(FF), tok(D), whole((5, D)), tok(D)] + [ANY] * nw,
        [
            tok(D),
            tok(D),
            tok(D),
            pl.BlockSpec((3, D), lambda i, *_: (0, 0)),
            pl.BlockSpec((1, SEGS, D), lambda i, *_: (i // per_row, 0, 0)),
        ],
        [
            shaped((t, D), BF),
            shaped((t, D), F32),
            shaped((t, D), BF),
            shaped((3, D), F32),
            shaped((t // SEQ, SEGS, D), F32),
        ],
        us=14,
        scratch=[pltpu.VMEM((FF, D), BF), pltpu.SemaphoreType.DMA((16,))],
        prefetch=1,
        after=after,
    )(lengths, active, xhat, vec, cot, *weights)


def back_up(d_down, gp, weights, after=()):
    t = d_down.shape[0]
    nw = len(weights)

    def kernel(dd_ref, gp_ref, *refs):
        wrefs, refs = refs[:nw], refs[nw:]
        du_ref, su_ref, wd, sd = refs
        i = pl.program_id(0)

        @pl.when(i == 0)
        def _():
            down_copies = weight_copies("down", wrefs, wd, sd)
            start_all(down_copies)
            wait_all(down_copies)

        dd = dd_ref[...]
        for c in range(0, FF, CH):
            du = (dot_t(dd, wd[c : c + CH, :]) * gp_ref[:, c : c + CH].astype(F32)).astype(BF)
            du_ref[:, c : c + CH] = du
            partial = jnp.sum(du.astype(F32), axis=0, keepdims=True)
            su_ref[:, c : c + CH] = jnp.where(i == 0, partial, su_ref[:, c : c + CH] + partial)

    tok = lambda n: pl.BlockSpec((TB, n), lambda i: (i, 0))
    return call(
        kernel,
        (t // TB,),
        [tok(D), tok(FF)] + [ANY] * nw,
        [tok(FF), pl.BlockSpec((1, FF), lambda i: (0, 0))],
        [shaped((t, FF), BF), shaped((1, FF), F32)],
        us=11,
        scratch=[pltpu.VMEM((FF, D), BF), pltpu.SemaphoreType.DMA((16,))],
        after=after,
    )(d_down, gp, *weights)


def back_first(d_upper, d_second, xhat, inverse, weights, gain, after=()):
    t = d_upper.shape[0]
    nw = len(weights)

    def kernel(du_ref, ds_ref, xhat_ref, inv_ref, gain_ref, *refs):
        wrefs, refs = refs[:nw], refs[nw:]
        df_ref, da_ref, sums_ref, wu, su = refs

        @pl.when(pl.program_id(0) == 0)
        def _():
            up_copies = weight_copies("up", wrefs, wu, su)
            start_all(up_copies)
            wait_all(up_copies)

        d_normed = ds_ref[...] + dot_t(du_ref[...], wu[...])
        xhat = xhat_ref[...]
        d_first = normalize_back(d_normed * gain_ref[...], xhat, inv_ref[...])
        df_ref[...] = d_first
        d_att = d_first.astype(BF)
        da_ref[...] = d_att
        add_rows(sums_ref, (d_att.astype(F32), d_normed * xhat, d_normed))

    tok = lambda n: pl.BlockSpec((TB, n), lambda i: (i, 0))
    return call(
        kernel,
        (t // TB,),
        [tok(FF), tok(D), tok(D), tok(1), whole((1, D))] + [ANY] * nw,
        [tok(D), tok(D), pl.BlockSpec((3, D), lambda i: (0, 0))],
        [shaped((t, D), F32), shaped((t, D), BF), shaped((3, D), F32)],
        us=1,
        scratch=[pltpu.VMEM((D, FF), BF), pltpu.SemaphoreType.DMA((64,))],
        after=after,
    )(d_upper, d_second, xhat, inverse, gain, *weights)


def input_gradient(d_first, d_projected, w_qkv, after=()):
    t = d_first.shape[0]

    def kernel(df_ref, p0, p1, w_ref, out_ref):
        total = df_ref[...]
        g = 0
        for p in (p0, p1):
            for local in range(p.shape[1] // D):
                for part in range(3):
                    start = part * D + g * GW
                    at = local * D + part * GW
                    total = total + dot_t(p[:, at : at + GW], w_ref[:, start : start + GW])
                g += 1
        out_ref[...] = total

    tok = lambda n: pl.BlockSpec((TB, n), lambda i: (i, 0))
    return call(
        kernel,
        (t // TB,),
        [tok(D), tok(d_projected[0].shape[1]), tok(d_projected[1].shape[1]), whole((D, 3 * D))],
        tok(D),
        shaped((t, D), F32),
        us=9,
        after=after,
    )(d_first, *d_projected, w_qkv)


def grad_down(where, active, d_down, direct, after=()):
    t = d_down.shape[0]
    half = D // 2
    blocks = 4
    n = FF // blocks

    def kernel(where_ref, a_ref, b_ref, *refs):
        outs, (acc, sems) = refs[:-2], refs[-2:]
        i = pl.program_id(0)
        if not direct:
            outs[0][...] = t_dot(a_ref[...], b_ref[...]).astype(BF)
            return
        acc[pl.ds(pl.multiple_of(i * n, n), n), :] = t_dot(a_ref[...], b_ref[...]).astype(BF)

        @pl.when(i == blocks - 1)
        def _():
            copies = term_copies(
                where_ref,
                lambda owner_rows, h: acc.at[owner_rows, h * half : (h + 1) * half],
                FF,
                lambda ref, where: ref.at[where],
                outs,
                sems,
                2,
            )
            start_all(copies)
            wait_all(copies)

    if direct:
        out_shapes, out_specs = [shaped((2, 2, 4, FF // RANKS, half), BF)] * 2, [ANY] * 2
    else:
        out_shapes, out_specs = [shaped((FF, D), BF)], [pl.BlockSpec((n, D), lambda i, *_: (i, 0))]
    return call(
        kernel,
        (blocks,),
        [pl.BlockSpec((t, n), lambda i, *_: (0, i)), whole((t, D))],
        out_specs,
        out_shapes,
        us=10,
        scratch=[pltpu.VMEM((FF, D), BF), pltpu.SemaphoreType.DMA((2 * RANKS,))],
        prefetch=1,
        after=after,
    )(where, active, d_down)


def grad_up(nl, d_upper, after=()):
    t = nl.shape[0]
    n = 768

    def kernel(nl_ref, du_ref, out_ref):
        out_ref[...] = t_dot(nl_ref[...], du_ref[...]).astype(BF)

    return call(
        kernel,
        (FF // n,),
        [whole((t, D)), pl.BlockSpec((t, n), lambda i: (0, i))],
        pl.BlockSpec((D, n), lambda i: (0, i)),
        shaped((D, FF), BF),
        us=9,
        after=after,
    )(nl, d_upper)


def swap(x, mask):
    return lax.ppermute(x, "fsdp", [(i, i ^ mask) for i in range(RANKS)])


def swap_replica(x):
    return lax.ppermute(x, "replica", [(0, 1), (1, 0)])


def added(*terms):
    total = terms[0].astype(F32)
    for term in terms[1:]:
        total = total + term.astype(F32)
    return total


def gather_qkv(where, w, replica):
    rows, columns = w.shape
    half = columns // 2
    own = lax.dynamic_slice_in_dim(w, replica * half, half, 1)
    z = jnp.stack([own] + [swap(own, m) for m in (4, 8, 12)])
    zy = jnp.stack([z, swap(z, 2)])
    x = swap_replica(zy)
    pieces = (zy, x, swap(zy, 1), swap(x, 1))

    def kernel(where_ref, p0, p1, p2, p3, out_ref, sems):
        me, other = where_ref[0], where_ref[1]
        copies = []
        for index, piece in enumerate((p0, p1, p2, p3)):
            start = pl.multiple_of((other ^ (index % 2)) * half, 128)
            for y in range(2):
                for k in range(4):
                    owner = me ^ (4 * k + 2 * y + index // 2)
                    target = out_ref.at[
                        pl.ds(pl.multiple_of(owner * rows, rows), rows), pl.ds(start, half)
                    ]
                    copies.append(
                        pltpu.make_async_copy(piece.at[y, k], target, sems.at[len(copies)])
                    )
        start_all(copies)
        wait_all(copies)

    return call(
        kernel,
        (1,),
        [ANY] * 4,
        pl.BlockSpec((RANKS * rows, columns), lambda *_: (0, 0)),
        shaped((RANKS * rows, columns), BF),
        us=4,
        scratch=[pltpu.SemaphoreType.DMA((32,))],
        prefetch=1,
    )(where, *pieces)


def ordered(own, other, replica):
    first = jnp.where(replica == 0, own, other)
    second = jnp.where(replica == 0, other, own)
    return first, second


class Chain:
    def __init__(self, keep, send, lines=None, grow=False):
        self.columns = keep.shape[-1]
        flat = lambda x: x.reshape(-1, self.columns)
        halves = [(swap_replica,)] if keep.ndim == 5 else []
        over = lambda m: lambda x: swap(x, m)
        along_z = [(over(8),), (over(4),)] if grow else [(over(4), over(8), over(12))]
        fsdp = [(over(1),)] + halves + [(over(2),)] + along_z
        self.moves = fsdp + [(swap_replica,)]
        self.owner_rows = keep.shape[-2]
        self.stay, self.away = flat(keep), [flat(send)]
        self.lines = None if lines is None else flat(lines)
        self.rides = (len(fsdp) + 1 - len(halves)) if lines is not None else 0
        self.grow = grow

    def send(self):
        moves = self.moves.pop(0)
        self.received = [move(x) for move, x in zip(moves, self.away)]
        self.beside = []
        if self.rides and len(self.received[0]) == len(self.stay):
            self.beside = [moves[0](self.lines)]
        self.arriving = self.rides > 0
        self.rides = max(self.rides - 1, 0)


def add_all(chains, after=()):
    operands, shapes, plans = [], [], []
    for c in chains:
        n = c.stay.shape[0]
        parts = len(c.moves[0]) + 1 if n > c.owner_rows else 1
        part = n // parts
        held = c.lines.shape[0] if c.arriving else 0
        grown = held * (2 if c.grow else 1)
        rides = grown if c.rides else 0
        ins = [c.stay] + c.received + (c.beside + [c.lines] if held else [])
        outs = [shaped((part, c.columns), BF)]
        sends = parts - 1 if parts > 1 else int(rides > 0)
        outs += [shaped((part + rides, c.columns), BF)] * sends
        if held:
            outs.append(shaped((grown, c.columns), BF))
        plans.append((len(ins), len(outs), n, part, parts, sends, held, rides, len(c.received), len(c.beside), c.grow))
        operands += ins
        shapes += outs

    def kernel(*refs):
        sources, targets = refs[: len(operands)], refs[len(operands) :]
        for n_in, n_out, n, part, parts, sends, held, rides, arrivals, beside, grow in plans:
            ins, sources = sources[:n_in], sources[n_in:]
            outs, targets = targets[:n_out], targets[n_out:]
            received = ins[1 : 1 + arrivals]
            for p in range(parts):
                rows = slice(p * part, (p + 1) * part)
                total = ins[0][rows, :].astype(F32)
                for r in received:
                    total = total + r[rows, :].astype(F32)
                total = total.astype(BF)
                outs[p][:part, :] = total
                if parts == 1 and sends:
                    outs[1][:part, :] = total
            if held:
                mine = ins[-1][...]
                if beside:
                    others = [ins[1 + arrivals][...]]
                else:
                    others = [r[n : n + held, :] for r in received]
                if grow:
                    lines = jnp.concatenate([mine, others[0]], axis=0)
                else:
                    total = mine.astype(F32)
                    for other in others:
                        total = total + other.astype(F32)
                    lines = total.astype(BF)
                outs[-1][...] = lines
                if rides:
                    for out in outs[1 : 1 + sends]:
                        out[part:, :] = lines

    results = list(
        call(
            kernel,
            (1,),
            [whole(x.shape) for x in operands],
            [whole(x.shape) for x in shapes],
            shapes,
            us=2,
            after=after,
        )(*operands)
    )
    for c, plan in zip(chains, plans):
        n_out, sends, held = plan[1], plan[5], plan[6]
        mine, results = results[:n_out], results[n_out:]
        c.stay = mine[0]
        c.away = mine[1 : 1 + sends] if sends else [mine[0]]
        if held:
            c.lines = mine[-1]


SMALL = ("bias_qv", "bias_out", "gain_one", "shift_one", "bias_up", "bias_down", "gain_two", "shift_two")
SMALL_SIZES = (2 * D, D, D, D, FF, D, D, D)
PAD = 256


def body(
    ranks,
    replicas,
    tokens,
    lengths,
    w_qkv,
    bias_qv,
    w_out,
    bias_out,
    gain_one,
    shift_one,
    w_up,
    bias_up,
    w_down,
    bias_down,
    gain_two,
    shift_two,
    cotangent,
):
    direct = ranks == RANKS and replicas == 2
    me = lax.axis_index("fsdp")
    replica = lax.axis_index("replica")
    where = jnp.stack([me, replica]).astype(jnp.int32)
    gather = lambda w: lax.all_gather(w, "fsdp", axis=0, tiled=True)

    small = jnp.concatenate(
        [bias_qv, bias_out, gain_one, shift_one, bias_up, bias_down, gain_two, shift_two]
    )
    count = small.shape[0]
    lines = -(-count // PAD)
    small = jnp.pad(small, (0, lines * PAD - count)).reshape(lines, PAD)
    small = jnp.pad(small, ((0, w_qkv.shape[0] - lines), (0, 0)))
    first = jnp.concatenate([w_qkv, small], axis=1)
    if direct:
        w_first = gather_qkv(where, first, replica)
        packed = gather(pack_weights(w_out, w_up, w_down))
        weights = (packed.reshape(ranks, -1, D),)
    else:
        w_first = gather(first)
        weights = (gather(w_out), gather(w_up), gather(w_down))
    small_all = w_first.reshape(ranks, -1, 3 * D + PAD)[:, :lines, 3 * D :].reshape(ranks, -1)
    vectors, start = {}, 0
    for name, size in zip(SMALL, SMALL_SIZES):
        part = size // ranks
        vectors[name] = small_all[:, start : start + part].reshape(size).astype(F32)
        start += part

    bias = vectors["bias_qv"].reshape(2, GROUPS, GW).transpose(1, 0, 2)
    kept = attend_forward(lengths, tokens, w_first, bias)
    mixed = kept[4]
    vec_one = jnp.stack([vectors["bias_out"], vectors["gain_one"], vectors["shift_one"]])
    xhat, inverse, nl, active, gp = up(tokens, mixed, weights, vec_one, vectors["bias_up"][None])
    vec_two = jnp.stack(
        [vectors[n] for n in ("gain_one", "shift_one", "bias_down", "gain_two", "shift_two")]
    )
    layer_out, d_second, d_down, sums_two, pool = down(
        lengths, active, xhat, weights, vec_two, cotangent
    )
    pooled = pool / lengths.astype(F32)[:, :, None]

    terms_down = grad_down(where, active, d_down, direct)
    if direct:
        chain_w = Chain(*terms_down, pooled.astype(BF), True)
        chain_w.send()
    d_upper, sums_up = back_up(d_down, gp, weights, after=(terms_down[0],))
    if direct:
        add_all([chain_w], after=(sums_up,))
        chain_w.send()
        term_up = grad_up(nl, d_upper, after=(chain_w.away[0],))
    else:
        term_up = grad_up(nl, d_upper)
    first_args = (d_upper, d_second, xhat, inverse, weights, vectors["gain_one"][None])
    scatter = lambda x: lax.psum_scatter(x, "fsdp", scatter_dimension=0, tiled=True)

    def small_lines(sums_one, sums_a, sums_b):
        return jnp.concatenate(
            [
                jnp.concatenate([sums_a, sums_b], axis=1),
                sums_one,
                sums_up.reshape(-1, D),
                sums_two,
            ]
        )

    shard_up = scatter(term_up)
    if direct:
        d_first, d_att, sums_one = back_first(*first_args, after=(term_up,))
        attend_back = functools.partial(attend_backward, where, d_att, tokens, weights)
        dp_a, sums_a, *terms_a = attend_back((0, 1), kept, True, 2, after=(chain_w.away[0],))
        chain_a = Chain(*terms_a)
        add_all([chain_w], after=(sums_a,))
        chain_w.send()
        chain_a.send()
        dp_b, sums_b, *terms_b = attend_back((2,), kept, True, 1, after=(chain_w.away[0],))
        small = small_lines(sums_one, sums_a, sums_b)
        small = jnp.pad(small, ((0, -small.shape[0] % 16), (0, 0))).astype(BF)
        chain_b = Chain(*terms_b, small, False)
        chain_b.send()
        add_all([chain_w, chain_a], after=(sums_b,))
        chain_w.send()
        chain_a.send()
        input_grad = input_gradient(
            d_first, (dp_a, dp_b), w_first, after=(chain_a.away[0], shard_up)
        )
        add_all([chain_w, chain_a, chain_b], after=(input_grad,))
        chain_w.send()
        chain_a.send()
        chain_b.send()
        while chain_w.moves or chain_a.moves or chain_b.moves:
            moving = [c for c in (chain_w, chain_a, chain_b) if c.moves]
            add_all(moving)
            for c in moving:
                c.send()
        h0, h1 = ordered(chain_w.stay, chain_w.received[0][: chain_w.owner_rows], replica)
        grad_w_down = jnp.concatenate([h0, h1], axis=1).astype(F32)
        grad_w_up = added(shard_up, swap_replica(shard_up))
        h0, h1 = ordered(chain_a.stay, chain_a.received[0], replica)
        span = 3 * GW // 2
        halves_a = [
            jnp.concatenate([h[:, i * span : (i + 1) * span] for h in (h0, h1)], axis=1).astype(F32)
            for i in range(3)
        ]
        sum_b = added(chain_b.stay, chain_b.received[0][: chain_b.owner_rows])
        lines = added(chain_b.lines, chain_b.received[0][chain_b.owner_rows :])
        grad_w_out = halves_a[0]
        parts = halves_a[1:] + [sum_b]
        relative = chain_w.lines.reshape((2,) * 5 + pooled.shape)
        relative = relative.transpose(3, 1, 0, 2, 4, 5, 6, 7).reshape((2, ranks) + pooled.shape)
        pooled_all = relative[jnp.arange(2) ^ replica][:, me ^ jnp.arange(ranks)]
        pooled_all = pooled_all.reshape((2 * ranks * pooled.shape[0],) + pooled.shape[1:]).astype(F32)
    else:
        d_first, d_att, sums_one = back_first(*first_args)
        attend_back = functools.partial(attend_backward, where, d_att, tokens, weights)
        dp_a, sums_a, term_a = attend_back((0, 1), kept, False, 1)
        dp_b, sums_b, term_b = attend_back((2,), kept, False, 1)
        input_grad = input_gradient(d_first, (dp_a, dp_b), w_first)
        pooled_all = lax.all_gather(pooled, ("replica", "fsdp"), axis=0, tiled=True)
        reduce = lambda x: lax.psum(scatter(x), "replica").astype(F32)
        grad_w_down = reduce(terms_down[0])
        grad_w_up = lax.psum(shard_up, "replica").astype(F32)
        sum_a, sum_b = reduce(term_a), reduce(term_b)
        lines = lax.psum(small_lines(sums_one, sums_a, sums_b), ("replica", "fsdp"))
        grad_w_out = sum_a[:, :D]
        parts = [sum_a[:, D : 2 * D], sum_a[:, 2 * D :], sum_b]
    grad_w_qkv = jnp.concatenate(
        [p[:, i * GW : (i + 1) * GW] for i in range(3) for p in parts], axis=1
    )
    small_grads, start = {}, 0
    for name, size in zip(SMALL, SMALL_SIZES):
        values = lines[start // D : (start + size) // D].reshape(ranks, -1)
        small_grads[name] = lax.dynamic_index_in_dim(values, me, keepdims=False)
        start += size
    return (
        layer_out,
        input_grad,
        pooled_all,
        grad_w_qkv,
        small_grads["bias_qv"],
        grad_w_out,
        small_grads["bias_out"],
        small_grads["gain_one"],
        small_grads["shift_one"],
        grad_w_up,
        small_grads["bias_up"],
        grad_w_down,
        small_grads["bias_down"],
        small_grads["gain_two"],
        small_grads["shift_two"],
    )


def solution(mesh):
    rows = P(("replica", "fsdp"), None)
    matrix = P("fsdp", None)
    vector = P("fsdp")
    return jax.shard_map(
        functools.partial(body, mesh.shape["fsdp"], mesh.shape["replica"]),
        mesh=mesh,
        in_specs=(
            rows,
            rows,
            matrix,
            vector,
            matrix,
            vector,
            vector,
            vector,
            matrix,
            vector,
            matrix,
            vector,
            vector,
            vector,
            rows,
        ),
        out_specs=(
            rows,
            rows,
            P(),
            matrix,
            vector,
            matrix,
            vector,
            vector,
            vector,
            matrix,
            vector,
            matrix,
            vector,
            vector,
            vector,
        ),
        check_vma=False,
    )
```

time: 565 us -> 357 us (0.63)
  Pallas kernels: 292 us -> 190 us
  waiting for transfers between devices: 140 us -> 85.7 us
  starting transfers between devices: 62.9 us -> 30 us
  other arithmetic: 24.7 us -> 6 us
    pallas_call x17, Pallas kernels: 292 us -> 190 us  [call(): pl.pallas_call(run, grid_spec=pltpu.PrefetchScalarGridSpec(num_scalar_pre...]
    ppermute x51 -> x22, waiting for transfers between devices: 119 us -> 68.8 us  [swap(): return lax.ppermute(x, 'fsdp', [(i, i ^ mask) for i in range(RANKS)])]
    ppermute x51 -> x22, starting transfers between devices: 56.7 us -> 21.1 us  [swap(): return lax.ppermute(x, 'fsdp', [(i, i ^ mask) for i in range(RANKS)])]
    convert_element_type x21 -> x7, other arithmetic: 14.6 us -> 1.85 us  [the longest x1 0.86 us: body(): grad_w_down = jnp.concatenate([h0, h1], axis=1).astype(F32)]
    unnamed x57 -> x106, local copies, waits for them, and re-layouts: 1.07 us -> 13.1 us
    slice x13 -> x5, local copies, waits for them, and re-layouts: 7.97 us -> 0.94 us  [the longest x1 0.85 us: body(): w_first.reshape(ranks, -1, 3 * D + PAD)[:, :lines, 3 * D:]]
    ppermute x8 -> x7, waiting for transfers between devices: 18.6 us -> 16.8 us  [swap_replica(): return lax.ppermute(x, 'replica', [(0, 1), (1, 0)])]
  transfers between devices with their start and end apart: 62 -> 31, of which waited for: 26 -> 12; matrix products, arithmetic and copies ran while one was open for 8% -> 5% of each run, Pallas kernels for 50% -> 36%
where the time goes in v2:
time: 357 us; the launch traced here: 351 us
  Pallas kernels  190 us (53%)
  waiting for transfers between devices  85.7 us (24%)
  starting transfers between devices  30 us (8%)
  local copies, waits for them, and re-layouts  24.8 us (7%)
  between operations  14.9 us (4%)
  other arithmetic  6 us (2%)
    pallas_call x17, Pallas kernels, call(): pl.pallas_call(run, grid_spec=pltpu.PrefetchScalarGridSpec(num_scalar_pre...  190 us
    ppermute x22, waiting for transfers between devices, swap(): return lax.ppermute(x, 'fsdp', [(i, i ^ mask) for i in range(RANKS)])  68.8 us
    ppermute x22, starting transfers between devices, swap(): return lax.ppermute(x, 'fsdp', [(i, i ^ mask) for i in range(RANKS)])  21.1 us
    ppermute x7, waiting for transfers between devices, swap_replica(): return lax.ppermute(x, 'replica', [(0, 1), (1, 0)])  16.8 us
    unnamed x106, local copies, waits for them, and re-layouts  13.1 us
    ppermute x7, starting transfers between devices, swap_replica(): return lax.ppermute(x, 'replica', [(0, 1), (1, 0)])  8.81 us
  transfers between devices with their start and end apart: 31, of which 12 were waited for; matrix products, arithmetic and copies ran while one was open for 5% of the time, Pallas kernels for 36%

profile of v2, /device:TPU:20, one launch (start us, length us, event | category | flops | bytes accessed | tf_op | source)
XLA Modules:
  0.0 351.2 jit_solution(16542503986330251278)
XLA Ops:
  20.3 5.0 %collective-permute-done.1 = bf16[48,1280]{1,0:T(8,128)(2,1)S(1)} collective-permute-done((bf16[48,1280]{1,0:T(8,128)(2,1)S(1)}, bf16[48,1280]{1,0:T(8,128)(2,1)S(1)}, u32[]{:S(2)}, u32[]{:S(2)}) %collective-permute-start.1) | collective-permute-done | bytes 122912 | tf_op jit(solution)/shard_map/ppermute | solution.py:681
  25.3 14.3 %collective-permute-done.2 = bf16[48,1280]{1,0:T(8,128)(2,1)S(1)} collective-permute-done((bf16[48,1280]{1,0:T(8,128)(2,1)S(1)}, bf16[48,1280]{1,0:T(8,128)(2,1)S(1)}, u32[]{:S(2)}, u32[]{:S(2)}) %collective-permute-start.2) | collective-permute-done | bytes 122912 | tf_op jit(solution)/shard_map/ppermute | solution.py:681
  40.4 8.1 %collective-permute-done.3 = bf16[4,48,1280]{2,1,0:T(8,128)(2,1)S(1)} collective-permute-done((bf16[4,48,1280]{2,1,0:T(8,128)(2,1)S(1)}, bf16[4,48,1280]{2,1,0:T(8,128)(2,1)S(1)}, u32[]{:S(2)}, u32[]{:S(2)}) %collective-permute-start.3) | collective-permute-done | bytes 491552 | tf_op jit(solution)/shard_map/ppermute | solution.py:681
  50.2 14.9 %collective-permute-done.4.refs_2_ = bf16[2,4,48,1280]{3,2,1,0:T(8,128)(2,1)S(1)} collective-permute-done((bf16[2,4,48,1280]{3,2,1,0:T(8,128)(2,1)S(1)}, bf16[2,4,48,1280]{3,2,1,0:T(8,128)(2,1)S(1)}, u32[]{:S(2)}, u32[]{:S(2)}) %collective-permute-start.4) | collective-permute-done | bytes 983072 | tf_op jit(solution)/shard_map/ppermute | solution.py:685
  67.9 5.1 %shard_map.262.refs_2_.refs_3_.refs_4_ = bf16[768,2560]{1,0:T(8,128)(2,1)} custom-call(s32[2]{0:T(128)} %pad_add_fusion.refs_0_, bf16[2,4,48,1280]{3,2,1,0:T(8,128)(2,1)} %copy-done.1, bf16[2,4,48,1280]{3,2,1,0:T(8,128)(2,1)} %copy-done.29, bf16[2,4,48,1280]{3,2,1,0:T(8,128)(2,1)} %copy-done.30, bf16[2,4,48,1280]{3,2,1,0:T(8,128)(2,1)} %collective-permute-done.6.refs_4_), custom_call_target="tpu_custom_call" | custom-call | flops 4600000000 | bytes 14400000 | tf_op jit(solution)/shard_map/pallas_call | solution.py:56
  77.2 27.7 %shard_map.263 = (bf16[1024,768]{1,0:T(8,128)(2,1)}, bf16[1024,768]{1,0:T(8,128)(2,1)}, bf16[1024,768]{1,0:T(8,128)(2,1)}, bf16[6,2,4,384,256]{4,3,2,1,0:T(8,128)(2,1)}, bf16[1024,768]{1,0:T(8,128)(2,1)}) custom-call(s32[2,8]{1,0:T(2,128)} %refs_0_.5, bf16[1024,768]{1,0:T(8,128)(2,1)} %refs_2_.3, bf16[768,2560]{1,0:T(8,128)(2,1)} %shard_map.262.refs_2_.refs_3_.refs_4_, ...), custom_call_target="tpu_custom_call" | custom-call | flops 32199999488 | bytes 100800000 | tf_op jit(solution)/shard_map/pallas_call | solution.py:56
  104.9 19.8 %shard_map.264 = (f32[1024,768]{1,0:T(8,128)}, f32[1024,1]{1,0:T(8,128)}, bf16[1024,768]{1,0:T(8,128)(2,1)}, bf16[1024,3072]{1,0:T(8,128)(2,1)}, bf16[1024,3072]{1,0:T(8,128)(2,1)}) custom-call(bf16[1024,768]{1,0:T(8,128)(2,1)} %refs_2_.3, bf16[1024,768]{1,0:T(8,128)(2,1)} %get-tuple-element.79.refs_1_.refs_3_, f32[3,768]{1,0:T(4,128)} %pad_maximum_fusion.2.refs_2_, ...), custom_call_target="tpu_custom_call" | custom-call | flops 20700000256 | bytes 64800000 | tf_op jit(solution)/shard_map/pallas_call | solution.py:56
  124.8 15.0 %shard_map.265 = (bf16[1024,768]{1,0:T(8,128)(2,1)}, f32[1024,768]{1,0:T(8,128)}, bf16[1024,768]{1,0:T(8,128)(2,1)}, f32[3,768]{1,0:T(4,128)}, f32[2,8,768]{2,1,0:T(8,128)}) custom-call(s32[2,8]{1,0:T(2,128)} %refs_0_.5, bf16[1024,3072]{1,0:T(8,128)(2,1)} %get-tuple-element.80.refs_1_, f32[1024,768]{1,0:T(8,128)} %get-tuple-element.81.refs_2_, ...), custom_call_target="tpu_custom_call" | custom-call | flops 16099999744 | bytes 50400000 | tf_op jit(solution)/shard_map/pallas_call | solution.py:56
  139.8 10.8 %shard_map.266 = (bf16[2,2,4,192,384]{4,3,2,1,0:T(8,128)(2,1)}, bf16[2,2,4,192,384]{4,3,2,1,0:T(8,128)(2,1)}) custom-call(s32[2]{0:T(128)} %pad_add_fusion.refs_0_, bf16[1024,3072]{1,0:T(8,128)(2,1)} %get-tuple-element.80.refs_1_, bf16[1024,768]{1,0:T(8,128)(2,1)} %get-tuple-element.83.refs_2_.refs_0_), custom_call_target="tpu_custom_call" | custom-call | flops 11500000256 | bytes 36000000 | tf_op jit(solution)/shard_map/pallas_call | solution.py:56
  151.5 12.2 %shard_map.267 = (bf16[1024,3072]{1,0:T(8,128)(2,1)}, f32[1,3072]{1,0:T(1,128)}) custom-call(bf16[1024,768]{1,0:T(8,128)(2,1)} %get-tuple-element.83.refs_2_.refs_0_, bf16[1024,3072]{1,0:T(8,128)(2,1)} %get-tuple-element.84.refs_1_, bf16[16,432,768]{2,1,0:T(8,128)(2,1)} %bitcast.49, bf16[2,2,4,192,384]{4,3,2,1,0:T(8,128)(2,1)} %get-tuple-element.85.refs_3_), custom_call_target="tpu_custom_call" | custom-call | flops 12650000384 | bytes 39600000 | tf_op jit(solution)/shard_map/pallas_call | solution.py:56
  165.1 4.1 %shard_map.268 = (bf16[1536,384]{1,0:T(8,128)(2,1)}, bf16[1600,384]{1,0:T(8,128)(2,1)}, bf16[64,384]{1,0:T(8,128)(2,1)}) custom-call(bf16[3072,384]{1,0:T(8,128)(2,1)} %bitcast.72, bf16[3072,384]{1,0:T(8,128)(2,1)} %copy-done.26, bf16[32,384]{1,0:T(8,128)(2,1)} %copy-done.45, bf16[32,384]{1,0:T(8,128)(2,1)} %copy-done.11, f32[1,3072]{1,0:T(1,128)} %get-tuple-element.92.refs_4_), custom_call_target="tpu_custom_call" | custom-call | flops 2300000000 | bytes 7200000 | tf_op jit(solution)/shard_map/pallas_call | solution.py:56
  169.2 9.2 %shard_map.269.refs_6_ = bf16[768,3072]{1,0:T(8,128)(2,1)} custom-call(bf16[1024,768]{1,0:T(8,128)(2,1)} %get-tuple-element.89.refs_0_, bf16[1024,3072]{1,0:T(8,128)(2,1)} %get-tuple-element.86.refs_1_.refs_0_, bf16[1600,384]{1,0:T(8,128)(2,1)} %get-tuple-element.93.refs_2_.refs_9_), custom_call_target="tpu_custom_call" | custom-call | flops 10350000128 | bytes 32400000 | tf_op jit(solution)/shard_map/pallas_call | solution.py:56
  181.5 14.4 %shard_map.270 = (f32[1024,768]{1,0:T(8,128)}, bf16[1024,768]{1,0:T(8,128)(2,1)}, f32[3,768]{1,0:T(4,128)}) custom-call(bf16[1024,3072]{1,0:T(8,128)(2,1)} %get-tuple-element.86.refs_1_.refs_0_, f32[1024,768]{1,0:T(8,128)} %get-tuple-element.87.refs_1_, f32[1024,768]{1,0:T(8,128)} %get-tuple-element.81.refs_2_, f32[1024,1]{1,0:T(8,128)} %get-tuple-element.88.refs_3_, ...), custom_call_target="tpu_custom_call" | custom-call | flops 1150000000 | bytes 3600000 | tf_op jit(solution)/shard_map/pallas_call | solution.py:56
  195.9 30.7 %shard_map.271 = (bf16[1024,1536]{1,0:T(8,128)(2,1)}, f32[2,512]{1,0:T(2,128)}, bf16[2,2,4,48,1152]{4,3,2,1,0:T(8,128)(2,1)}, bf16[2,2,4,48,1152]{4,3,2,1,0:T(8,128)(2,1)}) custom-call(s32[2]{0:T(128)} %pad_add_fusion.refs_0_, bf16[1024,768]{1,0:T(8,128)(2,1)} %get-tuple-element.95.refs_1_, bf16[1024,768]{1,0:T(8,128)(2,1)} %refs_2_.3, ...), custom_call_target="tpu_custom_call" | custom-call | flops 1150000000 | bytes 3600000 | tf_op jit(solution)/shard_map/pallas_call | solution.py:56
  227.7 3.0 shard_map.272
  231.8 15.9 %shard_map.273 = (bf16[1024,768]{1,0:T(8,128)(2,1)}, f32[2,256]{1,0:T(2,128)}, bf16[2,4,48,768]{3,2,1,0:T(8,128)(2,1)}, bf16[2,4,48,768]{3,2,1,0:T(8,128)(2,1)}) custom-call(s32[2]{0:T(128)} %pad_add_fusion.refs_0_, bf16[1024,768]{1,0:T(8,128)(2,1)} %get-tuple-element.95.refs_1_, bf16[1024,768]{1,0:T(8,128)(2,1)} %refs_2_.3, ...), custom_call_target="tpu_custom_call" | custom-call | flops 1150000000 | bytes 3600000 | tf_op jit(solution)/shard_map/pallas_call | solution.py:56
  252.7 4.1 %shard_map.274 = (bf16[384,384]{1,0:T(8,128)(2,1)}, bf16[640,384]{1,0:T(8,128)(2,1)}, bf16[256,384]{1,0:T(8,128)(2,1)}, bf16[384,1152]{1,0:T(8,128)(2,1)}, bf16[384,1152]{1,0:T(8,128)(2,1)}) custom-call(bf16[768,384]{1,0:T(8,128)(2,1)} %get-tuple-element.106.refs_0_, bf16[896,384]{1,0:T(8,128)(2,1)} %copy-done.32, ...), custom_call_target="tpu_custom_call" | custom-call | flops 2300000000 | bytes 7200000 | tf_op jit(solution)/shard_map/pallas_call | solution.py:56
  258.5 9.0 %shard_map.275.refs_9_ = f32[1024,768]{1,0:T(8,128)} custom-call(f32[1024,768]{1,0:T(8,128)} %get-tuple-element.94.refs_0_, bf16[1024,1536]{1,0:T(8,128)(2,1)} %get-tuple-element.100.refs_1_, bf16[1024,768]{1,0:T(8,128)(2,1)} %get-tuple-element.105.refs_2_, bf16[768,2560]{1,0:T(8,128)(2,1)} %shard_map.262.refs_2_.refs_3_.refs_4_, ...), custom_call_target="tpu_custom_call" | custom-call | flops 10350000128 | bytes 32400000 | tf_op jit(solution)/shard_map/pallas_call | solution.py:56
  267.5 11.9 %collective-permute-done.12.refs_1_ = bf16[640,384]{1,0:T(8,128)(2,1)S(1)} collective-permute-done((bf16[640,384]{1,0:T(8,128)(2,1)}, bf16[640,384]{1,0:T(8,128)(2,1)S(1)}, u32[]{:S(2)}, u32[]{:S(2)}) %collective-permute-start.12) | collective-permute-done | bytes 491552 | tf_op jit(solution)/shard_map/ppermute | solution.py:681
  280.6 3.7 %shard_map.276 = (bf16[192,384]{1,0:T(8,128)(2,1)}, bf16[704,384]{1,0:T(8,128)(2,1)}, bf16[512,384]{1,0:T(8,128)(2,1)}, bf16[192,1152]{1,0:T(8,128)(2,1)}, bf16[...) custom-call(bf16[384,384]{1,0:T(8,128)(2,1)} %get-tuple-element.112.refs_0_, ...), custom_call_target="tpu_custom_call" | custom-call | flops 2300000000 | bytes 7200000 | tf_op jit(solution)/shard_map/pallas_call | solution.py:56
  290.3 13.8 %collective-permute-done.18.refs_6_ = bf16[208,768]{1,0:T(8,128)(2,1)S(1)} collective-permute-done((bf16[208,768]{1,0:T(8,128)(2,1)}, bf16[208,768]{1,0:T(8,128)(2,1)S(1)}, u32[]{:S(2)}, u32[]{:S(2)}) %collective-permute-start.18) | collective-permute-done | bytes 319520 | tf_op jit(solution)/shard_map/ppermute | solution.py:681
  305.1 2.9 shard_map.277
  313.9 3.8 %collective-permute-start.23 = (bf16[64,768]{1,0:T(8,128)(2,1)}, bf16[64,768]{1,0:T(8,128)(2,1)S(1)}, u32[]{:S(2)}, u32[]{:S(2)}) collective-permute-start(bf16[64,768]{1,0:T(8,128)(2,1)} %get-tuple-element.135), channel_id=1, source_target_pairs={{0,8},{1,9},{2,10},{3,11},{4,12},{5,13},{6,14},{7,15},{8,0},{9,1},... | collective-permute-start | bytes 294920 | tf_op jit(solution)/shard_map/ppermute | solution.py:681
  321.9 7.6 %collective-permute-done.23.refs_6_ = bf16[64,768]{1,0:T(8,128)(2,1)S(1)} collective-permute-done((bf16[64,768]{1,0:T(8,128)(2,1)}, bf16[64,768]{1,0:T(8,128)(2,1)S(1)}, u32[]{:S(2)}, u32[]{:S(2)}) %collective-permute-start.23) | collective-permute-done | bytes 98336 | tf_op jit(solution)/shard_map/ppermute | solution.py:681
  (232 shorter events, 69.2 us)
Async XLA Ops:
  7.3 97.6 %all-gather.2.cloned.1.call-start = ((), (), s32[]{:S(2)}) async-start(), calls=%async_computation.1 | async-start | bytes 11280384 | tf_op jit(solution)/shard_map/all_gather | solution.py:864
  13.7 244.8 %reduce-scatter.2.cloned.1.call-start = ((), (), s32[]{:S(2)}) async-start(), calls=%async_computation.2 | async-start | bytes 5013504 | tf_op jit(solution)/shard_map/reduce_scatter | solution.py:913
  16.0 23.6 %collective-permute-start.2 = (bf16[48,1280]{1,0:T(8,128)(2,1)S(1)}, bf16[48,1280]{1,0:T(8,128)(2,1)S(1)}, u32[]{:S(2)}, u32[]{:S(2)}) collective-permute-start(bf16[48,1280]{1,0:T(8,128)(2,1)S(1)} %fusion.1), channel_id=1, source_target_pairs={{0,12},{1,13},{2,14},{3,15},{4,8},{5,9},{6,10},{7,11},{8,4},{9,5},... | collective-permute-start | bytes 368648 | tf_op jit(solution)/shard_map/ppermute | solution.py:681
  48.7 16.5 %collective-permute-start.4 = (bf16[2,4,48,1280]{3,2,1,0:T(8,128)(2,1)S(1)}, bf16[2,4,48,1280]{3,2,1,0:T(8,128)(2,1)S(1)}, u32[]{:S(2)}, u32[]{:S(2)}) collective-permute-start(bf16[2,4,48,1280]{3,2,1,0:T(8,128)(2,1)S(1)} %pad_maximum_fusion.refs_1_), channel_id=1, source_target_pairs={{0,16},{16,0},{1,17},{17,1},{2,18},{18,2},{3,19},{19,3},{4,20},{20... | collective-permute-start | bytes 2949128 | tf_op jit(solution)/shard_map/ppermute | solution.py:685
  50.2 15.6 %collective-permute-start.5 = (bf16[2,4,48,1280]{3,2,1,0:T(8,128)(2,1)S(1)}, bf16[2,4,48,1280]{3,2,1,0:T(8,128)(2,1)S(1)}, u32[]{:S(2)}, u32[]{:S(2)}) collective-permute-start(bf16[2,4,48,1280]{3,2,1,0:T(8,128)(2,1)S(1)} %pad_maximum_fusion.refs_1_), channel_id=1, source_target_pairs={{0,1},{1,0},{2,3},{3,2},{4,5},{5,4},{6,7},{7,6},{8,9},{9,8},{10,11... | collective-permute-start | bytes 2949128 | tf_op jit(solution)/shard_map/ppermute | solution.py:681
  150.7 13.0 %collective-permute-start.7 = (bf16[3072,384]{1,0:T(8,128)(2,1)}, bf16[3072,384]{1,0:T(8,128)(2,1)S(1)}, u32[]{:S(2)}, u32[]{:S(2)}) collective-permute-start(bf16[3072,384]{1,0:T(8,128)(2,1)} %bitcast.67), channel_id=1, source_target_pairs={{0,1},{1,0},{2,3},{3,2},{4,5},{5,4},{6,7},{7,6},{8,9},{9,8},{10,11... | collective-permute-start | bytes 7077896 | tf_op jit(solution)/shard_map/ppermute | solution.py:681
  151.0 12.6 %collective-permute-start.8 = (bf16[32,384]{1,0:T(8,128)(2,1)S(1)}, bf16[32,384]{1,0:T(8,128)(2,1)S(1)}, u32[]{:S(2)}, u32[]{:S(2)}) collective-permute-start(bf16[32,384]{1,0:T(8,128)(2,1)S(1)} %reshape.235.refs_3_), channel_id=1, source_target_pairs={{0,1},{1,0},{2,3},{3,2},{4,5},{5,4},{6,7},{7,6},{8,9},{9,8},{10,11... | collective-permute-start | bytes 73736 | tf_op jit(solution)/shard_map/ppermute | solution.py:681
  179.7 46.9 %collective-permute-start.9 = (bf16[1600,384]{1,0:T(8,128)(2,1)S(1)}, bf16[1600,384]{1,0:T(8,128)(2,1)S(1)}, u32[]{:S(2)}, u32[]{:S(2)}) collective-permute-start(bf16[1600,384]{1,0:T(8,128)(2,1)S(1)} %copy-done), channel_id=1, source_target_pairs={{0,16},{16,0},{1,17},{17,1},{2,18},{18,2},{3,19},{19,3},{4,20},{20... | collective-permute-start | bytes 3686408 | tf_op jit(solution)/shard_map/ppermute | solution.py:685
  226.6 22.5 %collective-permute-start.11 = (bf16[768,1152]{1,0:T(8,128)(2,1)}, bf16[768,1152]{1,0:T(8,128)(2,1)S(1)}, u32[]{:S(2)}, u32[]{:S(2)}) collective-permute-start(bf16[768,1152]{1,0:T(8,128)(2,1)} %bitcast.69), channel_id=1, source_target_pairs={{0,1},{1,0},{2,3},{3,2},{4,5},{5,4},{6,7},{7,6},{8,9},{9,8},{10,11... | collective-permute-start | bytes 5308424 | tf_op jit(solution)/shard_map/ppermute | solution.py:681
  230.7 21.2 %collective-permute-start.10 = (bf16[896,384]{1,0:T(8,128)(2,1)}, bf16[896,384]{1,0:T(8,128)(2,1)S(1)}, u32[]{:S(2)}, u32[]{:S(2)}) collective-permute-start(bf16[896,384]{1,0:T(8,128)(2,1)} %get-tuple-element.104.refs_9_), channel_id=1, source_target_pairs={{0,2},{1,3},{2,0},{3,1},{4,6},{5,7},{6,4},{7,5},{8,10},{9,11},{10,... | collective-permute-start | bytes 2064392 | tf_op jit(solution)/shard_map/ppermute | solution.py:681
  248.5 19.0 %collective-permute-start.15 = (bf16[16,768]{1,0:T(8,128)(2,1)S(1)}, bf16[16,768]{1,0:T(8,128)(2,1)S(1)}, u32[]{:S(2)}, u32[]{:S(2)}) collective-permute-start(bf16[16,768]{1,0:T(8,128)(2,1)S(1)} %fusion.10.refs_8_), channel_id=1, source_target_pairs={{0,1},{1,0},{2,3},{3,2},{4,5},{5,4},{6,7},{7,6},{8,9},{9,8},{10,11... | collective-permute-start | bytes 73736 | tf_op jit(solution)/shard_map/ppermute | solution.py:681
  248.7 18.8 %collective-permute-start.14 = (bf16[384,768]{1,0:T(8,128)(2,1)}, bf16[384,768]{1,0:T(8,128)(2,1)}, u32[]{:S(2)}, u32[]{:S(2)}) collective-permute-start(bf16[384,768]{1,0:T(8,128)(2,1)} %bitcast.71), channel_id=1, source_target_pairs={{0,1},{1,0},{2,3},{3,2},{4,5},{5,4},{6,7},{7,6},{8,9},{9,8},{10,11... | collective-permute-start | bytes 1769480 | tf_op jit(solution)/shard_map/ppermute | solution.py:681
  256.8 22.6 %collective-permute-start.13 = (bf16[384,1152]{1,0:T(8,128)(2,1)}, bf16[384,1152]{1,0:T(8,128)(2,1)S(1)}, u32[]{:S(2)}, u32[]{:S(2)}) collective-permute-start(bf16[384,1152]{1,0:T(8,128)(2,1)} %get-tuple-element.111.refs_4_), channel_id=1, source_target_pairs={{0,16},{16,0},{1,17},{17,1},{2,18},{18,2},{3,19},{19,3},{4,20},{20... | collective-permute-start | bytes 2654216 | tf_op jit(solution)/shard_map/ppermute | solution.py:685
  257.2 22.3 %collective-permute-start.12 = (bf16[640,384]{1,0:T(8,128)(2,1)}, bf16[640,384]{1,0:T(8,128)(2,1)S(1)}, u32[]{:S(2)}, u32[]{:S(2)}) collective-permute-start(bf16[640,384]{1,0:T(8,128)(2,1)} %get-tuple-element.113), channel_id=1, source_target_pairs={{0,8},{1,9},{2,10},{3,11},{4,12},{5,13},{6,14},{7,15},{8,0},{9,1},... | collective-permute-start | bytes 1474568 | tf_op jit(solution)/shard_map/ppermute | solution.py:681
  284.3 19.8 %collective-permute-start.16 = (bf16[704,384]{1,0:T(8,128)(2,1)}, bf16[704,384]{1,0:T(8,128)(2,1)S(1)}, u32[]{:S(2)}, u32[]{:S(2)}) collective-permute-start(bf16[704,384]{1,0:T(8,128)(2,1)} %get-tuple-element.121), channel_id=1, source_target_pairs={{0,4},{1,5},{2,6},{3,7},{4,0},{5,1},{6,2},{7,3},{8,12},{9,13},{10,... | collective-permute-start | bytes 1622024 | tf_op jit(solution)/shard_map/ppermute | solution.py:681
  286.5 17.5 %collective-permute-start.17 = (bf16[192,1152]{1,0:T(8,128)(2,1)}, bf16[192,1152]{1,0:T(8,128)(2,1)S(1)}, u32[]{:S(2)}, u32[]{:S(2)}) collective-permute-start(bf16[192,1152]{1,0:T(8,128)(2,1)} %get-tuple-element.124), channel_id=1, source_target_pairs={{0,2},{1,3},{2,0},{3,1},{4,6},{5,7},{6,4},{7,5},{8,10},{9,11},{10,... | collective-permute-start | bytes 1327112 | tf_op jit(solution)/shard_map/ppermute | solution.py:681
  288.0 16.0 %collective-permute-start.18 = (bf16[208,768]{1,0:T(8,128)(2,1)}, bf16[208,768]{1,0:T(8,128)(2,1)S(1)}, u32[]{:S(2)}, u32[]{:S(2)}) collective-permute-start(bf16[208,768]{1,0:T(8,128)(2,1)} %get-tuple-element.126), channel_id=1, source_target_pairs={{0,2},{1,3},{2,0},{3,1},{4,6},{5,7},{6,4},{7,5},{8,10},{9,11},{10,... | collective-permute-start | bytes 958472 | tf_op jit(solution)/shard_map/ppermute | solution.py:681
  288.6 20.6 %collective-permute-start.27 = (bf16[48,3072]{1,0:T(8,128)(2,1)S(1)}, bf16[48,3072]{1,0:T(8,128)(2,1)S(1)}, u32[]{:S(2)}, u32[]{:S(2)}) collective-permute-start(bf16[48,3072]{1,0:T(8,128)(2,1)S(1)} %copy-done.3), channel_id=1, source_target_pairs={{0,16},{16,0},{1,17},{17,1},{2,18},{18,2},{3,19},{19,3},{4,20},{20... | collective-permute-start | bytes 884744 | tf_op jit(solution)/shard_map/ppermute | solution.py:685
  308.0 12.3 %collective-permute-start.22 = (bf16[64,768]{1,0:T(8,128)(2,1)}, bf16[64,768]{1,0:T(8,128)(2,1)S(1)}, u32[]{:S(2)}, u32[]{:S(2)}) collective-permute-start(bf16[64,768]{1,0:T(8,128)(2,1)} %get-tuple-element.134), channel_id=1, source_target_pairs={{0,4},{1,5},{2,6},{3,7},{4,0},{5,1},{6,2},{7,3},{8,12},{9,13},{10,... | collective-permute-start | bytes 294920 | tf_op jit(solution)/shard_map/ppermute | solution.py:681
  310.0 21.5 %collective-permute-start.19 = (bf16[48,1152]{1,0:T(8,128)(2,1)}, bf16[48,1152]{1,0:T(8,128)(2,1)S(1)}, u32[]{:S(2)}, u32[]{:S(2)}) collective-permute-start(bf16[48,1152]{1,0:T(8,128)(2,1)} %get-tuple-element.130), channel_id=1, source_target_pairs={{0,4},{1,5},{2,6},{3,7},{4,0},{5,1},{6,2},{7,3},{8,12},{9,13},{10,... | collective-permute-start | bytes 331784 | tf_op jit(solution)/shard_map/ppermute | solution.py:681
  310.9 20.6 %collective-permute-start.20 = (bf16[48,1152]{1,0:T(8,128)(2,1)}, bf16[48,1152]{1,0:T(8,128)(2,1)S(1)}, u32[]{:S(2)}, u32[]{:S(2)}) collective-permute-start(bf16[48,1152]{1,0:T(8,128)(2,1)} %get-tuple-element.131), channel_id=1, source_target_pairs={{0,8},{1,9},{2,10},{3,11},{4,12},{5,13},{6,14},{7,15},{8,0},{9,1},... | collective-permute-start | bytes 331784 | tf_op jit(solution)/shard_map/ppermute | solution.py:681
  313.6 17.9 %collective-permute-start.21 = (bf16[48,1152]{1,0:T(8,128)(2,1)}, bf16[48,1152]{1,0:T(8,128)(2,1)S(1)}, u32[]{:S(2)}, u32[]{:S(2)}) collective-permute-start(bf16[48,1152]{1,0:T(8,128)(2,1)} %get-tuple-element.132), channel_id=1, source_target_pairs={{0,12},{1,13},{2,14},{3,15},{4,8},{5,9},{6,10},{7,11},{8,4},{9,5},... | collective-permute-start | bytes 331784 | tf_op jit(solution)/shard_map/ppermute | solution.py:681
  313.9 15.7 %collective-permute-start.23 = (bf16[64,768]{1,0:T(8,128)(2,1)}, bf16[64,768]{1,0:T(8,128)(2,1)S(1)}, u32[]{:S(2)}, u32[]{:S(2)}) collective-permute-start(bf16[64,768]{1,0:T(8,128)(2,1)} %get-tuple-element.135), channel_id=1, source_target_pairs={{0,8},{1,9},{2,10},{3,11},{4,12},{5,13},{6,14},{7,15},{8,0},{9,1},... | collective-permute-start | bytes 294920 | tf_op jit(solution)/shard_map/ppermute | solution.py:681
  320.4 11.1 %collective-permute-start.24 = (bf16[64,768]{1,0:T(8,128)(2,1)S(1)}, bf16[64,768]{1,0:T(8,128)(2,1)S(1)}, u32[]{:S(2)}, u32[]{:S(2)}) collective-permute-start(bf16[64,768]{1,0:T(8,128)(2,1)S(1)} %copy-done.41), channel_id=1, source_target_pairs={{0,12},{1,13},{2,14},{3,15},{4,8},{5,9},{6,10},{7,11},{8,4},{9,5},... | collective-permute-start | bytes 294920 | tf_op jit(solution)/shard_map/ppermute | solution.py:681
  (53 other events, 288.5 us)
Sparse Core Ops, SparseCore 0:
  13.8 90.9 all-gather.1
  178.6 76.4 reduce-scatter.1

commit v3 on v2

--- a/solution.py
+++ b/solution.py
@@ -46,7 +46,9 @@
     return max(0, (qb - 1) * BLOCK), min(SEQ, (qb + 2) * BLOCK)
 
 
-def call(kernel, grid, in_specs, out_specs, out_shape, us, scratch=(), prefetch=0, after=()):
+def call(
+    kernel, grid, in_specs, out_specs, out_shape, us, scratch=(), prefetch=0, after=(), aliases=None
+):
     first = prefetch + len(in_specs)
 
     def run(*refs):
@@ -63,6 +65,7 @@
                 scratch_shapes=list(scratch),
             ),
             out_shape=out_shape,
+            input_output_aliases=aliases or {},
             compiler_params=pltpu.CompilerParams(vmem_limit_bytes=VMEM_LIMIT),
             cost_estimate=pl.CostEstimate(
                 flops=int(us * 1.15e9), bytes_accessed=int(us * 3.6e6), transcendentals=0
@@ -83,9 +86,44 @@
 ANY = pl.BlockSpec(memory_space=pl.ANY)
 
 
-def pack_weights(w_out, w_up, w_down):
-    blocks = [w_up[:, i * D : (i + 1) * D] for i in range(FF // D)]
-    return jnp.concatenate([w_out] + blocks + [w_down], axis=0)
+def pack_weights(where, w_qkv, small, w_out, w_up, w_down):
+    r, f = w_out.shape[0], w_down.shape[0]
+    columns = w_qkv.shape[1]
+    half = (columns + PAD) // 2
+    count = len(small)
+
+    def kernel(where_ref, q_ref, wo_ref, wu_ref, wd_ref, *refs):
+        s_refs, (out_ref, own_ref) = refs[:count], refs[count:]
+        out_ref[:r, :] = wo_ref[...]
+        for i in range(FF // D):
+            out_ref[(1 + i) * r : (2 + i) * r, :] = wu_ref[:, i * D : (i + 1) * D]
+        out_ref[5 * r :, :] = wd_ref[...]
+
+        @pl.when(where_ref[1] == 0)
+        def _():
+            own_ref[...] = q_ref[:, :half]
+
+        @pl.when(where_ref[1] > 0)
+        def _():
+            own_ref[:, : columns - half] = q_ref[:, half:]
+            rows = []
+            for s_ref in s_refs:
+                v = s_ref[...].astype(F32)
+                rows.append(jnp.concatenate([v, jnp.zeros((1, PAD - v.shape[1]), F32)], axis=1))
+            rows.append(jnp.zeros((r - count, PAD), F32))
+            own_ref[:, columns - half :] = jnp.concatenate(rows, axis=0).astype(BF)
+
+    operands = (w_qkv, w_out, w_up, w_down) + tuple(v[None] for v in small)
+    shapes = [shaped((5 * r + f, D), BF), shaped((r, half), BF)]
+    return call(
+        kernel,
+        (1,),
+        [whole(x.shape) for x in operands],
+        [whole(x.shape) for x in shapes],
+        shapes,
+        us=2,
+        prefetch=1,
+    )(where, *operands)
 
 
 def weight_copies(name, refs, target, sems):
@@ -206,7 +244,7 @@
     g = pl.program_id(0)
     row = pl.program_id(1)
     first = groups[0]
-    with_out = first == 0
+    with_out = 0
     last = pl.num_programs(1) - 1
     span = 3 * GW
 
@@ -326,7 +364,7 @@
     t = datt.shape[0]
     rows = t // SEQ
     count, first = len(groups), groups[0]
-    extra = int(first == 0)
+    extra = 0
     group = lambda g: jnp.maximum(g - extra, 0) + first
     row_spec = pl.BlockSpec((SEQ, GW), lambda g, r, *_: (r, group(g)))
     full_row = pl.BlockSpec((SEQ, D), lambda g, r, *_: (r, 0))
@@ -406,185 +444,118 @@
     ref[...] = jnp.where(pl.program_id(0) == 0, stacked, ref[...] + stacked)
 
 
-def up(tokens, mixed, weights, vec, bias_up, after=()):
+def middle(lengths, tokens, mixed, weights, vec, bias_up, cot, after=()):
     t = tokens.shape[0]
     nw = len(weights)
-
-    def kernel(tok_ref, m_ref, vec_ref, bu_ref, *refs):
+    per_row = SEQ // TB
+
+    def kernel(lengths_ref, tok_ref, m_ref, vec_ref, bu_ref, cot_ref, *refs):
         wrefs, refs = refs[:nw], refs[nw:]
-        xhat_ref, inv_ref, nl_ref, act_ref, gp_ref, wo, wu, so, su = refs
+        out_ref, nl_ref, act_ref, dd_ref, du_ref, df_ref, da_ref, sums_ref, su_ref, pool_ref = refs[:10]
+        wo, wu, wd, gp, so, su, sd = refs[10:]
+        i = pl.program_id(0)
         out_copies = weight_copies("out", wrefs, wo, so)
         up_copies = weight_copies("up", wrefs, wu, su)
-
-        @pl.when(pl.program_id(0) == 0)
+        down_copies = weight_copies("down", wrefs, wd, sd)
+
+        @pl.when(i == 0)
         def _():
             start_all(out_copies)
             start_all(up_copies)
+            start_all(down_copies)
             wait_all(out_copies)
 
         att = dot(m_ref[...], wo[...]) + vec_ref[0:1, :]
         xhat, inverse = normalize(tok_ref[...].astype(F32) + att)
-        xhat_ref[...] = xhat
-        inv_ref[...] = inverse
-        nl_ref[...] = (xhat * vec_ref[1:2, :] + vec_ref[2:3, :]).astype(BF)
-
-        @pl.when(pl.program_id(0) == 0)
+        normed = xhat * vec_ref[1:2, :] + vec_ref[2:3, :]
+        nl = normed.astype(BF)
+        nl_ref[...] = nl
+
+        @pl.when(i == 0)
         def _():
             wait_all(up_copies)
 
-        nl = nl_ref[...]
         for c in range(0, FF, CH):
             u = dot(nl, wu[:, c : c + CH]) + bu_ref[:, c : c + CH]
             cdf = 0.5 * (1.0 + lax.erf(u * root_half))
             act_ref[:, c : c + CH] = (u * cdf).astype(BF)
-            gp_ref[:, c : c + CH] = (cdf + u * (jnp.exp(u * u * -0.5) * pdf_scale)).astype(BF)
-
-    tok = lambda n: pl.BlockSpec((TB, n), lambda i: (i, 0))
-    return call(
-        kernel,
-        (t // TB,),
-        [tok(D), tok(D), whole((3, D)), whole((1, FF))] + [ANY] * nw,
-        [tok(D), tok(1), tok(D), tok(FF), tok(FF)],
-        [shaped((t, D), F32), shaped((t, 1), F32), shaped((t, D), BF), shaped((t, FF), BF), shaped((t, FF), BF)],
-        us=18,
-        scratch=[
-            pltpu.VMEM((D, D), BF),
-            pltpu.VMEM((D, FF), BF),
-            pltpu.SemaphoreType.DMA((16,)),
-            pltpu.SemaphoreType.DMA((64,)),
-        ],
-        after=after,
-    )(tokens, mixed, vec, bias_up, *weights)
-
-
-def down(lengths, active, xhat, weights, vec, cot, after=()):
-    t = cot.shape[0]
-    nw = len(weights)
-    per_row = SEQ // TB
-
-    def kernel(lengths_ref, act_ref, xhat_ref, vec_ref, cot_ref, *refs):
-        wrefs, refs = refs[:nw], refs[nw:]
-        out_ref, ds_ref, dd_ref, sums_ref, pool_ref, wd, sems = refs
-        i = pl.program_id(0)
+            gp[:, c : c + CH] = cdf + u * (jnp.exp(u * u * -0.5) * pdf_scale)
 
         @pl.when(i == 0)
         def _():
-            copies = weight_copies("down", wrefs, wd, sems)
-            start_all(copies)
-            wait_all(copies)
-
-        normed = xhat_ref[...] * vec_ref[0:1, :] + vec_ref[1:2, :]
-        second = normed + (dot(act_ref[...], wd[...]) + vec_ref[2:3, :])
-        xhat, inverse = normalize(second)
-        out = (xhat * vec_ref[3:4, :] + vec_ref[4:5, :]).astype(BF)
+            wait_all(down_copies)
+
+        second = normed + (dot(act_ref[...], wd[...]) + vec_ref[3:4, :])
+        xhat_two, inverse_two = normalize(second)
+        out = (xhat_two * vec_ref[4:5, :] + vec_ref[5:6, :]).astype(BF)
         out_ref[...] = out
         cot = cot_ref[...].astype(F32)
-        d_second = normalize_back(cot * vec_ref[3:4, :], xhat, inverse)
-        ds_ref[...] = d_second
-        d_down = d_second.astype(BF)
-        dd_ref[...] = d_down
-        add_rows(sums_ref, (d_down.astype(F32), cot * xhat, cot))
+        d_second = normalize_back(cot * vec_ref[4:5, :], xhat_two, inverse_two)
+        dd = d_second.astype(BF)
+        dd_ref[...] = dd
         row = i // per_row
         places = lax.broadcasted_iota(jnp.int32, (1, TB), 1) + (i % per_row) * TB
         segment = segment_of(places, lengths_ref, row)
         ids = lax.broadcasted_iota(jnp.int32, (SEGS, TB), 0)
-        sums = dot(jnp.where(segment == ids, 1.0, 0.0).astype(BF), out)
-        pool_ref[0] = jnp.where(i % per_row == 0, sums, pool_ref[0] + sums)
+        pooled = dot(jnp.where(segment == ids, 1.0, 0.0).astype(BF), out)
+        pool_ref[0] = jnp.where(i % per_row == 0, pooled, pool_ref[0] + pooled)
+        for c in range(0, FF, CH):
+            du = (dot_t(dd, wd[c : c + CH, :]) * gp[:, c : c + CH]).astype(BF)
+            du_ref[:, c : c + CH] = du
+            partial = jnp.sum(du.astype(F32), axis=0, keepdims=True)
+            su_ref[:, c : c + CH] = jnp.where(i == 0, partial, su_ref[:, c : c + CH] + partial)
+        d_normed = d_second + dot_t(du_ref[...], wu[...])
+        d_first = normalize_back(d_normed * vec_ref[1:2, :], xhat, inverse)
+        df_ref[...] = d_first
+        d_att = d_first.astype(BF)
+        da_ref[...] = d_att
+        add_rows(
+            sums_ref,
+            (dd.astype(F32), cot * xhat_two, cot, d_att.astype(F32), d_normed * xhat, d_normed),
+        )
 
     tok = lambda n: pl.BlockSpec((TB, n), lambda i, *_: (i, 0))
     return call(
         kernel,
         (t // TB,),
-        [tok(FF), tok(D), whole((5, D)), tok(D)] + [ANY] * nw,
+        [tok(D), tok(D), whole((6, D)), whole((1, FF)), tok(D)] + [ANY] * nw,
         [
             tok(D),
             tok(D),
+            tok(FF),
             tok(D),
-            pl.BlockSpec((3, D), lambda i, *_: (0, 0)),
+            tok(FF),
+            tok(D),
+            tok(D),
+            pl.BlockSpec((6, D), lambda i, *_: (0, 0)),
+            pl.BlockSpec((1, FF), lambda i, *_: (0, 0)),
             pl.BlockSpec((1, SEGS, D), lambda i, *_: (i // per_row, 0, 0)),
         ],
         [
             shaped((t, D), BF),
+            shaped((t, D), BF),
+            shaped((t, FF), BF),
+            shaped((t, D), BF),
+            shaped((t, FF), BF),
             shaped((t, D), F32),
             shaped((t, D), BF),
-            shaped((3, D), F32),
+            shaped((6, D), F32),
+            shaped((1, FF), F32),
             shaped((t // SEQ, SEGS, D), F32),
         ],
-        us=14,
-        scratch=[pltpu.VMEM((FF, D), BF), pltpu.SemaphoreType.DMA((16,))],
+        us=45,
+        scratch=[
+            pltpu.VMEM((D, D), BF),
+            pltpu.VMEM((D, FF), BF),
+            pltpu.VMEM((FF, D), BF),
+            pltpu.VMEM((TB, FF), F32),
+            pltpu.SemaphoreType.DMA((16,)),
+            pltpu.SemaphoreType.DMA((64,)),
+            pltpu.SemaphoreType.DMA((16,)),
+        ],
         prefetch=1,
         after=after,
-    )(lengths, active, xhat, vec, cot, *weights)
-
-
-def back_up(d_down, gp, weights, after=()):
-    t = d_down.shape[0]
-    nw = len(weights)
-
-    def kernel(dd_ref, gp_ref, *refs):
-        wrefs, refs = refs[:nw], refs[nw:]
-        du_ref, su_ref, wd, sd = refs
-        i = pl.program_id(0)
-
-        @pl.when(i == 0)
-        def _():
-            down_copies = weight_copies("down", wrefs, wd, sd)
-            start_all(down_copies)
-            wait_all(down_copies)
-
-        dd = dd_ref[...]
-        for c in range(0, FF, CH):
-            du = (dot_t(dd, wd[c : c + CH, :]) * gp_ref[:, c : c + CH].astype(F32)).astype(BF)
-            du_ref[:, c : c + CH] = du
-            partial = jnp.sum(du.astype(F32), axis=0, keepdims=True)
-            su_ref[:, c : c + CH] = jnp.where(i == 0, partial, su_ref[:, c : c + CH] + partial)
-
-    tok = lambda n: pl.BlockSpec((TB, n), lambda i: (i, 0))
-    return call(
-        kernel,
-        (t // TB,),
-        [tok(D), tok(FF)] + [ANY] * nw,
-        [tok(FF), pl.BlockSpec((1, FF), lambda i: (0, 0))],
-        [shaped((t, FF), BF), shaped((1, FF), F32)],
-        us=11,
-        scratch=[pltpu.VMEM((FF, D), BF), pltpu.SemaphoreType.DMA((16,))],
-        after=after,
-    )(d_down, gp, *weights)
-
-
-def back_first(d_upper, d_second, xhat, inverse, weights, gain, after=()):
-    t = d_upper.shape[0]
-    nw = len(weights)
-
-    def kernel(du_ref, ds_ref, xhat_ref, inv_ref, gain_ref, *refs):
-        wrefs, refs = refs[:nw], refs[nw:]
-        df_ref, da_ref, sums_ref, wu, su = refs
-
-        @pl.when(pl.program_id(0) == 0)
-        def _():
-            up_copies = weight_copies("up", wrefs, wu, su)
-            start_all(up_copies)
-            wait_all(up_copies)
-
-        d_normed = ds_ref[...] + dot_t(du_ref[...], wu[...])
-        xhat = xhat_ref[...]
-        d_first = normalize_back(d_normed * gain_ref[...], xhat, inv_ref[...])
-        df_ref[...] = d_first
-        d_att = d_first.astype(BF)
-        da_ref[...] = d_att
-        add_rows(sums_ref, (d_att.astype(F32), d_normed * xhat, d_normed))
-
-    tok = lambda n: pl.BlockSpec((TB, n), lambda i: (i, 0))
-    return call(
-        kernel,
-        (t // TB,),
-        [tok(FF), tok(D), tok(D), tok(1), whole((1, D))] + [ANY] * nw,
-        [tok(D), tok(D), pl.BlockSpec((3, D), lambda i: (0, 0))],
-        [shaped((t, D), F32), shaped((t, D), BF), shaped((3, D), F32)],
-        us=1,
-        scratch=[pltpu.VMEM((D, FF), BF), pltpu.SemaphoreType.DMA((64,))],
-        after=after,
-    )(d_upper, d_second, xhat, inverse, gain, *weights)
+    )(lengths, tokens, mixed, vec, bias_up, cot, *weights)
 
 
 def input_gradient(d_first, d_projected, w_qkv, after=()):
@@ -614,67 +585,83 @@
     )(d_first, *d_projected, w_qkv)
 
 
-def grad_down(where, active, d_down, direct, after=()):
+def grad_down(active, d_down, after=()):
     t = d_down.shape[0]
-    half = D // 2
-    blocks = 4
-    n = FF // blocks
-
-    def kernel(where_ref, a_ref, b_ref, *refs):
-        outs, (acc, sems) = refs[:-2], refs[-2:]
-        i = pl.program_id(0)
-        if not direct:
-            outs[0][...] = t_dot(a_ref[...], b_ref[...]).astype(BF)
-            return
-        acc[pl.ds(pl.multiple_of(i * n, n), n), :] = t_dot(a_ref[...], b_ref[...]).astype(BF)
-
-        @pl.when(i == blocks - 1)
-        def _():
-            copies = term_copies(
-                where_ref,
-                lambda owner_rows, h: acc.at[owner_rows, h * half : (h + 1) * half],
-                FF,
-                lambda ref, where: ref.at[where],
-                outs,
-                sems,
-                2,
-            )
-            start_all(copies)
-            wait_all(copies)
-
-    if direct:
-        out_shapes, out_specs = [shaped((2, 2, 4, FF // RANKS, half), BF)] * 2, [ANY] * 2
-    else:
-        out_shapes, out_specs = [shaped((FF, D), BF)], [pl.BlockSpec((n, D), lambda i, *_: (i, 0))]
-    return call(
-        kernel,
-        (blocks,),
-        [pl.BlockSpec((t, n), lambda i, *_: (0, i)), whole((t, D))],
-        out_specs,
-        out_shapes,
-        us=10,
-        scratch=[pltpu.VMEM((FF, D), BF), pltpu.SemaphoreType.DMA((2 * RANKS,))],
-        prefetch=1,
-        after=after,
-    )(where, active, d_down)
-
-
-def grad_up(nl, d_upper, after=()):
-    t = nl.shape[0]
     n = 768
 
-    def kernel(nl_ref, du_ref, out_ref):
-        out_ref[...] = t_dot(nl_ref[...], du_ref[...]).astype(BF)
+    def kernel(a_ref, b_ref, out_ref):
+        out_ref[...] = t_dot(a_ref[...], b_ref[...]).astype(BF)
 
     return call(
         kernel,
         (FF // n,),
-        [whole((t, D)), pl.BlockSpec((t, n), lambda i: (0, i))],
-        pl.BlockSpec((D, n), lambda i: (0, i)),
-        shaped((D, FF), BF),
+        [pl.BlockSpec((t, n), lambda i: (0, i)), whole((t, D))],
+        pl.BlockSpec((n, D), lambda i: (i, 0)),
+        shaped((FF, D), BF),
         us=9,
         after=after,
-    )(nl, d_upper)
+    )(active, d_down)
+
+
+STRIP = 384
+STRIPS = (FF + D) // 2 // STRIP
+
+
+def grad_up_out(where, nl, d_upper, mixed, d_att, direct, after=()):
+    t = nl.shape[0]
+
+    def kernel(where_ref, nl_ref, du_ref, m_ref, da_ref, *refs):
+        outs, (acc, sems) = refs[:-2], refs[-2:]
+        h = pl.program_id(0)
+        acc[h, :, : FF // 2] = t_dot(nl_ref[...], du_ref[...]).astype(BF)
+        acc[h, :, FF // 2 :] = t_dot(m_ref[...], da_ref[...]).astype(BF)
+
+        def copies_of(h):
+            if not direct:
+                return [pltpu.make_async_copy(acc.at[h], outs[0].at[h], sems.at[h, 0])]
+            me, replica = where_ref[0], where_ref[1]
+            rows = D // RANKS
+            copies = []
+            for j in range(RANKS):
+                owner_rows = pl.ds(pl.multiple_of((me ^ j) * rows, rows), rows)
+                for strip in range(STRIPS):
+                    target = outs[j & 1].at[
+                        h ^ replica, (j >> 1) & 1, j >> 2, strip * rows : (strip + 1) * rows
+                    ]
+                    source = acc.at[h, owner_rows, strip * STRIP : (strip + 1) * STRIP]
+                    copies.append(pltpu.make_async_copy(source, target, sems.at[h, len(copies)]))
+            return copies
+
+        start_all(copies_of(h))
+
+        @pl.when(h == 1)
+        def _():
+            wait_all(copies_of(0))
+            wait_all(copies_of(1))
+
+    if direct:
+        out_shapes = [shaped((2, 2, 4, STRIPS * D // RANKS, STRIP), BF)] * 2
+    else:
+        out_shapes = [shaped((2, D, (FF + D) // 2), BF)]
+    return call(
+        kernel,
+        (2,),
+        [
+            whole((t, D)),
+            pl.BlockSpec((t, FF // 2), lambda h, *_: (0, h)),
+            whole((t, D)),
+            pl.BlockSpec((t, D // 2), lambda h, *_: (0, h)),
+        ],
+        [ANY] * len(out_shapes),
+        out_shapes,
+        us=13,
+        scratch=[
+            pltpu.VMEM((2, D, (FF + D) // 2), BF),
+            pltpu.SemaphoreType.DMA((2, RANKS * STRIPS)),
+        ],
+        prefetch=1,
+        after=after,
+    )(where, nl, d_upper, mixed, d_att)
 
 
 def swap(x, mask):
@@ -692,10 +679,9 @@
     return total
 
 
-def gather_qkv(where, w, replica):
-    rows, columns = w.shape
-    half = columns // 2
-    own = lax.dynamic_slice_in_dim(w, replica * half, half, 1)
+def gather_qkv(where, own):
+    rows, half = own.shape
+    columns = 2 * half
     z = jnp.stack([own] + [swap(own, m) for m in (4, 8, 12)])
     zy = jnp.stack([z, swap(z, 2)])
     x = swap_replica(zy)
@@ -737,19 +723,18 @@
 
 
 class Chain:
-    def __init__(self, keep, send, lines=None, grow=False):
+    def __init__(self, keep, send, lines=None, two_steps=False):
         self.columns = keep.shape[-1]
         flat = lambda x: x.reshape(-1, self.columns)
         halves = [(swap_replica,)] if keep.ndim == 5 else []
         over = lambda m: lambda x: swap(x, m)
-        along_z = [(over(8),), (over(4),)] if grow else [(over(4), over(8), over(12))]
+        along_z = [(over(8),), (over(4),)] if two_steps else [(over(4), over(8), over(12))]
         fsdp = [(over(1),)] + halves + [(over(2),)] + along_z
         self.moves = fsdp + [(swap_replica,)]
         self.owner_rows = keep.shape[-2]
         self.stay, self.away = flat(keep), [flat(send)]
         self.lines = None if lines is None else flat(lines)
         self.rides = (len(fsdp) + 1 - len(halves)) if lines is not None else 0
-        self.grow = grow
 
     def send(self):
         moves = self.moves.pop(0)
@@ -761,28 +746,29 @@
         self.rides = max(self.rides - 1, 0)
 
 
-def add_all(chains, after=()):
+def add_all(chains, after=(), passing=()):
     operands, shapes, plans = [], [], []
     for c in chains:
         n = c.stay.shape[0]
         parts = len(c.moves[0]) + 1 if n > c.owner_rows else 1
         part = n // parts
         held = c.lines.shape[0] if c.arriving else 0
-        grown = held * (2 if c.grow else 1)
-        rides = grown if c.rides else 0
+        rides = held if c.rides else 0
         ins = [c.stay] + c.received + (c.beside + [c.lines] if held else [])
         outs = [shaped((part, c.columns), BF)]
         sends = parts - 1 if parts > 1 else int(rides > 0)
         outs += [shaped((part + rides, c.columns), BF)] * sends
         if held:
-            outs.append(shaped((grown, c.columns), BF))
-        plans.append((len(ins), len(outs), n, part, parts, sends, held, rides, len(c.received), len(c.beside), c.grow))
+            outs.append(shaped((held, c.columns), BF))
+        plans.append((len(ins), len(outs), n, part, parts, sends, held, rides, len(c.received), len(c.beside)))
         operands += ins
         shapes += outs
 
+    passed, inputs = len(passing), len(operands)
+
     def kernel(*refs):
-        sources, targets = refs[: len(operands)], refs[len(operands) :]
-        for n_in, n_out, n, part, parts, sends, held, rides, arrivals, beside, grow in plans:
+        sources, targets = refs[: len(operands)], refs[len(operands) + passed :]
+        for n_in, n_out, n, part, parts, sends, held, rides, arrivals, beside in plans:
             ins, sources = sources[:n_in], sources[n_in:]
             outs, targets = targets[:n_out], targets[n_out:]
             received = ins[1 : 1 + arrivals]
@@ -801,13 +787,10 @@
                     others = [ins[1 + arrivals][...]]
                 else:
                     others = [r[n : n + held, :] for r in received]
-                if grow:
-                    lines = jnp.concatenate([mine, others[0]], axis=0)
-                else:
-                    total = mine.astype(F32)
-                    for other in others:
-                        total = total + other.astype(F32)
-                    lines = total.astype(BF)
+                total = mine.astype(F32)
+                for other in others:
+                    total = total + other.astype(F32)
+                lines = total.astype(BF)
                 outs[-1][...] = lines
                 if rides:
                     for out in outs[1 : 1 + sends]:
@@ -817,12 +800,13 @@
         call(
             kernel,
             (1,),
-            [whole(x.shape) for x in operands],
-            [whole(x.shape) for x in shapes],
-            shapes,
+            [whole(x.shape) for x in operands] + [ANY] * passed,
+            [whole(x.shape) for x in shapes] + [ANY] * passed,
+            shapes + [shaped(x.shape, x.dtype) for x in passing],
             us=2,
             after=after,
-        )(*operands)
+            aliases={inputs + i: len(shapes) + i for i in range(passed)},
+        )(*operands, *passing)
     )
     for c, plan in zip(chains, plans):
         n_out, sends, held = plan[1], plan[5], plan[6]
@@ -831,6 +815,7 @@
         c.away = mine[1 : 1 + sends] if sends else [mine[0]]
         if held:
             c.lines = mine[-1]
+    return results
 
 
 SMALL = ("bias_qv", "bias_out", "gain_one", "shift_one", "bias_up", "bias_down", "gain_two", "shift_two")
@@ -863,125 +848,106 @@
     where = jnp.stack([me, replica]).astype(jnp.int32)
     gather = lambda w: lax.all_gather(w, "fsdp", axis=0, tiled=True)
 
-    small = jnp.concatenate(
-        [bias_qv, bias_out, gain_one, shift_one, bias_up, bias_down, gain_two, shift_two]
-    )
-    count = small.shape[0]
-    lines = -(-count // PAD)
-    small = jnp.pad(small, (0, lines * PAD - count)).reshape(lines, PAD)
-    small = jnp.pad(small, ((0, w_qkv.shape[0] - lines), (0, 0)))
-    first = jnp.concatenate([w_qkv, small], axis=1)
+    small = (bias_qv, bias_out, gain_one, shift_one, bias_up, bias_down, gain_two, shift_two)
     if direct:
-        w_first = gather_qkv(where, first, replica)
-        packed = gather(pack_weights(w_out, w_up, w_down))
-        weights = (packed.reshape(ranks, -1, D),)
+        packed, own = pack_weights(where, w_qkv, small, w_out, w_up, w_down)
+        w_first = gather_qkv(where, own)
+        weights = (gather(packed).reshape(ranks, -1, D),)
     else:
-        w_first = gather(first)
+        w_first = gather(w_qkv)
         weights = (gather(w_out), gather(w_up), gather(w_down))
-    small_all = w_first.reshape(ranks, -1, 3 * D + PAD)[:, :lines, 3 * D :].reshape(ranks, -1)
-    vectors, start = {}, 0
-    for name, size in zip(SMALL, SMALL_SIZES):
-        part = size // ranks
-        vectors[name] = small_all[:, start : start + part].reshape(size).astype(F32)
-        start += part
+    vectors = {}
+    if direct:
+        beside = w_first[:, 3 * D :].reshape(ranks, -1, PAD)
+    for k, (name, value) in enumerate(zip(SMALL, small)):
+        got = beside[:, k, : value.shape[0]].reshape(-1) if direct else gather(value)
+        vectors[name] = got.astype(F32)
 
     bias = vectors["bias_qv"].reshape(2, GROUPS, GW).transpose(1, 0, 2)
     kept = attend_forward(lengths, tokens, w_first, bias)
     mixed = kept[4]
-    vec_one = jnp.stack([vectors["bias_out"], vectors["gain_one"], vectors["shift_one"]])
-    xhat, inverse, nl, active, gp = up(tokens, mixed, weights, vec_one, vectors["bias_up"][None])
-    vec_two = jnp.stack(
-        [vectors[n] for n in ("gain_one", "shift_one", "bias_down", "gain_two", "shift_two")]
+    vec = jnp.stack(
+        [
+            vectors[n]
+            for n in ("bias_out", "gain_one", "shift_one", "bias_down", "gain_two", "shift_two")
+        ]
     )
-    layer_out, d_second, d_down, sums_two, pool = down(
-        lengths, active, xhat, weights, vec_two, cotangent
+    (layer_out, nl, active, d_down, d_upper, d_first, d_att, sums, sums_up, pool) = middle(
+        lengths, tokens, mixed, weights, vec, vectors["bias_up"][None], cotangent
     )
     pooled = pool / lengths.astype(F32)[:, :, None]
 
-    terms_down = grad_down(where, active, d_down, direct)
+    terms_up = grad_up_out(where, nl, d_upper, mixed, d_att, direct)
+    term_down = grad_down(active, d_down, after=(terms_up[0],))
+    scatter = lambda x: lax.psum_scatter(x, "fsdp", scatter_dimension=0, tiled=True)
+
+    def small_lines(sums_a, sums_b):
+        both = jnp.concatenate([sums_a, sums_b], axis=1)
+        return jnp.concatenate([both, sums[3:], sums_up.reshape(-1, D), sums[:3]])
+
+    shard_down = scatter(term_down)
+    attend_back = functools.partial(attend_backward, where, d_att, tokens, weights)
     if direct:
-        chain_w = Chain(*terms_down, pooled.astype(BF), True)
-        chain_w.send()
-    d_upper, sums_up = back_up(d_down, gp, weights, after=(terms_down[0],))
-    if direct:
-        add_all([chain_w], after=(sums_up,))
-        chain_w.send()
-        term_up = grad_up(nl, d_upper, after=(chain_w.away[0],))
-    else:
-        term_up = grad_up(nl, d_upper)
-    first_args = (d_upper, d_second, xhat, inverse, weights, vectors["gain_one"][None])
-    scatter = lambda x: lax.psum_scatter(x, "fsdp", scatter_dimension=0, tiled=True)
-
-    def small_lines(sums_one, sums_a, sums_b):
-        return jnp.concatenate(
-            [
-                jnp.concatenate([sums_a, sums_b], axis=1),
-                sums_one,
-                sums_up.reshape(-1, D),
-                sums_two,
-            ]
-        )
-
-    shard_up = scatter(term_up)
-    if direct:
-        d_first, d_att, sums_one = back_first(*first_args, after=(term_up,))
-        attend_back = functools.partial(attend_backward, where, d_att, tokens, weights)
-        dp_a, sums_a, *terms_a = attend_back((0, 1), kept, True, 2, after=(chain_w.away[0],))
+        chain_u = Chain(*terms_up, two_steps=True)
+        chain_u.send()
+        add_all([chain_u], after=(term_down,))
+        chain_u.send()
+        dp_a, sums_a, *terms_a = attend_back((0, 1), kept, True, 2, after=(chain_u.away[0],))
         chain_a = Chain(*terms_a)
-        add_all([chain_w], after=(sums_a,))
-        chain_w.send()
+        chain_a.away[0], pooled = add_all([chain_u], after=(sums_a,), passing=(chain_a.away[0], pooled))
+        pooled_all = lax.all_gather(pooled, ("replica", "fsdp"), axis=0, tiled=True)
+        chain_u.send()
         chain_a.send()
-        dp_b, sums_b, *terms_b = attend_back((2,), kept, True, 1, after=(chain_w.away[0],))
-        small = small_lines(sums_one, sums_a, sums_b)
+        add_all([chain_a])
+        chain_a.send()
+        dp_b, sums_b, *terms_b = attend_back((2,), kept, True, 1, after=(chain_a.away[0],))
+        small = small_lines(sums_a, sums_b)
         small = jnp.pad(small, ((0, -small.shape[0] % 16), (0, 0))).astype(BF)
-        chain_b = Chain(*terms_b, small, False)
+        chain_b = Chain(*terms_b, small)
         chain_b.send()
-        add_all([chain_w, chain_a], after=(sums_b,))
-        chain_w.send()
+        add_all([chain_u, chain_a], after=(sums_b,))
+        chain_u.send()
         chain_a.send()
         input_grad = input_gradient(
-            d_first, (dp_a, dp_b), w_first, after=(chain_a.away[0], shard_up)
+            d_first, (dp_a, dp_b), w_first, after=(chain_a.away[0],)
         )
-        add_all([chain_w, chain_a, chain_b], after=(input_grad,))
-        chain_w.send()
+        add_all([chain_u, chain_a, chain_b], after=(input_grad,))
+        chain_u.send()
         chain_a.send()
         chain_b.send()
-        while chain_w.moves or chain_a.moves or chain_b.moves:
-            moving = [c for c in (chain_w, chain_a, chain_b) if c.moves]
-            add_all(moving)
+        while chain_u.moves or chain_a.moves or chain_b.moves:
+            moving = [c for c in (chain_u, chain_a, chain_b) if c.moves]
+            add_all(moving, after=(shard_down,) if len(moving) > 1 else (shard_down, pooled_all))
             for c in moving:
                 c.send()
-        h0, h1 = ordered(chain_w.stay, chain_w.received[0][: chain_w.owner_rows], replica)
-        grad_w_down = jnp.concatenate([h0, h1], axis=1).astype(F32)
-        grad_w_up = added(shard_up, swap_replica(shard_up))
+        halves_u = ordered(chain_u.stay, chain_u.received[0][: chain_u.owner_rows], replica)
+        halves_u = [
+            h.reshape(STRIPS, -1, STRIP).transpose(1, 0, 2).reshape(-1, STRIPS * STRIP)
+            for h in halves_u
+        ]
+        grad_w_down = added(shard_down, swap_replica(shard_down))
         h0, h1 = ordered(chain_a.stay, chain_a.received[0], replica)
         span = 3 * GW // 2
         halves_a = [
             jnp.concatenate([h[:, i * span : (i + 1) * span] for h in (h0, h1)], axis=1).astype(F32)
-            for i in range(3)
+            for i in range(2)
         ]
         sum_b = added(chain_b.stay, chain_b.received[0][: chain_b.owner_rows])
         lines = added(chain_b.lines, chain_b.received[0][chain_b.owner_rows :])
-        grad_w_out = halves_a[0]
-        parts = halves_a[1:] + [sum_b]
-        relative = chain_w.lines.reshape((2,) * 5 + pooled.shape)
-        relative = relative.transpose(3, 1, 0, 2, 4, 5, 6, 7).reshape((2, ranks) + pooled.shape)
-        pooled_all = relative[jnp.arange(2) ^ replica][:, me ^ jnp.arange(ranks)]
-        pooled_all = pooled_all.reshape((2 * ranks * pooled.shape[0],) + pooled.shape[1:]).astype(F32)
+        parts = halves_a + [sum_b]
     else:
-        d_first, d_att, sums_one = back_first(*first_args)
-        attend_back = functools.partial(attend_backward, where, d_att, tokens, weights)
         dp_a, sums_a, term_a = attend_back((0, 1), kept, False, 1)
         dp_b, sums_b, term_b = attend_back((2,), kept, False, 1)
         input_grad = input_gradient(d_first, (dp_a, dp_b), w_first)
         pooled_all = lax.all_gather(pooled, ("replica", "fsdp"), axis=0, tiled=True)
         reduce = lambda x: lax.psum(scatter(x), "replica").astype(F32)
-        grad_w_down = reduce(terms_down[0])
-        grad_w_up = lax.psum(shard_up, "replica").astype(F32)
+        grad_w_down = lax.psum(shard_down, "replica").astype(F32)
+        halves_u = [reduce(terms_up[0][h]) for h in range(2)]
         sum_a, sum_b = reduce(term_a), reduce(term_b)
-        lines = lax.psum(small_lines(sums_one, sums_a, sums_b), ("replica", "fsdp"))
-        grad_w_out = sum_a[:, :D]
-        parts = [sum_a[:, D : 2 * D], sum_a[:, 2 * D :], sum_b]
+        lines = lax.psum(small_lines(sums_a, sums_b), ("replica", "fsdp"))
+        parts = [sum_a[:, :D], sum_a[:, D:], sum_b]
+    grad_w_up = jnp.concatenate([h[:, : FF // 2] for h in halves_u], axis=1).astype(F32)
+    grad_w_out = jnp.concatenate([h[:, FF // 2 :] for h in halves_u], axis=1).astype(F32)
     grad_w_qkv = jnp.concatenate(
         [p[:, i * GW : (i + 1) * GW] for i in range(3) for p in parts], axis=1
     )

time: 357 us -> 337 us (0.944)
  Pallas kernels: 190 us -> 177 us
  local copies, waits for them, and re-layouts: 24.8 us -> 18.1 us
  other arithmetic: 6 us -> 9.68 us
    ppermute x22 -> x21, waiting for transfers between devices: 68.8 us -> 47.9 us  [swap(): return lax.ppermute(x, 'fsdp', [(i, i ^ mask) for i in range(RANKS)])]
    ppermute x7, waiting for transfers between devices: 16.8 us -> 37 us  [swap_replica(): return lax.ppermute(x, 'replica', [(0, 1), (1, 0)])]
    pallas_call x17 -> x16, Pallas kernels: 190 us -> 177 us  [call(): pl.pallas_call(run, grid_spec=pltpu.PrefetchScalarGridSpec(num_scalar_pre...]
    unnamed x106 -> x75, local copies, waits for them, and re-layouts: 13.1 us -> 10.3 us
    ppermute x22 -> x21, starting transfers between devices: 21.1 us -> 18.7 us  [swap(): return lax.ppermute(x, 'fsdp', [(i, i ^ mask) for i in range(RANKS)])]
  transfers between devices with their start and end apart: 31 -> 31, of which waited for: 12 -> 14; matrix products, arithmetic and copies ran while one was open for 5% -> 3% of each run, Pallas kernels for 36% -> 31%
where the time goes in v3:
time: 337 us; the launch traced here: 333 us
  Pallas kernels  177 us (53%)
  waiting for transfers between devices  87.5 us (26%)
  starting transfers between devices  26.8 us (8%)
  local copies, waits for them, and re-layouts  18.1 us (5%)
  between operations  14.3 us (4%)
  other arithmetic  9.68 us (3%)
    pallas_call x16, Pallas kernels, call(): pl.pallas_call(run, grid_spec=pltpu.PrefetchScalarGridSpec(num_scalar_pre...  177 us
    ppermute x21, waiting for transfers between devices, swap(): return lax.ppermute(x, 'fsdp', [(i, i ^ mask) for i in range(RANKS)])  47.9 us
    ppermute x7, waiting for transfers between devices, swap_replica(): return lax.ppermute(x, 'replica', [(0, 1), (1, 0)])  37 us
    ppermute x21, starting transfers between devices, swap(): return lax.ppermute(x, 'fsdp', [(i, i ^ mask) for i in range(RANKS)])  18.7 us
    unnamed x75, local copies, waits for them, and re-layouts  10.3 us
    ppermute x7, starting transfers between devices, swap_replica(): return lax.ppermute(x, 'replica', [(0, 1), (1, 0)])  8.05 us
  transfers between devices with their start and end apart: 31, of which 14 were waited for; matrix products, arithmetic and copies ran while one was open for 3% of the time, Pallas kernels for 31%

profile of v3, /device:TPU:20, one launch (start us, length us, event | category | flops | bytes accessed | tf_op | source)
XLA Modules:
  0.0 333.4 jit_solution(8105634733286943387)
XLA Ops:
  9.0 2.8 shard_map.262
  12.5 3.5 %collective-permute-start.1 = (bf16[48,1280]{1,0:T(8,128)(2,1)}, bf16[48,1280]{1,0:T(8,128)(2,1)S(1)}, u32[]{:S(2)}, u32[]{:S(2)}) collective-permute-start(bf16[48,1280]{1,0:T(8,128)(2,1)} %get-tuple-element.73), channel_id=1, source_target_pairs={{0,8},{1,9},{2,10},{3,11},{4,12},{5,13},{6,14},{7,15},{8,0},{9,1},... | collective-permute-start | bytes 368648 | tf_op jit(solution)/shard_map/ppermute | solution.py:668
  16.0 8.6 %collective-permute-done.2 = bf16[48,1280]{1,0:T(8,128)(2,1)S(1)} collective-permute-done((bf16[48,1280]{1,0:T(8,128)(2,1)}, bf16[48,1280]{1,0:T(8,128)(2,1)S(1)}, u32[]{:S(2)}, u32[]{:S(2)}) %collective-permute-start.2) | collective-permute-done | bytes 122912 | tf_op jit(solution)/shard_map/ppermute | solution.py:668
  26.6 14.1 %collective-permute-done.3 = bf16[4,48,1280]{2,1,0:T(8,128)(2,1)S(1)} collective-permute-done((bf16[4,48,1280]{2,1,0:T(8,128)(2,1)S(1)}, bf16[4,48,1280]{2,1,0:T(8,128)(2,1)S(1)}, u32[]{:S(2)}, u32[]{:S(2)}) %collective-permute-start.3) | collective-permute-done | bytes 491552 | tf_op jit(solution)/shard_map/ppermute | solution.py:668
  42.3 21.2 %collective-permute-done.4.refs_2_ = bf16[2,4,48,1280]{3,2,1,0:T(8,128)(2,1)S(1)} collective-permute-done((bf16[2,4,48,1280]{3,2,1,0:T(8,128)(2,1)S(1)}, bf16[2,4,48,1280]{3,2,1,0:T(8,128)(2,1)S(1)}, u32[]{:S(2)}, u32[]{:S(2)}) %collective-permute-start.4) | collective-permute-done | bytes 983072 | tf_op jit(solution)/shard_map/ppermute | solution.py:672
  67.0 5.1 %shard_map.263.refs_2_.refs_3_.refs_4_ = bf16[768,2560]{1,0:T(8,128)(2,1)} custom-call(s32[2]{0:T(128)} %pad_add_fusion.refs_0_, bf16[2,4,48,1280]{3,2,1,0:T(8,128)(2,1)} %copy-done.2, bf16[2,4,48,1280]{3,2,1,0:T(8,128)(2,1)} %copy-done.15, bf16[2,4,48,1280]{3,2,1,0:T(8,128)(2,1)} %copy-done.16, bf16[2,4,48,1280]{3,2,1,0:T(8,128)(2,1)} %copy-done.17), custom_call_target="tpu_custom_call" | custom-call | flops 4600000000 | bytes 14400000 | tf_op jit(solution)/shard_map/pallas_call | solution.py:58
  75.9 27.8 %shard_map.264 = (bf16[1024,768]{1,0:T(8,128)(2,1)}, bf16[1024,768]{1,0:T(8,128)(2,1)}, bf16[1024,768]{1,0:T(8,128)(2,1)}, bf16[6,2,4,384,256]{4,3,2,1,0:T(8,128)(2,1)}, bf16[1024,768]{1,0:T(8,128)(2,1)}) custom-call(s32[2,8]{1,0:T(2,128)} %refs_0_.3, bf16[1024,768]{1,0:T(8,128)(2,1)} %refs_2_.5, bf16[768,2560]{1,0:T(8,128)(2,1)} %shard_map.263.refs_2_.refs_3_.refs_4_, ...), custom_call_target="tpu_custom_call" | custom-call | flops 32199999488 | bytes 100800000 | tf_op jit(solution)/shard_map/pallas_call | solution.py:58
  103.7 46.1 %shard_map.265 = (bf16[1024,768]{1,0:T(8,128)(2,1)}, bf16[1024,768]{1,0:T(8,128)(2,1)}, bf16[1024,3072]{1,0:T(8,128)(2,1)}, bf16[1024,768]{1,0:T(8,128)(2,1)}, b...) custom-call(s32[2,8]{1,0:T(2,128)} %refs_0_.3, ...), custom_call_target="tpu_custom_call" | custom-call | flops 51749998592 | bytes 162000000 | tf_op jit(solution)/shard_map/pallas_call | solution.py:58
  149.8 14.0 %shard_map.266 = (bf16[2,2,4,240,384]{4,3,2,1,0:T(8,128)(2,1)}, bf16[2,2,4,240,384]{4,3,2,1,0:T(8,128)(2,1)}) custom-call(s32[2]{0:T(128)} %pad_add_fusion.refs_0_, bf16[1024,768]{1,0:T(8,128)(2,1)} %get-tuple-element.83.refs_1_, bf16[1024,3072]{1,0:T(8,128)(2,1)} %get-tuple-element.84.refs_2_, bf16[1024,768]{1,0:T(8,128)(2,1)} %get-tuple-element.74.refs_2_.refs_3_, ...), custom_call_target="tpu_custom_call" | custom-call | flops 14949999616 | bytes 46800000 | tf_op jit(solution)/shard_map/pallas_call | solution.py:58
  163.8 9.2 %shard_map.267.refs_2_ = bf16[3072,768]{1,0:T(8,128)(2,1)} custom-call(bf16[1024,3072]{1,0:T(8,128)(2,1)} %get-tuple-element.87.refs_0_, bf16[1024,768]{1,0:T(8,128)(2,1)} %get-tuple-element.88.refs_1_, bf16[2,2,4,240,384]{4,3,2,1,0:T(8,128)(2,1)} %get-tuple-element.85.refs_2_), custom_call_target="tpu_custom_call" | custom-call | flops 10350000128 | bytes 32400000 | tf_op jit(solution)/shard_map/pallas_call | solution.py:58
  175.0 5.2 %collective-permute-done.7.refs_1_ = bf16[3840,384]{1,0:T(8,128)(2,1)S(1)} collective-permute-done((bf16[3840,384]{1,0:T(8,128)(2,1)S(1)}, bf16[3840,384]{1,0:T(8,128)(2,1)S(1)}, u32[]{:S(2)}, u32[]{:S(2)}) %collective-permute-start.7) | collective-permute-done | bytes 2949152 | tf_op jit(solution)/shard_map/ppermute | solution.py:668
  181.8 5.1 %shard_map.268 = (bf16[1920,384]{1,0:T(8,128)(2,1)}, bf16[1920,384]{1,0:T(8,128)(2,1)}) custom-call(bf16[3840,384]{1,0:T(8,128)(2,1)} %bitcast.61, bf16[3840,384]{1,0:T(8,128)(2,1)} %copy-done, bf16[3072,768]{1,0:T(8,128)(2,1)} %shard_map.267.refs_2_), custom_call_target="tpu_custom_call" | custom-call | flops 2300000000 | bytes 7200000 | tf_op jit(solution)/shard_map/pallas_call | solution.py:58
  189.0 26.4 %shard_map.269 = (bf16[1024,1536]{1,0:T(8,128)(2,1)}, f32[2,512]{1,0:T(2,128)}, bf16[2,2,4,48,768]{4,3,2,1,0:T(8,128)(2,1)}, bf16[2,2,4,48,768]{4,3,2,1,0:T(8,128)(2,1)}) custom-call(s32[2]{0:T(128)} %pad_add_fusion.refs_0_, bf16[1024,768]{1,0:T(8,128)(2,1)} %get-tuple-element.78.refs_4_.refs_1_, bf16[1024,768]{1,0:T(8,128)(2,1)} %refs_2_.5, ...), custom_call_target="tpu_custom_call" | custom-call | flops 1150000000 | bytes 3600000 | tf_op jit(solution)/shard_map/pallas_call | solution.py:58
  215.5 6.0 %collective-permute-done.8.refs_1_ = bf16[1920,384]{1,0:T(8,128)(2,1)S(1)} collective-permute-done((bf16[1920,384]{1,0:T(8,128)(2,1)}, bf16[1920,384]{1,0:T(8,128)(2,1)S(1)}, u32[]{:S(2)}, u32[]{:S(2)}) %collective-permute-start.8) | collective-permute-done | bytes 1474592 | tf_op jit(solution)/shard_map/ppermute | solution.py:672
  222.5 3.2 shard_map.270
  229.9 2.8 shard_map.271
  234.3 15.7 %shard_map.272 = (bf16[1024,768]{1,0:T(8,128)(2,1)}, f32[2,256]{1,0:T(2,128)}, bf16[2,4,48,768]{3,2,1,0:T(8,128)(2,1)}, bf16[2,4,48,768]{3,2,1,0:T(8,128)(2,1)}) custom-call(s32[2]{0:T(128)} %pad_add_fusion.refs_0_, bf16[1024,768]{1,0:T(8,128)(2,1)} %get-tuple-element.78.refs_4_.refs_1_, bf16[1024,768]{1,0:T(8,128)(2,1)} %refs_2_.5, ...), custom_call_target="tpu_custom_call" | custom-call | flops 1150000000 | bytes 3600000 | tf_op jit(solution)/shard_map/pallas_call | solution.py:58
  252.4 2.8 shard_map.273
  256.7 9.1 %shard_map.274.refs_8_ = f32[1024,768]{1,0:T(8,128)} custom-call(f32[1024,768]{1,0:T(8,128)} %get-tuple-element.77.refs_0_, bf16[1024,1536]{1,0:T(8,128)(2,1)} %get-tuple-element.90.refs_1_, bf16[1024,768]{1,0:T(8,128)(2,1)} %get-tuple-element.98.refs_2_, bf16[768,2560]{1,0:T(8,128)(2,1)} %shard_map.263.refs_2_.refs_3_.refs_4_, ...), custom_call_target="tpu_custom_call" | custom-call | flops 10350000128 | bytes 32400000 | tf_op jit(solution)/shard_map/pallas_call | solution.py:58
  265.8 7.5 %collective-permute-done.12.refs_1_ = bf16[480,384]{1,0:T(8,128)(2,1)S(1)} collective-permute-done((bf16[480,384]{1,0:T(8,128)(2,1)}, bf16[480,384]{1,0:T(8,128)(2,1)S(1)}, u32[]{:S(2)}, u32[]{:S(2)}) %collective-permute-start.12) | collective-permute-done | bytes 368672 | tf_op jit(solution)/shard_map/ppermute | solution.py:668
  279.8 3.1 collective-permute-start.18
  283.2 5.2 %collective-permute-done.17.refs_3_ = bf16[48,768]{1,0:T(8,128)(2,1)S(1)} collective-permute-done((bf16[48,768]{1,0:T(8,128)(2,1)}, bf16[48,768]{1,0:T(8,128)(2,1)S(1)}, u32[]{:S(2)}, u32[]{:S(2)}) %collective-permute-start.17) | collective-permute-done | bytes 73760 | tf_op jit(solution)/shard_map/ppermute | solution.py:668
  301.5 6.8 %collective-permute-done.26 = bf16[240,384]{1,0:T(8,128)(2,1)S(1)} collective-permute-done((bf16[240,384]{1,0:T(8,128)(2,1)}, bf16[240,384]{1,0:T(8,128)(2,1)S(1)}, u32[]{:S(2)}, u32[]{:S(2)}) %collective-permute-start.26) | collective-permute-done | bytes 184352 | tf_op jit(solution)/shard_map/ppermute | solution.py:672
  317.5 3.0 collective-permute-done.25
  (193 shorter events, 64.8 us)
Async XLA Ops:
  7.2 96.6 %all-gather.3.cloned.1.call-start = ((), (), s32[]{:S(2)}) async-start(), calls=%async_computation.1 | async-start | bytes 11280384 | tf_op jit(solution)/shard_map/all_gather | solution.py:849
  11.9 279.2 %reduce-scatter.2.cloned.1.call-start = ((), (), s32[]{:S(2)}) async-start(), calls=%async_computation.3 | async-start | bytes 5013504 | tf_op jit(solution)/shard_map/reduce_scatter | solution.py:882
  12.0 12.6 %collective-permute-start.2 = (bf16[48,1280]{1,0:T(8,128)(2,1)}, bf16[48,1280]{1,0:T(8,128)(2,1)S(1)}, u32[]{:S(2)}, u32[]{:S(2)}) collective-permute-start(bf16[48,1280]{1,0:T(8,128)(2,1)} %get-tuple-element.73), channel_id=1, source_target_pairs={{0,12},{1,13},{2,14},{3,15},{4,8},{5,9},{6,10},{7,11},{8,4},{9,5},... | collective-permute-start | bytes 368648 | tf_op jit(solution)/shard_map/ppermute | solution.py:668
  12.5 12.6 %collective-permute-start.1 = (bf16[48,1280]{1,0:T(8,128)(2,1)}, bf16[48,1280]{1,0:T(8,128)(2,1)S(1)}, u32[]{:S(2)}, u32[]{:S(2)}) collective-permute-start(bf16[48,1280]{1,0:T(8,128)(2,1)} %get-tuple-element.73), channel_id=1, source_target_pairs={{0,8},{1,9},{2,10},{3,11},{4,12},{5,13},{6,14},{7,15},{8,0},{9,1},... | collective-permute-start | bytes 368648 | tf_op jit(solution)/shard_map/ppermute | solution.py:668
  16.0 9.2 %collective-permute-start = (bf16[48,1280]{1,0:T(8,128)(2,1)}, bf16[48,1280]{1,0:T(8,128)(2,1)S(1)}, u32[]{:S(2)}, u32[]{:S(2)}) collective-permute-start(bf16[48,1280]{1,0:T(8,128)(2,1)} %get-tuple-element.73), channel_id=1, source_target_pairs={{0,4},{1,5},{2,6},{3,7},{4,0},{5,1},{6,2},{7,3},{8,12},{9,13},{10,... | collective-permute-start | bytes 368648 | tf_op jit(solution)/shard_map/ppermute | solution.py:668
  26.1 14.6 %collective-permute-start.3 = (bf16[4,48,1280]{2,1,0:T(8,128)(2,1)S(1)}, bf16[4,48,1280]{2,1,0:T(8,128)(2,1)S(1)}, u32[]{:S(2)}, u32[]{:S(2)}) collective-permute-start(bf16[4,48,1280]{2,1,0:T(8,128)(2,1)S(1)} %get-tuple-element.144), channel_id=1, source_target_pairs={{0,2},{1,3},{2,0},{3,1},{4,6},{5,7},{6,4},{7,5},{8,10},{9,11},{10,... | collective-permute-start | bytes 1474568 | tf_op jit(solution)/shard_map/ppermute | solution.py:668
  40.8 22.7 %collective-permute-start.4 = (bf16[2,4,48,1280]{3,2,1,0:T(8,128)(2,1)S(1)}, bf16[2,4,48,1280]{3,2,1,0:T(8,128)(2,1)S(1)}, u32[]{:S(2)}, u32[]{:S(2)}) collective-permute-start(bf16[2,4,48,1280]{3,2,1,0:T(8,128)(2,1)S(1)} %pad_maximum_fusion.refs_1_), channel_id=1, source_target_pairs={{0,16},{16,0},{1,17},{17,1},{2,18},{18,2},{3,19},{19,3},{4,20},{20... | collective-permute-start | bytes 2949128 | tf_op jit(solution)/shard_map/ppermute | solution.py:672
  42.3 21.2 %collective-permute-start.5 = (bf16[2,4,48,1280]{3,2,1,0:T(8,128)(2,1)S(1)}, bf16[2,4,48,1280]{3,2,1,0:T(8,128)(2,1)S(1)}, u32[]{:S(2)}, u32[]{:S(2)}) collective-permute-start(bf16[2,4,48,1280]{3,2,1,0:T(8,128)(2,1)S(1)} %pad_maximum_fusion.refs_1_), channel_id=1, source_target_pairs={{0,1},{1,0},{2,3},{3,2},{4,5},{5,4},{6,7},{7,6},{8,9},{9,8},{10,11... | collective-permute-start | bytes 2949128 | tf_op jit(solution)/shard_map/ppermute | solution.py:668
  173.0 140.5 %all-gather.5.cloned.1.call-start = ((), (), s32[]{:S(2)}) async-start(), calls=%async_computation.2 | async-start | bytes 1622016 | tf_op jit(solution)/shard_map/all_gather | solution.py:898
  186.9 34.5 %collective-permute-start.8 = (bf16[1920,384]{1,0:T(8,128)(2,1)}, bf16[1920,384]{1,0:T(8,128)(2,1)S(1)}, u32[]{:S(2)}, u32[]{:S(2)}) collective-permute-start(bf16[1920,384]{1,0:T(8,128)(2,1)} %get-tuple-element.89.refs_9_), channel_id=1, source_target_pairs={{0,16},{16,0},{1,17},{17,1},{2,18},{18,2},{3,19},{19,3},{4,20},{20... | collective-permute-start | bytes 4423688 | tf_op jit(solution)/shard_map/ppermute | solution.py:672
  225.8 25.5 %collective-permute-start.10 = (bf16[960,384]{1,0:T(8,128)(2,1)}, bf16[960,384]{1,0:T(8,128)(2,1)S(1)}, u32[]{:S(2)}, u32[]{:S(2)}) collective-permute-start(bf16[960,384]{1,0:T(8,128)(2,1)} %get-tuple-element.100), channel_id=1, source_target_pairs={{0,2},{1,3},{2,0},{3,1},{4,6},{5,7},{6,4},{7,5},{8,10},{9,11},{10,... | collective-permute-start | bytes 2211848 | tf_op jit(solution)/shard_map/ppermute | solution.py:668
  232.7 18.6 %collective-permute-start.11 = (bf16[384,768]{1,0:T(8,128)(2,1)}, bf16[384,768]{1,0:T(8,128)(2,1)S(1)}, u32[]{:S(2)}, u32[]{:S(2)}) collective-permute-start(bf16[384,768]{1,0:T(8,128)(2,1)} %get-tuple-element.97.refs_9_), channel_id=1, source_target_pairs={{0,16},{16,0},{1,17},{17,1},{2,18},{18,2},{3,19},{19,3},{4,20},{20... | collective-permute-start | bytes 1769480 | tf_op jit(solution)/shard_map/ppermute | solution.py:672
  250.7 15.0 %collective-permute-start.15 = (bf16[16,768]{1,0:T(8,128)(2,1)S(1)}, bf16[16,768]{1,0:T(8,128)(2,1)S(1)}, u32[]{:S(2)}, u32[]{:S(2)}) collective-permute-start(bf16[16,768]{1,0:T(8,128)(2,1)S(1)} %fusion.8.refs_7_), channel_id=1, source_target_pairs={{0,1},{1,0},{2,3},{3,2},{4,5},{5,4},{6,7},{7,6},{8,9},{9,8},{10,11... | collective-permute-start | bytes 73736 | tf_op jit(solution)/shard_map/ppermute | solution.py:668
  250.8 15.0 %collective-permute-start.14 = (bf16[384,768]{1,0:T(8,128)(2,1)}, bf16[384,768]{1,0:T(8,128)(2,1)S(1)}, u32[]{:S(2)}, u32[]{:S(2)}) collective-permute-start(bf16[384,768]{1,0:T(8,128)(2,1)} %bitcast.82), channel_id=1, source_target_pairs={{0,1},{1,0},{2,3},{3,2},{4,5},{5,4},{6,7},{7,6},{8,9},{9,8},{10,11... | collective-permute-start | bytes 1769480 | tf_op jit(solution)/shard_map/ppermute | solution.py:668
  255.2 10.6 %collective-permute-start.13 = (bf16[192,768]{1,0:T(8,128)(2,1)}, bf16[192,768]{1,0:T(8,128)(2,1)S(1)}, u32[]{:S(2)}, u32[]{:S(2)}) collective-permute-start(bf16[192,768]{1,0:T(8,128)(2,1)} %get-tuple-element.103.refs_4_), channel_id=1, source_target_pairs={{0,2},{1,3},{2,0},{3,1},{4,6},{5,7},{6,4},{7,5},{8,10},{9,11},{10,... | collective-permute-start | bytes 884744 | tf_op jit(solution)/shard_map/ppermute | solution.py:668
  256.7 16.6 %collective-permute-start.12 = (bf16[480,384]{1,0:T(8,128)(2,1)}, bf16[480,384]{1,0:T(8,128)(2,1)S(1)}, u32[]{:S(2)}, u32[]{:S(2)}) collective-permute-start(bf16[480,384]{1,0:T(8,128)(2,1)} %get-tuple-element.106), channel_id=1, source_target_pairs={{0,8},{1,9},{2,10},{3,11},{4,12},{5,13},{6,14},{7,15},{8,0},{9,1},... | collective-permute-start | bytes 1105928 | tf_op jit(solution)/shard_map/ppermute | solution.py:668
  276.8 14.3 %collective-permute-start.20 = (bf16[208,768]{1,0:T(8,128)(2,1)}, bf16[208,768]{1,0:T(8,128)(2,1)S(1)}, u32[]{:S(2)}, u32[]{:S(2)}) collective-permute-start(bf16[208,768]{1,0:T(8,128)(2,1)} %get-tuple-element.119), channel_id=1, source_target_pairs={{0,2},{1,3},{2,0},{3,1},{4,6},{5,7},{6,4},{7,5},{8,10},{9,11},{10,... | collective-permute-start | bytes 958472 | tf_op jit(solution)/shard_map/ppermute | solution.py:668
  277.5 13.6 %collective-permute-start.16 = (bf16[240,384]{1,0:T(8,128)(2,1)}, bf16[240,384]{1,0:T(8,128)(2,1)S(1)}, u32[]{:S(2)}, u32[]{:S(2)}) collective-permute-start(bf16[240,384]{1,0:T(8,128)(2,1)} %get-tuple-element.113), channel_id=1, source_target_pairs={{0,4},{1,5},{2,6},{3,7},{4,0},{5,1},{6,2},{7,3},{8,12},{9,13},{10,... | collective-permute-start | bytes 552968 | tf_op jit(solution)/shard_map/ppermute | solution.py:668
  279.8 11.3 %collective-permute-start.18 = (bf16[48,768]{1,0:T(8,128)(2,1)}, bf16[48,768]{1,0:T(8,128)(2,1)S(1)}, u32[]{:S(2)}, u32[]{:S(2)}) collective-permute-start(bf16[48,768]{1,0:T(8,128)(2,1)} %get-tuple-element.116), channel_id=1, source_target_pairs={{0,8},{1,9},{2,10},{3,11},{4,12},{5,13},{6,14},{7,15},{8,0},{9,1},... | collective-permute-start | bytes 221192 | tf_op jit(solution)/shard_map/ppermute | solution.py:668
  294.5 16.5 %collective-permute-start.22 = (bf16[64,768]{1,0:T(8,128)(2,1)}, bf16[64,768]{1,0:T(8,128)(2,1)S(1)}, u32[]{:S(2)}, u32[]{:S(2)}) collective-permute-start(bf16[64,768]{1,0:T(8,128)(2,1)} %get-tuple-element.123), channel_id=1, source_target_pairs={{0,4},{1,5},{2,6},{3,7},{4,0},{5,1},{6,2},{7,3},{8,12},{9,13},{10,... | collective-permute-start | bytes 294920 | tf_op jit(solution)/shard_map/ppermute | solution.py:668
  297.0 13.9 %collective-permute-start.23 = (bf16[64,768]{1,0:T(8,128)(2,1)}, bf16[64,768]{1,0:T(8,128)(2,1)S(1)}, u32[]{:S(2)}, u32[]{:S(2)}) collective-permute-start(bf16[64,768]{1,0:T(8,128)(2,1)} %get-tuple-element.124), channel_id=1, source_target_pairs={{0,8},{1,9},{2,10},{3,11},{4,12},{5,13},{6,14},{7,15},{8,0},{9,1},... | collective-permute-start | bytes 294920 | tf_op jit(solution)/shard_map/ppermute | solution.py:668
  298.1 12.9 %collective-permute-start.24 = (bf16[64,768]{1,0:T(8,128)(2,1)}, bf16[64,768]{1,0:T(8,128)(2,1)S(1)}, u32[]{:S(2)}, u32[]{:S(2)}) collective-permute-start(bf16[64,768]{1,0:T(8,128)(2,1)} %get-tuple-element.125), channel_id=1, source_target_pairs={{0,12},{1,13},{2,14},{3,15},{4,8},{5,9},{6,10},{7,11},{8,4},{9,5},... | collective-permute-start | bytes 294920 | tf_op jit(solution)/shard_map/ppermute | solution.py:668
  298.5 9.9 %collective-permute-start.26 = (bf16[240,384]{1,0:T(8,128)(2,1)}, bf16[240,384]{1,0:T(8,128)(2,1)S(1)}, u32[]{:S(2)}, u32[]{:S(2)}) collective-permute-start(bf16[240,384]{1,0:T(8,128)(2,1)} %get-tuple-element.130), channel_id=1, source_target_pairs={{0,16},{16,0},{1,17},{17,1},{2,18},{18,2},{3,19},{19,3},{4,20},{20... | collective-permute-start | bytes 552968 | tf_op jit(solution)/shard_map/ppermute | solution.py:672
  299.9 16.8 %collective-permute-start.27 = (bf16[192,768]{1,0:T(8,128)(2,1)S(1)}, bf16[192,768]{1,0:T(8,128)(2,1)S(1)}, u32[]{:S(2)}, u32[]{:S(2)}) collective-permute-start(bf16[192,768]{1,0:T(8,128)(2,1)S(1)} %copy-done.3), channel_id=1, source_target_pairs={{0,16},{16,0},{1,17},{17,1},{2,18},{18,2},{3,19},{19,3},{4,20},{20... | collective-permute-start | bytes 884744 | tf_op jit(solution)/shard_map/ppermute | solution.py:672
  (39 other events, 169.0 us)
Sparse Core Ops, SparseCore 0:
  12.0 89.7 all-gather.2
  173.1 76.7 reduce-scatter.1
  253.3 60.2 all-gather.4

commit v4 on v3

--- a/solution.py
+++ b/solution.py
@@ -498,7 +498,12 @@
         segment = segment_of(places, lengths_ref, row)
         ids = lax.broadcasted_iota(jnp.int32, (SEGS, TB), 0)
         pooled = dot(jnp.where(segment == ids, 1.0, 0.0).astype(BF), out)
-        pool_ref[0] = jnp.where(i % per_row == 0, pooled, pool_ref[0] + pooled)
+        pooled = jnp.where(i % per_row == 0, pooled, pool_ref[0] + pooled)
+        counts = jnp.zeros((SEGS, 1), F32)
+        places = lax.broadcasted_iota(jnp.int32, (SEGS, 1), 0)
+        for s in range(SEGS):
+            counts = jnp.where(places == s, lengths_ref[row, s].astype(F32), counts)
+        pool_ref[0] = jnp.where(i % per_row == per_row - 1, pooled / counts, pooled)
         for c in range(0, FF, CH):
             du = (dot_t(dd, wd[c : c + CH, :]) * gp[:, c : c + CH]).astype(BF)
             du_ref[:, c : c + CH] = du
@@ -723,7 +728,7 @@
 
 
 class Chain:
-    def __init__(self, keep, send, lines=None, two_steps=False):
+    def __init__(self, keep, send, lines=None, grow=False, two_steps=False):
         self.columns = keep.shape[-1]
         flat = lambda x: x.reshape(-1, self.columns)
         halves = [(swap_replica,)] if keep.ndim == 5 else []
@@ -734,16 +739,18 @@
         self.owner_rows = keep.shape[-2]
         self.stay, self.away = flat(keep), [flat(send)]
         self.lines = None if lines is None else flat(lines)
-        self.rides = (len(fsdp) + 1 - len(halves)) if lines is not None else 0
+        self.ride = [False] * len(self.moves)
+        if lines is not None:
+            self.ride = [not grow] + [True] * (len(fsdp) - 1) + [not halves]
+        self.grow = grow
 
     def send(self):
         moves = self.moves.pop(0)
         self.received = [move(x) for move, x in zip(moves, self.away)]
         self.beside = []
-        if self.rides and len(self.received[0]) == len(self.stay):
+        self.arriving = self.ride.pop(0)
+        if self.arriving and len(self.received[0]) == len(self.stay):
             self.beside = [moves[0](self.lines)]
-        self.arriving = self.rides > 0
-        self.rides = max(self.rides - 1, 0)
 
 
 def add_all(chains, after=(), passing=()):
@@ -752,15 +759,17 @@
         n = c.stay.shape[0]
         parts = len(c.moves[0]) + 1 if n > c.owner_rows else 1
         part = n // parts
-        held = c.lines.shape[0] if c.arriving else 0
-        rides = held if c.rides else 0
-        ins = [c.stay] + c.received + (c.beside + [c.lines] if held else [])
+        lines = c.lines.shape[0] if c.arriving or c.ride[0] else 0
+        held = lines if c.arriving else 0
+        grown = held * (2 if c.grow else 1)
+        rides = (grown or lines) if c.ride[0] else 0
+        ins = [c.stay] + c.received + (c.beside + [c.lines] if lines else [])
         outs = [shaped((part, c.columns), BF)]
         sends = parts - 1 if parts > 1 else int(rides > 0)
         outs += [shaped((part + rides, c.columns), BF)] * sends
         if held:
-            outs.append(shaped((held, c.columns), BF))
-        plans.append((len(ins), len(outs), n, part, parts, sends, held, rides, len(c.received), len(c.beside)))
+            outs.append(shaped((grown, c.columns), BF))
+        plans.append((len(ins), len(outs), n, part, parts, sends, held, rides, len(c.received), len(c.beside), c.grow))
         operands += ins
         shapes += outs
 
@@ -768,7 +777,7 @@
 
     def kernel(*refs):
         sources, targets = refs[: len(operands)], refs[len(operands) + passed :]
-        for n_in, n_out, n, part, parts, sends, held, rides, arrivals, beside in plans:
+        for n_in, n_out, n, part, parts, sends, held, rides, arrivals, beside, grow in plans:
             ins, sources = sources[:n_in], sources[n_in:]
             outs, targets = targets[:n_out], targets[n_out:]
             received = ins[1 : 1 + arrivals]
@@ -787,14 +796,19 @@
                     others = [ins[1 + arrivals][...]]
                 else:
                     others = [r[n : n + held, :] for r in received]
-                total = mine.astype(F32)
-                for other in others:
-                    total = total + other.astype(F32)
-                lines = total.astype(BF)
+                if grow:
+                    lines = jnp.concatenate([mine, others[0]], axis=0)
+                else:
+                    total = mine.astype(F32)
+                    for other in others:
+                        total = total + other.astype(F32)
+                    lines = total.astype(BF)
                 outs[-1][...] = lines
-                if rides:
-                    for out in outs[1 : 1 + sends]:
-                        out[part:, :] = lines
+            elif rides:
+                lines = ins[-1][...]
+            if rides:
+                for out in outs[1 : 1 + sends]:
+                    out[part:, :] = lines
 
     results = list(
         call(
@@ -872,10 +886,9 @@
             for n in ("bias_out", "gain_one", "shift_one", "bias_down", "gain_two", "shift_two")
         ]
     )
-    (layer_out, nl, active, d_down, d_upper, d_first, d_att, sums, sums_up, pool) = middle(
+    (layer_out, nl, active, d_down, d_upper, d_first, d_att, sums, sums_up, pooled) = middle(
         lengths, tokens, mixed, weights, vec, vectors["bias_up"][None], cotangent
     )
-    pooled = pool / lengths.astype(F32)[:, :, None]
 
     terms_up = grad_up_out(where, nl, d_upper, mixed, d_att, direct)
     term_down = grad_down(active, d_down, after=(terms_up[0],))
@@ -885,17 +898,16 @@
         both = jnp.concatenate([sums_a, sums_b], axis=1)
         return jnp.concatenate([both, sums[3:], sums_up.reshape(-1, D), sums[:3]])
 
-    shard_down = scatter(term_down)
     attend_back = functools.partial(attend_backward, where, d_att, tokens, weights)
     if direct:
         chain_u = Chain(*terms_up, two_steps=True)
         chain_u.send()
-        add_all([chain_u], after=(term_down,))
+        (term_down,) = add_all([chain_u], passing=(term_down,))
+        shard_down = scatter(term_down)
         chain_u.send()
         dp_a, sums_a, *terms_a = attend_back((0, 1), kept, True, 2, after=(chain_u.away[0],))
-        chain_a = Chain(*terms_a)
-        chain_a.away[0], pooled = add_all([chain_u], after=(sums_a,), passing=(chain_a.away[0], pooled))
-        pooled_all = lax.all_gather(pooled, ("replica", "fsdp"), axis=0, tiled=True)
+        chain_a = Chain(*terms_a, pooled.astype(BF), grow=True, two_steps=True)
+        (chain_a.away[0],) = add_all([chain_u], after=(sums_a,), passing=(chain_a.away[0],))
         chain_u.send()
         chain_a.send()
         add_all([chain_a])
@@ -917,7 +929,7 @@
         chain_b.send()
         while chain_u.moves or chain_a.moves or chain_b.moves:
             moving = [c for c in (chain_u, chain_a, chain_b) if c.moves]
-            add_all(moving, after=(shard_down,) if len(moving) > 1 else (shard_down, pooled_all))
+            add_all(moving, after=(shard_down,))
             for c in moving:
                 c.send()
         halves_u = ordered(chain_u.stay, chain_u.received[0][: chain_u.owner_rows], replica)
@@ -926,6 +938,11 @@
             for h in halves_u
         ]
         grad_w_down = added(shard_down, swap_replica(shard_down))
+        lines = chain_a.lines.reshape((2,) * 4 + pooled.shape)
+        relative = jnp.stack([lines, swap(lines, 1)]).transpose(4, 2, 1, 3, 0, 5, 6, 7)
+        relative = relative.reshape((2, ranks) + pooled.shape)
+        pooled_all = relative[jnp.arange(2) ^ replica][:, me ^ jnp.arange(ranks)]
+        pooled_all = pooled_all.reshape((2 * ranks * pooled.shape[0],) + pooled.shape[1:]).astype(F32)
         h0, h1 = ordered(chain_a.stay, chain_a.received[0], replica)
         span = 3 * GW // 2
         halves_a = [
@@ -941,7 +958,7 @@
         input_grad = input_gradient(d_first, (dp_a, dp_b), w_first)
         pooled_all = lax.all_gather(pooled, ("replica", "fsdp"), axis=0, tiled=True)
         reduce = lambda x: lax.psum(scatter(x), "replica").astype(F32)
-        grad_w_down = lax.psum(shard_down, "replica").astype(F32)
+        grad_w_down = reduce(term_down)
         halves_u = [reduce(terms_up[0][h]) for h in range(2)]
         sum_a, sum_b = reduce(term_a), reduce(term_b)
         lines = lax.psum(small_lines(sums_a, sums_b), ("replica", "fsdp"))

time: 337 us -> 333 us (0.988)
  waiting for transfers between devices: 87.5 us -> 78.6 us
    ppermute x7, waiting for transfers between devices: 37 us -> 28.8 us  [swap_replica(): return lax.ppermute(x, 'replica', [(0, 1), (1, 0)])]
    unnamed x75 -> x72, local copies, waits for them, and re-layouts: 10.3 us -> 9.49 us
  transfers between devices with their start and end apart: 31 -> 30, of which waited for: 14 -> 13; matrix products, arithmetic and copies ran while one was open for 3% -> 5% of each run, Pallas kernels for 31% -> 33%
where the time goes in v4:
time: 333 us; the launch traced here: 328 us
  Pallas kernels  177 us (53%)
  waiting for transfers between devices  78.6 us (24%)
  starting transfers between devices  29.1 us (9%)
  local copies, waits for them, and re-layouts  20.8 us (6%)
  between operations  14.6 us (4%)
  other arithmetic  8.36 us (3%)
    pallas_call x16, Pallas kernels, call(): pl.pallas_call(run, grid_spec=pltpu.PrefetchScalarGridSpec(num_scalar_pre...  177 us
    ppermute x21, waiting for transfers between devices, swap(): return lax.ppermute(x, 'fsdp', [(i, i ^ mask) for i in range(RANKS)])  49.8 us
    ppermute x7, waiting for transfers between devices, swap_replica(): return lax.ppermute(x, 'replica', [(0, 1), (1, 0)])  28.8 us
    ppermute x21, starting transfers between devices, swap(): return lax.ppermute(x, 'fsdp', [(i, i ^ mask) for i in range(RANKS)])  20.6 us
    unnamed x72, local copies, waits for them, and re-layouts  9.49 us
    ppermute x7, starting transfers between devices, swap_replica(): return lax.ppermute(x, 'replica', [(0, 1), (1, 0)])  8.39 us
  transfers between devices with their start and end apart: 30, of which 13 were waited for; matrix products, arithmetic and copies ran while one was open for 5% of the time, Pallas kernels for 33%

profile of v4, /device:TPU:20, one launch (start us, length us, event | category | flops | bytes accessed | tf_op | source)
XLA Modules:
  0.0 328.3 jit_solution(14969307651339733507)
XLA Ops:
  9.0 2.8 shard_map.262
  12.5 3.5 %collective-permute-start.1 = (bf16[48,1280]{1,0:T(8,128)(2,1)}, bf16[48,1280]{1,0:T(8,128)(2,1)S(1)}, u32[]{:S(2)}, u32[]{:S(2)}) collective-permute-start(bf16[48,1280]{1,0:T(8,128)(2,1)} %get-tuple-element.77), channel_id=1, source_target_pairs={{0,8},{1,9},{2,10},{3,11},{4,12},{5,13},{6,14},{7,15},{8,0},{9,1},... | collective-permute-start | bytes 368648 | tf_op jit(solution)/shard_map/ppermute | solution.py:673
  16.0 8.6 %collective-permute-done.2 = bf16[48,1280]{1,0:T(8,128)(2,1)S(1)} collective-permute-done((bf16[48,1280]{1,0:T(8,128)(2,1)}, bf16[48,1280]{1,0:T(8,128)(2,1)S(1)}, u32[]{:S(2)}, u32[]{:S(2)}) %collective-permute-start.2) | collective-permute-done | bytes 122912 | tf_op jit(solution)/shard_map/ppermute | solution.py:673
  26.6 14.1 %collective-permute-done.3 = bf16[4,48,1280]{2,1,0:T(8,128)(2,1)S(1)} collective-permute-done((bf16[4,48,1280]{2,1,0:T(8,128)(2,1)S(1)}, bf16[4,48,1280]{2,1,0:T(8,128)(2,1)S(1)}, u32[]{:S(2)}, u32[]{:S(2)}) %collective-permute-start.3) | collective-permute-done | bytes 491552 | tf_op jit(solution)/shard_map/ppermute | solution.py:673
  42.3 21.2 %collective-permute-done.4.refs_2_ = bf16[2,4,48,1280]{3,2,1,0:T(8,128)(2,1)S(1)} collective-permute-done((bf16[2,4,48,1280]{3,2,1,0:T(8,128)(2,1)S(1)}, bf16[2,4,48,1280]{3,2,1,0:T(8,128)(2,1)S(1)}, u32[]{:S(2)}, u32[]{:S(2)}) %collective-permute-start.4) | collective-permute-done | bytes 983072 | tf_op jit(solution)/shard_map/ppermute | solution.py:677
  67.0 5.0 %shard_map.263.refs_2_.refs_3_.refs_4_ = bf16[768,2560]{1,0:T(8,128)(2,1)} custom-call(s32[2]{0:T(128)} %pad_add_fusion.refs_0_, bf16[2,4,48,1280]{3,2,1,0:T(8,128)(2,1)} %copy-done.3, bf16[2,4,48,1280]{3,2,1,0:T(8,128)(2,1)} %copy-done.15, bf16[2,4,48,1280]{3,2,1,0:T(8,128)(2,1)} %copy-done.16, bf16[2,4,48,1280]{3,2,1,0:T(8,128)(2,1)} %copy-done.17), custom_call_target="tpu_custom_call" | custom-call | flops 4600000000 | bytes 14400000 | tf_op jit(solution)/shard_map/pallas_call | solution.py:58
  75.9 27.8 %shard_map.264 = (bf16[1024,768]{1,0:T(8,128)(2,1)}, bf16[1024,768]{1,0:T(8,128)(2,1)}, bf16[1024,768]{1,0:T(8,128)(2,1)}, bf16[6,2,4,384,256]{4,3,2,1,0:T(8,128)(2,1)}, bf16[1024,768]{1,0:T(8,128)(2,1)}) custom-call(s32[2,8]{1,0:T(2,128)} %refs_0_.3, bf16[1024,768]{1,0:T(8,128)(2,1)} %refs_2_.5, bf16[768,2560]{1,0:T(8,128)(2,1)} %shard_map.263.refs_2_.refs_3_.refs_4_, ...), custom_call_target="tpu_custom_call" | custom-call | flops 32199999488 | bytes 100800000 | tf_op jit(solution)/shard_map/pallas_call | solution.py:58
  103.7 46.1 %shard_map.265 = (bf16[1024,768]{1,0:T(8,128)(2,1)}, bf16[1024,768]{1,0:T(8,128)(2,1)}, bf16[1024,3072]{1,0:T(8,128)(2,1)}, bf16[1024,768]{1,0:T(8,128)(2,1)}, b...) custom-call(s32[2,8]{1,0:T(2,128)} %refs_0_.3, ...), custom_call_target="tpu_custom_call" | custom-call | flops 51749998592 | bytes 162000000 | tf_op jit(solution)/shard_map/pallas_call | solution.py:58
  149.8 14.0 %shard_map.266 = (bf16[2,2,4,240,384]{4,3,2,1,0:T(8,128)(2,1)}, bf16[2,2,4,240,384]{4,3,2,1,0:T(8,128)(2,1)}) custom-call(s32[2]{0:T(128)} %pad_add_fusion.refs_0_, bf16[1024,768]{1,0:T(8,128)(2,1)} %get-tuple-element.87.refs_1_, bf16[1024,3072]{1,0:T(8,128)(2,1)} %get-tuple-element.88.refs_2_, bf16[1024,768]{1,0:T(8,128)(2,1)} %get-tuple-element.78.refs_2_.refs_3_, ...), custom_call_target="tpu_custom_call" | custom-call | flops 14949999616 | bytes 46800000 | tf_op jit(solution)/shard_map/pallas_call | solution.py:58
  164.0 9.2 %shard_map.267.refs_2_ = bf16[3072,768]{1,0:T(8,128)(2,1)} custom-call(bf16[1024,3072]{1,0:T(8,128)(2,1)} %get-tuple-element.91.refs_0_, bf16[1024,768]{1,0:T(8,128)(2,1)} %get-tuple-element.92.refs_1_, bf16[2,2,4,240,384]{4,3,2,1,0:T(8,128)(2,1)} %get-tuple-element.89.refs_2_), custom_call_target="tpu_custom_call" | custom-call | flops 10350000128 | bytes 32400000 | tf_op jit(solution)/shard_map/pallas_call | solution.py:58
  174.8 4.6 %shard_map.268 = (bf16[1920,384]{1,0:T(8,128)(2,1)}, bf16[1920,384]{1,0:T(8,128)(2,1)}, bf16[3072,768]{1,0:T(8,128)(2,1)}) custom-call(bf16[3840,384]{1,0:T(8,128)(2,1)} %bitcast.77, bf16[3840,384]{1,0:T(8,128)(2,1)} %copy-done, bf16[3072,768]{1,0:T(8,128)(2,1)} %shard_map.267.refs_2_), custom_call_target="tpu_custom_call", output_to_operand_aliasing={{2}: (2, {})} | custom-call | flops 2300000000 | bytes 7200000 | tf_op jit(solution)/shard_map/pallas_call | solution.py:58
  182.3 26.0 %shard_map.269 = (bf16[1024,1536]{1,0:T(8,128)(2,1)}, f32[2,512]{1,0:T(2,128)}, bf16[2,2,4,48,768]{4,3,2,1,0:T(8,128)(2,1)}, bf16[2,2,4,48,768]{4,3,2,1,0:T(8,128)(2,1)}) custom-call(s32[2]{0:T(128)} %pad_add_fusion.refs_0_, bf16[1024,768]{1,0:T(8,128)(2,1)} %get-tuple-element.82.refs_4_.refs_1_, bf16[1024,768]{1,0:T(8,128)(2,1)} %refs_2_.5, ...), custom_call_target="tpu_custom_call" | custom-call | flops 1150000000 | bytes 3600000 | tf_op jit(solution)/shard_map/pallas_call | solution.py:58
  208.3 7.1 %collective-permute-done.8.refs_1_ = bf16[1920,384]{1,0:T(8,128)(2,1)S(1)} collective-permute-done((bf16[1920,384]{1,0:T(8,128)(2,1)S(1)}, bf16[1920,384]{1,0:T(8,128)(2,1)S(1)}, u32[]{:S(2)}, u32[]{:S(2)}) %collective-permute-start.8) | collective-permute-done | bytes 1474592 | tf_op jit(solution)/shard_map/ppermute | solution.py:677
  216.5 3.1 shard_map.270
  223.7 2.9 shard_map.271
  228.1 15.9 %shard_map.272 = (bf16[1024,768]{1,0:T(8,128)(2,1)}, f32[2,256]{1,0:T(2,128)}, bf16[2,4,48,768]{3,2,1,0:T(8,128)(2,1)}, bf16[2,4,48,768]{3,2,1,0:T(8,128)(2,1)}) custom-call(s32[2]{0:T(128)} %pad_add_fusion.refs_0_, bf16[1024,768]{1,0:T(8,128)(2,1)} %get-tuple-element.82.refs_4_.refs_1_, bf16[1024,768]{1,0:T(8,128)(2,1)} %refs_2_.5, ...), custom_call_target="tpu_custom_call" | custom-call | flops 1150000000 | bytes 3600000 | tf_op jit(solution)/shard_map/pallas_call | solution.py:58
  246.4 2.9 shard_map.273
  250.8 9.1 %shard_map.274.refs_9_ = f32[1024,768]{1,0:T(8,128)} custom-call(f32[1024,768]{1,0:T(8,128)} %get-tuple-element.81.refs_0_, bf16[1024,1536]{1,0:T(8,128)(2,1)} %get-tuple-element.94.refs_1_, bf16[1024,768]{1,0:T(8,128)(2,1)} %get-tuple-element.102.refs_2_, bf16[768,2560]{1,0:T(8,128)(2,1)} %shard_map.263.refs_2_.refs_3_.refs_4_, ...), custom_call_target="tpu_custom_call" | custom-call | flops 10350000128 | bytes 32400000 | tf_op jit(solution)/shard_map/pallas_call | solution.py:58
  259.9 8.7 %collective-permute-done.12.refs_1_ = bf16[480,384]{1,0:T(8,128)(2,1)S(1)} collective-permute-done((bf16[480,384]{1,0:T(8,128)(2,1)}, bf16[480,384]{1,0:T(8,128)(2,1)S(1)}, u32[]{:S(2)}, u32[]{:S(2)}) %collective-permute-start.12) | collective-permute-done | bytes 368672 | tf_op jit(solution)/shard_map/ppermute | solution.py:673
  269.4 2.8 shard_map.275
  273.1 3.3 collective-permute-start.17
  276.4 9.0 %collective-permute-done.16.refs_1_ = bf16[240,384]{1,0:T(8,128)(2,1)S(1)} collective-permute-done((bf16[240,384]{1,0:T(8,128)(2,1)}, bf16[240,384]{1,0:T(8,128)(2,1)S(1)}, u32[]{:S(2)}, u32[]{:S(2)}) %collective-permute-start.16) | collective-permute-done | bytes 184352 | tf_op jit(solution)/shard_map/ppermute | solution.py:673
  290.1 3.6 %collective-permute-start.20 = (bf16[64,768]{1,0:T(8,128)(2,1)}, bf16[64,768]{1,0:T(8,128)(2,1)S(1)}, u32[]{:S(2)}, u32[]{:S(2)}) collective-permute-start(bf16[64,768]{1,0:T(8,128)(2,1)} %get-tuple-element.129), channel_id=1, source_target_pairs={{0,4},{1,5},{2,6},{3,7},{4,0},{5,1},{6,2},{7,3},{8,12},{9,13},{10,... | collective-permute-start | bytes 294920 | tf_op jit(solution)/shard_map/ppermute | solution.py:673
  295.3 2.8 collective-permute-start.19
  (195 shorter events, 59.5 us)
Async XLA Ops:
  7.2 96.5 %all-gather.2.cloned.1.call-start = ((), (), s32[]{:S(2)}) async-start(), calls=%async_computation.1 | async-start | bytes 11280384 | tf_op jit(solution)/shard_map/all_gather | solution.py:863
  11.9 273.9 %reduce-scatter.2.cloned.1.call-start = ((), (), s32[]{:S(2)}) async-start(), calls=%async_computation.2 | async-start | bytes 5013504 | tf_op jit(solution)/shard_map/reduce_scatter | solution.py:895
  12.0 12.6 %collective-permute-start.2 = (bf16[48,1280]{1,0:T(8,128)(2,1)}, bf16[48,1280]{1,0:T(8,128)(2,1)S(1)}, u32[]{:S(2)}, u32[]{:S(2)}) collective-permute-start(bf16[48,1280]{1,0:T(8,128)(2,1)} %get-tuple-element.77), channel_id=1, source_target_pairs={{0,12},{1,13},{2,14},{3,15},{4,8},{5,9},{6,10},{7,11},{8,4},{9,5},... | collective-permute-start | bytes 368648 | tf_op jit(solution)/shard_map/ppermute | solution.py:673
  12.5 12.6 %collective-permute-start.1 = (bf16[48,1280]{1,0:T(8,128)(2,1)}, bf16[48,1280]{1,0:T(8,128)(2,1)S(1)}, u32[]{:S(2)}, u32[]{:S(2)}) collective-permute-start(bf16[48,1280]{1,0:T(8,128)(2,1)} %get-tuple-element.77), channel_id=1, source_target_pairs={{0,8},{1,9},{2,10},{3,11},{4,12},{5,13},{6,14},{7,15},{8,0},{9,1},... | collective-permute-start | bytes 368648 | tf_op jit(solution)/shard_map/ppermute | solution.py:673
  16.0 9.2 %collective-permute-start = (bf16[48,1280]{1,0:T(8,128)(2,1)}, bf16[48,1280]{1,0:T(8,128)(2,1)S(1)}, u32[]{:S(2)}, u32[]{:S(2)}) collective-permute-start(bf16[48,1280]{1,0:T(8,128)(2,1)} %get-tuple-element.77), channel_id=1, source_target_pairs={{0,4},{1,5},{2,6},{3,7},{4,0},{5,1},{6,2},{7,3},{8,12},{9,13},{10,... | collective-permute-start | bytes 368648 | tf_op jit(solution)/shard_map/ppermute | solution.py:673
  26.1 14.6 %collective-permute-start.3 = (bf16[4,48,1280]{2,1,0:T(8,128)(2,1)S(1)}, bf16[4,48,1280]{2,1,0:T(8,128)(2,1)S(1)}, u32[]{:S(2)}, u32[]{:S(2)}) collective-permute-start(bf16[4,48,1280]{2,1,0:T(8,128)(2,1)S(1)} %get-tuple-element.152), channel_id=1, source_target_pairs={{0,2},{1,3},{2,0},{3,1},{4,6},{5,7},{6,4},{7,5},{8,10},{9,11},{10,... | collective-permute-start | bytes 1474568 | tf_op jit(solution)/shard_map/ppermute | solution.py:673
  40.8 22.7 %collective-permute-start.4 = (bf16[2,4,48,1280]{3,2,1,0:T(8,128)(2,1)S(1)}, bf16[2,4,48,1280]{3,2,1,0:T(8,128)(2,1)S(1)}, u32[]{:S(2)}, u32[]{:S(2)}) collective-permute-start(bf16[2,4,48,1280]{3,2,1,0:T(8,128)(2,1)S(1)} %pad_maximum_fusion.refs_1_), channel_id=1, source_target_pairs={{0,16},{16,0},{1,17},{17,1},{2,18},{18,2},{3,19},{19,3},{4,20},{20... | collective-permute-start | bytes 2949128 | tf_op jit(solution)/shard_map/ppermute | solution.py:677
  42.3 21.2 %collective-permute-start.5 = (bf16[2,4,48,1280]{3,2,1,0:T(8,128)(2,1)S(1)}, bf16[2,4,48,1280]{3,2,1,0:T(8,128)(2,1)S(1)}, u32[]{:S(2)}, u32[]{:S(2)}) collective-permute-start(bf16[2,4,48,1280]{3,2,1,0:T(8,128)(2,1)S(1)} %pad_maximum_fusion.refs_1_), channel_id=1, source_target_pairs={{0,1},{1,0},{2,3},{3,2},{4,5},{5,4},{6,7},{7,6},{8,9},{9,8},{10,11... | collective-permute-start | bytes 2949128 | tf_op jit(solution)/shard_map/ppermute | solution.py:673
  163.8 9.4 %collective-permute-start.7 = (bf16[3840,384]{1,0:T(8,128)(2,1)}, bf16[3840,384]{1,0:T(8,128)(2,1)S(1)}, u32[]{:S(2)}, u32[]{:S(2)}) collective-permute-start(bf16[3840,384]{1,0:T(8,128)(2,1)} %bitcast.98), channel_id=1, source_target_pairs={{0,1},{1,0},{2,3},{3,2},{4,5},{5,4},{6,7},{7,6},{8,9},{9,8},{10,11... | collective-permute-start | bytes 8847368 | tf_op jit(solution)/shard_map/ppermute | solution.py:673
  180.8 34.5 %collective-permute-start.8 = (bf16[1920,384]{1,0:T(8,128)(2,1)S(1)}, bf16[1920,384]{1,0:T(8,128)(2,1)S(1)}, u32[]{:S(2)}, u32[]{:S(2)}) collective-permute-start(bf16[1920,384]{1,0:T(8,128)(2,1)S(1)} %copy-done.2), channel_id=1, source_target_pairs={{0,16},{16,0},{1,17},{17,1},{2,18},{18,2},{3,19},{19,3},{4,20},{20... | collective-permute-start | bytes 4423688 | tf_op jit(solution)/shard_map/ppermute | solution.py:677
  220.2 25.1 %collective-permute-start.10 = (bf16[960,384]{1,0:T(8,128)(2,1)}, bf16[960,384]{1,0:T(8,128)(2,1)S(1)}, u32[]{:S(2)}, u32[]{:S(2)}) collective-permute-start(bf16[960,384]{1,0:T(8,128)(2,1)} %get-tuple-element.104), channel_id=1, source_target_pairs={{0,2},{1,3},{2,0},{3,1},{4,6},{5,7},{6,4},{7,5},{8,10},{9,11},{10,... | collective-permute-start | bytes 2211848 | tf_op jit(solution)/shard_map/ppermute | solution.py:673
  226.5 18.8 %collective-permute-start.11 = (bf16[400,768]{1,0:T(8,128)(2,1)}, bf16[400,768]{1,0:T(8,128)(2,1)S(1)}, u32[]{:S(2)}, u32[]{:S(2)}) collective-permute-start(bf16[400,768]{1,0:T(8,128)(2,1)} %get-tuple-element.101.refs_9_), channel_id=1, source_target_pairs={{0,16},{16,0},{1,17},{17,1},{2,18},{18,2},{3,19},{19,3},{4,20},{20... | collective-permute-start | bytes 1843208 | tf_op jit(solution)/shard_map/ppermute | solution.py:677
  244.8 15.1 %collective-permute-start.15 = (bf16[16,768]{1,0:T(8,128)(2,1)S(1)}, bf16[16,768]{1,0:T(8,128)(2,1)S(1)}, u32[]{:S(2)}, u32[]{:S(2)}) collective-permute-start(bf16[16,768]{1,0:T(8,128)(2,1)S(1)} %fusion.8.refs_8_), channel_id=1, source_target_pairs={{0,1},{1,0},{2,3},{3,2},{4,5},{5,4},{6,7},{7,6},{8,9},{9,8},{10,11... | collective-permute-start | bytes 73736 | tf_op jit(solution)/shard_map/ppermute | solution.py:673
  244.8 15.1 %collective-permute-start.14 = (bf16[384,768]{1,0:T(8,128)(2,1)}, bf16[384,768]{1,0:T(8,128)(2,1)S(1)}, u32[]{:S(2)}, u32[]{:S(2)}) collective-permute-start(bf16[384,768]{1,0:T(8,128)(2,1)} %bitcast.102), channel_id=1, source_target_pairs={{0,1},{1,0},{2,3},{3,2},{4,5},{5,4},{6,7},{7,6},{8,9},{9,8},{10,11... | collective-permute-start | bytes 1769480 | tf_op jit(solution)/shard_map/ppermute | solution.py:673
  249.3 10.6 %collective-permute-start.13 = (bf16[224,768]{1,0:T(8,128)(2,1)}, bf16[224,768]{1,0:T(8,128)(2,1)S(1)}, u32[]{:S(2)}, u32[]{:S(2)}) collective-permute-start(bf16[224,768]{1,0:T(8,128)(2,1)} %get-tuple-element.107.refs_4_), channel_id=1, source_target_pairs={{0,2},{1,3},{2,0},{3,1},{4,6},{5,7},{6,4},{7,5},{8,10},{9,11},{10,... | collective-permute-start | bytes 1032200 | tf_op jit(solution)/shard_map/ppermute | solution.py:673
  250.8 17.8 %collective-permute-start.12 = (bf16[480,384]{1,0:T(8,128)(2,1)}, bf16[480,384]{1,0:T(8,128)(2,1)S(1)}, u32[]{:S(2)}, u32[]{:S(2)}) collective-permute-start(bf16[480,384]{1,0:T(8,128)(2,1)} %get-tuple-element.109), channel_id=1, source_target_pairs={{0,8},{1,9},{2,10},{3,11},{4,12},{5,13},{6,14},{7,15},{8,0},{9,1},... | collective-permute-start | bytes 1105928 | tf_op jit(solution)/shard_map/ppermute | solution.py:673
  272.2 13.6 %collective-permute-start.18 = (bf16[208,768]{1,0:T(8,128)(2,1)}, bf16[208,768]{1,0:T(8,128)(2,1)S(1)}, u32[]{:S(2)}, u32[]{:S(2)}) collective-permute-start(bf16[208,768]{1,0:T(8,128)(2,1)} %get-tuple-element.122), channel_id=1, source_target_pairs={{0,2},{1,3},{2,0},{3,1},{4,6},{5,7},{6,4},{7,5},{8,10},{9,11},{10,... | collective-permute-start | bytes 958472 | tf_op jit(solution)/shard_map/ppermute | solution.py:673
  273.1 12.6 %collective-permute-start.17 = (bf16[160,768]{1,0:T(8,128)(2,1)}, bf16[160,768]{1,0:T(8,128)(2,1)S(1)}, u32[]{:S(2)}, u32[]{:S(2)}) collective-permute-start(bf16[160,768]{1,0:T(8,128)(2,1)} %get-tuple-element.119), channel_id=1, source_target_pairs={{0,8},{1,9},{2,10},{3,11},{4,12},{5,13},{6,14},{7,15},{8,0},{9,1},... | collective-permute-start | bytes 737288 | tf_op jit(solution)/shard_map/ppermute | solution.py:673
  276.4 9.0 %collective-permute-start.16 = (bf16[240,384]{1,0:T(8,128)(2,1)}, bf16[240,384]{1,0:T(8,128)(2,1)S(1)}, u32[]{:S(2)}, u32[]{:S(2)}) collective-permute-start(bf16[240,384]{1,0:T(8,128)(2,1)} %get-tuple-element.117), channel_id=1, source_target_pairs={{0,4},{1,5},{2,6},{3,7},{4,0},{5,1},{6,2},{7,3},{8,12},{9,13},{10,... | collective-permute-start | bytes 552968 | tf_op jit(solution)/shard_map/ppermute | solution.py:673
  288.9 9.2 %collective-permute-start.26 = (bf16[240,384]{1,0:T(8,128)(2,1)}, bf16[240,384]{1,0:T(8,128)(2,1)S(1)}, u32[]{:S(2)}, u32[]{:S(2)}) collective-permute-start(bf16[240,384]{1,0:T(8,128)(2,1)} %get-tuple-element.138), channel_id=1, source_target_pairs={{0,16},{16,0},{1,17},{17,1},{2,18},{18,2},{3,19},{19,3},{4,20},{20... | collective-permute-start | bytes 552968 | tf_op jit(solution)/shard_map/ppermute | solution.py:677
  290.1 11.4 %collective-permute-start.20 = (bf16[64,768]{1,0:T(8,128)(2,1)}, bf16[64,768]{1,0:T(8,128)(2,1)S(1)}, u32[]{:S(2)}, u32[]{:S(2)}) collective-permute-start(bf16[64,768]{1,0:T(8,128)(2,1)} %get-tuple-element.129), channel_id=1, source_target_pairs={{0,4},{1,5},{2,6},{3,7},{4,0},{5,1},{6,2},{7,3},{8,12},{9,13},{10,... | collective-permute-start | bytes 294920 | tf_op jit(solution)/shard_map/ppermute | solution.py:673
  293.7 10.3 %collective-permute-start.22 = (bf16[64,768]{1,0:T(8,128)(2,1)}, bf16[64,768]{1,0:T(8,128)(2,1)S(1)}, u32[]{:S(2)}, u32[]{:S(2)}) collective-permute-start(bf16[64,768]{1,0:T(8,128)(2,1)} %get-tuple-element.131), channel_id=1, source_target_pairs={{0,12},{1,13},{2,14},{3,15},{4,8},{5,9},{6,10},{7,11},{8,4},{9,5},... | collective-permute-start | bytes 294920 | tf_op jit(solution)/shard_map/ppermute | solution.py:673
  295.3 11.3 %collective-permute-start.19 = (bf16[176,768]{1,0:T(8,128)(2,1)}, bf16[176,768]{1,0:T(8,128)(2,1)S(1)}, u32[]{:S(2)}, u32[]{:S(2)}) collective-permute-start(bf16[176,768]{1,0:T(8,128)(2,1)} %get-tuple-element.126), channel_id=1, source_target_pairs={{0,4},{1,5},{2,6},{3,7},{4,0},{5,1},{6,2},{7,3},{8,12},{9,13},{10,... | collective-permute-start | bytes 811016 | tf_op jit(solution)/shard_map/ppermute | solution.py:673
  298.1 14.5 %collective-permute-start.27 = (bf16[192,768]{1,0:T(8,128)(2,1)}, bf16[192,768]{1,0:T(8,128)(2,1)S(1)}, u32[]{:S(2)}, u32[]{:S(2)}) collective-permute-start(bf16[192,768]{1,0:T(8,128)(2,1)} %reduce-scatter.2.cloned.1.call-done.refs_8_), channel_id=1, source_target_pairs={{0,16},{16,0},{1,17},{17,1},{2,18},{18,2},{3,19},{19,3},{4,20},{20... | collective-permute-start | bytes 884744 | tf_op jit(solution)/shard_map/ppermute | solution.py:677
  (37 other events, 151.0 us)
Sparse Core Ops, SparseCore 0:
  12.0 89.7 all-gather.1
  179.6 83.3 reduce-scatter.1

commit v5 on v4

--- a/solution.py
+++ b/solution.py
@@ -590,36 +590,86 @@
     )(d_first, *d_projected, w_qkv)
 
 
-def grad_down(active, d_down, after=()):
+def grad_down_out(active, d_down, mixed, d_att, ranks, direct, after=()):
     t = d_down.shape[0]
     n = 768
-
-    def kernel(a_ref, b_ref, out_ref):
-        out_ref[...] = t_dot(a_ref[...], b_ref[...]).astype(BF)
-
+    steps = FF // n
+    f, r = FF // ranks, D // ranks
+
+    def kernel(a_ref, dd_ref, m_ref, da_ref, *refs):
+        outs, (acc, sems) = refs[:-2], refs[-2:]
+        i = pl.program_id(0)
+        slot = i % 2
+
+        def copies_of(i, slot, last):
+            source = acc.at[slot]
+            if not direct:
+                target = outs[1] if last else outs[0].at[pl.ds(pl.multiple_of(i * n, n), n)]
+                return [pltpu.make_async_copy(source, target, sems.at[slot, 0])]
+            if last:
+                return [
+                    pltpu.make_async_copy(
+                        source.at[o * r : (o + 1) * r], outs[0].at[o, f : f + r], sems.at[slot, o]
+                    )
+                    for o in range(ranks)
+                ]
+            count = n // f
+            return [
+                pltpu.make_async_copy(
+                    source.at[k * f : (k + 1) * f], outs[0].at[i * count + k, :f], sems.at[slot, k]
+                )
+                for k in range(count)
+            ]
+
+        @pl.when(i >= 2)
+        def _():
+            wait_all(copies_of(i - 2, slot, False))
+
+        @pl.when(i < steps)
+        def _():
+            acc[slot] = t_dot(a_ref[...], dd_ref[...]).astype(BF)
+            start_all(copies_of(i, slot, False))
+
+        @pl.when(i == steps)
+        def _():
+            acc[slot] = t_dot(m_ref[...], da_ref[...]).astype(BF)
+            copies = copies_of(i, slot, True)
+            start_all(copies)
+            wait_all(copies_of(i - 1, (steps - 1) % 2, False))
+            wait_all(copies)
+
+    if direct:
+        out_shapes = [shaped((ranks, f + r, D), BF)]
+    else:
+        out_shapes = [shaped((FF, D), BF), shaped((D, D), BF)]
     return call(
         kernel,
-        (FF // n,),
-        [pl.BlockSpec((t, n), lambda i: (0, i)), whole((t, D))],
-        pl.BlockSpec((n, D), lambda i: (i, 0)),
-        shaped((FF, D), BF),
-        us=9,
+        (steps + 1,),
+        [
+            pl.BlockSpec((t, n), lambda i: (0, jnp.minimum(i, steps - 1))),
+            whole((t, D)),
+            whole((t, D)),
+            whole((t, D)),
+        ],
+        [ANY] * len(out_shapes),
+        out_shapes,
+        us=11,
+        scratch=[pltpu.VMEM((2, n, D), BF), pltpu.SemaphoreType.DMA((2, 16))],
         after=after,
-    )(active, d_down)
+    )(active, d_down, mixed, d_att)
 
 
 STRIP = 384
-STRIPS = (FF + D) // 2 // STRIP
-
-
-def grad_up_out(where, nl, d_upper, mixed, d_att, direct, after=()):
+STRIPS = FF // 2 // STRIP
+
+
+def grad_up(where, nl, d_upper, direct, after=()):
     t = nl.shape[0]
 
-    def kernel(where_ref, nl_ref, du_ref, m_ref, da_ref, *refs):
+    def kernel(where_ref, nl_ref, du_ref, *refs):
         outs, (acc, sems) = refs[:-2], refs[-2:]
         h = pl.program_id(0)
-        acc[h, :, : FF // 2] = t_dot(nl_ref[...], du_ref[...]).astype(BF)
-        acc[h, :, FF // 2 :] = t_dot(m_ref[...], da_ref[...]).astype(BF)
+        acc[h] = t_dot(nl_ref[...], du_ref[...]).astype(BF)
 
         def copies_of(h):
             if not direct:
@@ -647,26 +697,21 @@
     if direct:
         out_shapes = [shaped((2, 2, 4, STRIPS * D // RANKS, STRIP), BF)] * 2
     else:
-        out_shapes = [shaped((2, D, (FF + D) // 2), BF)]
+        out_shapes = [shaped((2, D, FF // 2), BF)]
     return call(
         kernel,
         (2,),
-        [
-            whole((t, D)),
-            pl.BlockSpec((t, FF // 2), lambda h, *_: (0, h)),
-            whole((t, D)),
-            pl.BlockSpec((t, D // 2), lambda h, *_: (0, h)),
-        ],
+        [whole((t, D)), pl.BlockSpec((t, FF // 2), lambda h, *_: (0, h))],
         [ANY] * len(out_shapes),
         out_shapes,
-        us=13,
+        us=11,
         scratch=[
-            pltpu.VMEM((2, D, (FF + D) // 2), BF),
+            pltpu.VMEM((2, D, FF // 2), BF),
             pltpu.SemaphoreType.DMA((2, RANKS * STRIPS)),
         ],
         prefetch=1,
         after=after,
-    )(where, nl, d_upper, mixed, d_att)
+    )(where, nl, d_upper)
 
 
 def swap(x, mask):
@@ -890,8 +935,8 @@
         lengths, tokens, mixed, weights, vec, vectors["bias_up"][None], cotangent
     )
 
-    terms_up = grad_up_out(where, nl, d_upper, mixed, d_att, direct)
-    term_down = grad_down(active, d_down, after=(terms_up[0],))
+    terms_down = grad_down_out(active, d_down, mixed, d_att, ranks, direct)
+    terms_up = grad_up(where, nl, d_upper, direct, after=(terms_down[0],))
     scatter = lambda x: lax.psum_scatter(x, "fsdp", scatter_dimension=0, tiled=True)
 
     def small_lines(sums_a, sums_b):
@@ -902,8 +947,9 @@
     if direct:
         chain_u = Chain(*terms_up, two_steps=True)
         chain_u.send()
-        (term_down,) = add_all([chain_u], passing=(term_down,))
-        shard_down = scatter(term_down)
+        add_all([chain_u])
+        shard_down = scatter(terms_down[0].reshape(-1, D))
+        shard_other = swap_replica(shard_down)
         chain_u.send()
         dp_a, sums_a, *terms_a = attend_back((0, 1), kept, True, 2, after=(chain_u.away[0],))
         chain_a = Chain(*terms_a, pooled.astype(BF), grow=True, two_steps=True)
@@ -929,7 +975,8 @@
         chain_b.send()
         while chain_u.moves or chain_a.moves or chain_b.moves:
             moving = [c for c in (chain_u, chain_a, chain_b) if c.moves]
-            add_all(moving, after=(shard_down,))
+            last = all(len(c.moves) == 1 for c in moving)
+            add_all(moving, after=(shard_other,) if last else ())
             for c in moving:
                 c.send()
         halves_u = ordered(chain_u.stay, chain_u.received[0][: chain_u.owner_rows], replica)
@@ -937,7 +984,8 @@
             h.reshape(STRIPS, -1, STRIP).transpose(1, 0, 2).reshape(-1, STRIPS * STRIP)
             for h in halves_u
         ]
-        grad_w_down = added(shard_down, swap_replica(shard_down))
+        both = added(shard_down, shard_other)
+        grad_w_down, grad_w_out = both[: FF // ranks], both[FF // ranks :]
         lines = chain_a.lines.reshape((2,) * 4 + pooled.shape)
         relative = jnp.stack([lines, swap(lines, 1)]).transpose(4, 2, 1, 3, 0, 5, 6, 7)
         relative = relative.reshape((2, ranks) + pooled.shape)
@@ -958,13 +1006,12 @@
         input_grad = input_gradient(d_first, (dp_a, dp_b), w_first)
         pooled_all = lax.all_gather(pooled, ("replica", "fsdp"), axis=0, tiled=True)
         reduce = lambda x: lax.psum(scatter(x), "replica").astype(F32)
-        grad_w_down = reduce(term_down)
+        grad_w_down, grad_w_out = reduce(terms_down[0]), reduce(terms_down[1])
         halves_u = [reduce(terms_up[0][h]) for h in range(2)]
         sum_a, sum_b = reduce(term_a), reduce(term_b)
         lines = lax.psum(small_lines(sums_a, sums_b), ("replica", "fsdp"))
         parts = [sum_a[:, :D], sum_a[:, D:], sum_b]
-    grad_w_up = jnp.concatenate([h[:, : FF // 2] for h in halves_u], axis=1).astype(F32)
-    grad_w_out = jnp.concatenate([h[:, FF // 2 :] for h in halves_u], axis=1).astype(F32)
+    grad_w_up = jnp.concatenate(halves_u, axis=1).astype(F32)
     grad_w_qkv = jnp.concatenate(
         [p[:, i * GW : (i + 1) * GW] for i in range(3) for p in parts], axis=1
     )

time: 333 us -> 325 us (0.976)
  waiting for transfers between devices: 78.6 us -> 73.5 us
    unnamed x72 -> x76, local copies, waits for them, and re-layouts: 9.49 us -> 7.98 us
  transfers between devices with their start and end apart: 30 -> 30, of which waited for: 13 -> 15; matrix products, arithmetic and copies ran while one was open for 5% -> 4% of each run, Pallas kernels for 33% -> 35%
where the time goes in v5:
time: 325 us; the launch traced here: 321 us
  Pallas kernels  176 us (54%)
  waiting for transfers between devices  73.5 us (23%)
  starting transfers between devices  29.9 us (9%)
  local copies, waits for them, and re-layouts  19.7 us (6%)
  between operations  14.7 us (5%)
  other arithmetic  6.82 us (2%)
    pallas_call x16, Pallas kernels, call(): pl.pallas_call(run, grid_spec=pltpu.PrefetchScalarGridSpec(num_scalar_pre...  176 us
    ppermute x21, waiting for transfers between devices, swap(): return lax.ppermute(x, 'fsdp', [(i, i ^ mask) for i in range(RANKS)])  47.8 us
    ppermute x7, waiting for transfers between devices, swap_replica(): return lax.ppermute(x, 'replica', [(0, 1), (1, 0)])  25.6 us
    ppermute x21, starting transfers between devices, swap(): return lax.ppermute(x, 'fsdp', [(i, i ^ mask) for i in range(RANKS)])  21.3 us
    ppermute x7, starting transfers between devices, swap_replica(): return lax.ppermute(x, 'replica', [(0, 1), (1, 0)])  8.59 us
    unnamed x76, local copies, waits for them, and re-layouts  7.98 us
  transfers between devices with their start and end apart: 30, of which 15 were waited for; matrix products, arithmetic and copies ran while one was open for 4% of the time, Pallas kernels for 35%

profile of v5, /device:TPU:20, one launch (start us, length us, event | category | flops | bytes accessed | tf_op | source)
XLA Modules:
  0.0 320.6 jit_solution(205040488436798190)
XLA Ops:
  9.0 2.9 shard_map.262
  12.5 3.5 %collective-permute-start.1 = (bf16[48,1280]{1,0:T(8,128)(2,1)}, bf16[48,1280]{1,0:T(8,128)(2,1)S(1)}, u32[]{:S(2)}, u32[]{:S(2)}) collective-permute-start(bf16[48,1280]{1,0:T(8,128)(2,1)} %get-tuple-element.76), channel_id=1, source_target_pairs={{0,8},{1,9},{2,10},{3,11},{4,12},{5,13},{6,14},{7,15},{8,0},{9,1},... | collective-permute-start | bytes 368648 | tf_op jit(solution)/shard_map/ppermute | solution.py:718
  16.0 8.6 %collective-permute-done.2 = bf16[48,1280]{1,0:T(8,128)(2,1)S(1)} collective-permute-done((bf16[48,1280]{1,0:T(8,128)(2,1)}, bf16[48,1280]{1,0:T(8,128)(2,1)S(1)}, u32[]{:S(2)}, u32[]{:S(2)}) %collective-permute-start.2) | collective-permute-done | bytes 122912 | tf_op jit(solution)/shard_map/ppermute | solution.py:718
  26.6 14.1 %collective-permute-done.3 = bf16[4,48,1280]{2,1,0:T(8,128)(2,1)S(1)} collective-permute-done((bf16[4,48,1280]{2,1,0:T(8,128)(2,1)S(1)}, bf16[4,48,1280]{2,1,0:T(8,128)(2,1)S(1)}, u32[]{:S(2)}, u32[]{:S(2)}) %collective-permute-start.3) | collective-permute-done | bytes 491552 | tf_op jit(solution)/shard_map/ppermute | solution.py:718
  42.3 21.2 %collective-permute-done.4.refs_2_ = bf16[2,4,48,1280]{3,2,1,0:T(8,128)(2,1)S(1)} collective-permute-done((bf16[2,4,48,1280]{3,2,1,0:T(8,128)(2,1)S(1)}, bf16[2,4,48,1280]{3,2,1,0:T(8,128)(2,1)S(1)}, u32[]{:S(2)}, u32[]{:S(2)}) %collective-permute-start.4) | collective-permute-done | bytes 983072 | tf_op jit(solution)/shard_map/ppermute | solution.py:722
  67.0 5.0 %shard_map.263.refs_2_.refs_3_.refs_4_ = bf16[768,2560]{1,0:T(8,128)(2,1)} custom-call(s32[2]{0:T(128)} %pad_add_fusion.refs_0_, bf16[2,4,48,1280]{3,2,1,0:T(8,128)(2,1)} %copy-done.1, bf16[2,4,48,1280]{3,2,1,0:T(8,128)(2,1)} %copy-done.16, bf16[2,4,48,1280]{3,2,1,0:T(8,128)(2,1)} %copy-done.17, bf16[2,4,48,1280]{3,2,1,0:T(8,128)(2,1)} %copy-done.18), custom_call_target="tpu_custom_call" | custom-call | flops 4600000000 | bytes 14400000 | tf_op jit(solution)/shard_map/pallas_call | solution.py:58
  75.9 27.8 %shard_map.264 = (bf16[1024,768]{1,0:T(8,128)(2,1)}, bf16[1024,768]{1,0:T(8,128)(2,1)}, bf16[1024,768]{1,0:T(8,128)(2,1)}, bf16[6,2,4,384,256]{4,3,2,1,0:T(8,128)(2,1)}, bf16[1024,768]{1,0:T(8,128)(2,1)}) custom-call(s32[2,8]{1,0:T(2,128)} %refs_0_.3, bf16[1024,768]{1,0:T(8,128)(2,1)} %refs_2_.5, bf16[768,2560]{1,0:T(8,128)(2,1)} %shard_map.263.refs_2_.refs_3_.refs_4_, ...), custom_call_target="tpu_custom_call" | custom-call | flops 32199999488 | bytes 100800000 | tf_op jit(solution)/shard_map/pallas_call | solution.py:58
  103.7 46.0 %shard_map.265 = (bf16[1024,768]{1,0:T(8,128)(2,1)}, bf16[1024,768]{1,0:T(8,128)(2,1)}, bf16[1024,3072]{1,0:T(8,128)(2,1)}, bf16[1024,768]{1,0:T(8,128)(2,1)}, b...) custom-call(s32[2,8]{1,0:T(2,128)} %refs_0_.3, ...), custom_call_target="tpu_custom_call" | custom-call | flops 51749998592 | bytes 162000000 | tf_op jit(solution)/shard_map/pallas_call | solution.py:58
  149.8 12.1 %shard_map.266.refs_3_ = bf16[16,240,768]{2,1,0:T(8,128)(2,1)} custom-call(bf16[1024,3072]{1,0:T(8,128)(2,1)} %get-tuple-element.88.refs_0_, bf16[1024,768]{1,0:T(8,128)(2,1)} %get-tuple-element.89.refs_1_, bf16[1024,768]{1,0:T(8,128)(2,1)} %get-tuple-element.77.refs_2_.refs_3_, bf16[1024,768]{1,0:T(8,128)(2,1)} %get-tuple-element.81.refs_3_.refs_1_), custom_call_target="tpu_custom_call" | custom-call | flops 12650000384 | bytes 39600000 | tf_op jit(solution)/shard_map/pallas_call | solution.py:58
  161.9 11.0 %shard_map.267 = (bf16[2,2,4,192,384]{4,3,2,1,0:T(8,128)(2,1)}, bf16[2,2,4,192,384]{4,3,2,1,0:T(8,128)(2,1)}) custom-call(s32[2]{0:T(128)} %pad_add_fusion.refs_0_, bf16[1024,768]{1,0:T(8,128)(2,1)} %get-tuple-element.86.refs_1_, bf16[1024,3072]{1,0:T(8,128)(2,1)} %get-tuple-element.87.refs_2_, bf16[16,240,768]{2,1,0:T(8,128)(2,1)} %shard_map.266.refs_3_), custom_call_target="tpu_custom_call" | custom-call | flops 12650000384 | bytes 39600000 | tf_op jit(solution)/shard_map/pallas_call | solution.py:58
  173.1 4.6 %collective-permute-done.7.refs_1_ = bf16[3072,384]{1,0:T(8,128)(2,1)S(1)} collective-permute-done((bf16[3072,384]{1,0:T(8,128)(2,1)}, bf16[3072,384]{1,0:T(8,128)(2,1)S(1)}, u32[]{:S(2)}, u32[]{:S(2)}) %collective-permute-start.7) | collective-permute-done | bytes 2359328 | tf_op jit(solution)/shard_map/ppermute | solution.py:718
  179.1 4.4 %shard_map.268 = (bf16[1536,384]{1,0:T(8,128)(2,1)}, bf16[1536,384]{1,0:T(8,128)(2,1)}) custom-call(bf16[3072,384]{1,0:T(8,128)(2,1)} %bitcast.107, bf16[3072,384]{1,0:T(8,128)(2,1)} %copy-done.13), custom_call_target="tpu_custom_call" | custom-call | flops 2300000000 | bytes 7200000 | tf_op jit(solution)/shard_map/pallas_call | solution.py:58
  185.0 25.8 %shard_map.269 = (bf16[1024,1536]{1,0:T(8,128)(2,1)}, f32[2,512]{1,0:T(2,128)}, bf16[2,2,4,48,768]{4,3,2,1,0:T(8,128)(2,1)}, bf16[2,2,4,48,768]{4,3,2,1,0:T(8,128)(2,1)}) custom-call(s32[2]{0:T(128)} %pad_add_fusion.refs_0_, bf16[1024,768]{1,0:T(8,128)(2,1)} %get-tuple-element.81.refs_3_.refs_1_, bf16[1024,768]{1,0:T(8,128)(2,1)} %refs_2_.5, ...), custom_call_target="tpu_custom_call" | custom-call | flops 1150000000 | bytes 3600000 | tf_op jit(solution)/shard_map/pallas_call | solution.py:58
  212.9 3.0 shard_map.270
  220.0 2.9 shard_map.271
  226.1 16.0 %shard_map.272 = (bf16[1024,768]{1,0:T(8,128)(2,1)}, f32[2,256]{1,0:T(2,128)}, bf16[2,4,48,768]{3,2,1,0:T(8,128)(2,1)}, bf16[2,4,48,768]{3,2,1,0:T(8,128)(2,1)}) custom-call(s32[2]{0:T(128)} %pad_add_fusion.refs_0_, bf16[1024,768]{1,0:T(8,128)(2,1)} %get-tuple-element.81.refs_3_.refs_1_, bf16[1024,768]{1,0:T(8,128)(2,1)} %refs_2_.5, ...), custom_call_target="tpu_custom_call" | custom-call | flops 1150000000 | bytes 3600000 | tf_op jit(solution)/shard_map/pallas_call | solution.py:58
  248.9 9.0 %shard_map.274.refs_9_ = f32[1024,768]{1,0:T(8,128)} custom-call(f32[1024,768]{1,0:T(8,128)} %get-tuple-element.80.refs_0_, bf16[1024,1536]{1,0:T(8,128)(2,1)} %get-tuple-element.93.refs_1_, bf16[1024,768]{1,0:T(8,128)(2,1)} %get-tuple-element.101.refs_2_, bf16[768,2560]{1,0:T(8,128)(2,1)} %shard_map.263.refs_2_.refs_3_.refs_4_, ...), custom_call_target="tpu_custom_call" | custom-call | flops 10350000128 | bytes 32400000 | tf_op jit(solution)/shard_map/pallas_call | solution.py:58
  260.3 2.8 shard_map.275
  264.4 3.3 %collective-permute-start.17 = (bf16[160,768]{1,0:T(8,128)(2,1)}, bf16[160,768]{1,0:T(8,128)(2,1)S(1)}, u32[]{:S(2)}, u32[]{:S(2)}) collective-permute-start(bf16[160,768]{1,0:T(8,128)(2,1)} %get-tuple-element.118), channel_id=1, source_target_pairs={{0,8},{1,9},{2,10},{3,11},{4,12},{5,13},{6,14},{7,15},{8,0},{9,1},... | collective-permute-start | bytes 737288 | tf_op jit(solution)/shard_map/ppermute | solution.py:718
  267.7 6.6 %collective-permute-done.16.refs_1_ = bf16[192,384]{1,0:T(8,128)(2,1)S(1)} collective-permute-done((bf16[192,384]{1,0:T(8,128)(2,1)}, bf16[192,384]{1,0:T(8,128)(2,1)S(1)}, u32[]{:S(2)}, u32[]{:S(2)}) %collective-permute-start.16) | collective-permute-done | bytes 147488 | tf_op jit(solution)/shard_map/ppermute | solution.py:718
  279.7 3.6 %collective-permute-start.20 = (bf16[64,768]{1,0:T(8,128)(2,1)}, bf16[64,768]{1,0:T(8,128)(2,1)S(1)}, u32[]{:S(2)}, u32[]{:S(2)}) collective-permute-start(bf16[64,768]{1,0:T(8,128)(2,1)} %get-tuple-element.127), channel_id=1, source_target_pairs={{0,4},{1,5},{2,6},{3,7},{4,0},{5,1},{6,2},{7,3},{8,12},{9,13},{10,... | collective-permute-start | bytes 294920 | tf_op jit(solution)/shard_map/ppermute | solution.py:718
  284.9 2.8 collective-permute-start.19
  292.8 3.4 %collective-permute-done.19.refs_1_ = bf16[176,768]{1,0:T(8,128)(2,1)S(1)} collective-permute-done((bf16[176,768]{1,0:T(8,128)(2,1)}, bf16[176,768]{1,0:T(8,128)(2,1)S(1)}, u32[]{:S(2)}, u32[]{:S(2)}) %collective-permute-start.19) | collective-permute-done | bytes 270368 | tf_op jit(solution)/shard_map/ppermute | solution.py:718
  304.1 3.3 %collective-permute-done.26 = bf16[64,768]{1,0:T(8,128)(2,1)S(1)} collective-permute-done((bf16[64,768]{1,0:T(8,128)(2,1)S(1)}, bf16[64,768]{1,0:T(8,128)(2,1)S(1)}, u32[]{:S(2)}, u32[]{:S(2)}) %collective-permute-start.26) | collective-permute-done | bytes 98336 | tf_op jit(solution)/shard_map/ppermute | solution.py:722
  (198 shorter events, 62.3 us)
Async XLA Ops:
  7.2 96.5 %all-gather.2.cloned.1.call-start = ((), (), s32[]{:S(2)}) async-start(), calls=%async_computation.1 | async-start | bytes 11280384 | tf_op jit(solution)/shard_map/all_gather | solution.py:908
  11.9 275.8 %reduce-scatter.2.cloned.1.call-start = ((), (), s32[]{:S(2)}) async-start(), calls=%async_computation.2 | async-start | bytes 6266880 | tf_op jit(solution)/shard_map/reduce_scatter | solution.py:940
  12.0 12.6 %collective-permute-start.2 = (bf16[48,1280]{1,0:T(8,128)(2,1)}, bf16[48,1280]{1,0:T(8,128)(2,1)S(1)}, u32[]{:S(2)}, u32[]{:S(2)}) collective-permute-start(bf16[48,1280]{1,0:T(8,128)(2,1)} %get-tuple-element.76), channel_id=1, source_target_pairs={{0,12},{1,13},{2,14},{3,15},{4,8},{5,9},{6,10},{7,11},{8,4},{9,5},... | collective-permute-start | bytes 368648 | tf_op jit(solution)/shard_map/ppermute | solution.py:718
  12.5 12.6 %collective-permute-start.1 = (bf16[48,1280]{1,0:T(8,128)(2,1)}, bf16[48,1280]{1,0:T(8,128)(2,1)S(1)}, u32[]{:S(2)}, u32[]{:S(2)}) collective-permute-start(bf16[48,1280]{1,0:T(8,128)(2,1)} %get-tuple-element.76), channel_id=1, source_target_pairs={{0,8},{1,9},{2,10},{3,11},{4,12},{5,13},{6,14},{7,15},{8,0},{9,1},... | collective-permute-start | bytes 368648 | tf_op jit(solution)/shard_map/ppermute | solution.py:718
  16.0 9.2 %collective-permute-start = (bf16[48,1280]{1,0:T(8,128)(2,1)}, bf16[48,1280]{1,0:T(8,128)(2,1)S(1)}, u32[]{:S(2)}, u32[]{:S(2)}) collective-permute-start(bf16[48,1280]{1,0:T(8,128)(2,1)} %get-tuple-element.76), channel_id=1, source_target_pairs={{0,4},{1,5},{2,6},{3,7},{4,0},{5,1},{6,2},{7,3},{8,12},{9,13},{10,... | collective-permute-start | bytes 368648 | tf_op jit(solution)/shard_map/ppermute | solution.py:718
  26.1 14.6 %collective-permute-start.3 = (bf16[4,48,1280]{2,1,0:T(8,128)(2,1)S(1)}, bf16[4,48,1280]{2,1,0:T(8,128)(2,1)S(1)}, u32[]{:S(2)}, u32[]{:S(2)}) collective-permute-start(bf16[4,48,1280]{2,1,0:T(8,128)(2,1)S(1)} %get-tuple-element.150), channel_id=1, source_target_pairs={{0,2},{1,3},{2,0},{3,1},{4,6},{5,7},{6,4},{7,5},{8,10},{9,11},{10,... | collective-permute-start | bytes 1474568 | tf_op jit(solution)/shard_map/ppermute | solution.py:718
  40.8 22.7 %collective-permute-start.4 = (bf16[2,4,48,1280]{3,2,1,0:T(8,128)(2,1)S(1)}, bf16[2,4,48,1280]{3,2,1,0:T(8,128)(2,1)S(1)}, u32[]{:S(2)}, u32[]{:S(2)}) collective-permute-start(bf16[2,4,48,1280]{3,2,1,0:T(8,128)(2,1)S(1)} %pad_maximum_fusion.refs_1_), channel_id=1, source_target_pairs={{0,16},{16,0},{1,17},{17,1},{2,18},{18,2},{3,19},{19,3},{4,20},{20... | collective-permute-start | bytes 2949128 | tf_op jit(solution)/shard_map/ppermute | solution.py:722
  42.3 21.2 %collective-permute-start.5 = (bf16[2,4,48,1280]{3,2,1,0:T(8,128)(2,1)S(1)}, bf16[2,4,48,1280]{3,2,1,0:T(8,128)(2,1)S(1)}, u32[]{:S(2)}, u32[]{:S(2)}) collective-permute-start(bf16[2,4,48,1280]{3,2,1,0:T(8,128)(2,1)S(1)} %pad_maximum_fusion.refs_1_), channel_id=1, source_target_pairs={{0,1},{1,0},{2,3},{3,2},{4,5},{5,4},{6,7},{7,6},{8,9},{9,8},{10,11... | collective-permute-start | bytes 2949128 | tf_op jit(solution)/shard_map/ppermute | solution.py:718
  183.5 28.4 %collective-permute-start.8 = (bf16[1536,384]{1,0:T(8,128)(2,1)}, bf16[1536,384]{1,0:T(8,128)(2,1)S(1)}, u32[]{:S(2)}, u32[]{:S(2)}) collective-permute-start(bf16[1536,384]{1,0:T(8,128)(2,1)} %get-tuple-element.92.refs_9_), channel_id=1, source_target_pairs={{0,16},{16,0},{1,17},{17,1},{2,18},{18,2},{3,19},{19,3},{4,20},{20... | collective-permute-start | bytes 3538952 | tf_op jit(solution)/shard_map/ppermute | solution.py:722
  222.9 20.5 %collective-permute-start.11 = (bf16[400,768]{1,0:T(8,128)(2,1)}, bf16[400,768]{1,0:T(8,128)(2,1)S(1)}, u32[]{:S(2)}, u32[]{:S(2)}) collective-permute-start(bf16[400,768]{1,0:T(8,128)(2,1)} %get-tuple-element.100.refs_9_), channel_id=1, source_target_pairs={{0,16},{16,0},{1,17},{17,1},{2,18},{18,2},{3,19},{19,3},{4,20},{20... | collective-permute-start | bytes 1843208 | tf_op jit(solution)/shard_map/ppermute | solution.py:722
  224.4 19.0 %collective-permute-start.10 = (bf16[768,384]{1,0:T(8,128)(2,1)S(1)}, bf16[768,384]{1,0:T(8,128)(2,1)S(1)}, u32[]{:S(2)}, u32[]{:S(2)}) collective-permute-start(bf16[768,384]{1,0:T(8,128)(2,1)S(1)} %copy-done.20), channel_id=1, source_target_pairs={{0,2},{1,3},{2,0},{3,1},{4,6},{5,7},{6,4},{7,5},{8,10},{9,11},{10,... | collective-permute-start | bytes 1769480 | tf_op jit(solution)/shard_map/ppermute | solution.py:718
  242.8 15.2 %collective-permute-start.15 = (bf16[16,768]{1,0:T(8,128)(2,1)S(1)}, bf16[16,768]{1,0:T(8,128)(2,1)S(1)}, u32[]{:S(2)}, u32[]{:S(2)}) collective-permute-start(bf16[16,768]{1,0:T(8,128)(2,1)S(1)} %fusion.8.refs_8_), channel_id=1, source_target_pairs={{0,1},{1,0},{2,3},{3,2},{4,5},{5,4},{6,7},{7,6},{8,9},{9,8},{10,11... | collective-permute-start | bytes 73736 | tf_op jit(solution)/shard_map/ppermute | solution.py:718
  242.8 15.1 %collective-permute-start.14 = (bf16[384,768]{1,0:T(8,128)(2,1)}, bf16[384,768]{1,0:T(8,128)(2,1)S(1)}, u32[]{:S(2)}, u32[]{:S(2)}) collective-permute-start(bf16[384,768]{1,0:T(8,128)(2,1)} %bitcast.99), channel_id=1, source_target_pairs={{0,1},{1,0},{2,3},{3,2},{4,5},{5,4},{6,7},{7,6},{8,9},{9,8},{10,11... | collective-permute-start | bytes 1769480 | tf_op jit(solution)/shard_map/ppermute | solution.py:718
  247.2 12.3 %collective-permute-start.12 = (bf16[384,384]{1,0:T(8,128)(2,1)}, bf16[384,384]{1,0:T(8,128)(2,1)S(1)}, u32[]{:S(2)}, u32[]{:S(2)}) collective-permute-start(bf16[384,384]{1,0:T(8,128)(2,1)} %get-tuple-element.108), channel_id=1, source_target_pairs={{0,8},{1,9},{2,10},{3,11},{4,12},{5,13},{6,14},{7,15},{8,0},{9,1},... | collective-permute-start | bytes 884744 | tf_op jit(solution)/shard_map/ppermute | solution.py:718
  247.2 12.3 %collective-permute-start.13 = (bf16[224,768]{1,0:T(8,128)(2,1)}, bf16[224,768]{1,0:T(8,128)(2,1)S(1)}, u32[]{:S(2)}, u32[]{:S(2)}) collective-permute-start(bf16[224,768]{1,0:T(8,128)(2,1)} %get-tuple-element.106.refs_4_), channel_id=1, source_target_pairs={{0,2},{1,3},{2,0},{3,1},{4,6},{5,7},{6,4},{7,5},{8,10},{9,11},{10,... | collective-permute-start | bytes 1032200 | tf_op jit(solution)/shard_map/ppermute | solution.py:718
  263.1 12.3 %collective-permute-start.18 = (bf16[208,768]{1,0:T(8,128)(2,1)}, bf16[208,768]{1,0:T(8,128)(2,1)S(1)}, u32[]{:S(2)}, u32[]{:S(2)}) collective-permute-start(bf16[208,768]{1,0:T(8,128)(2,1)} %get-tuple-element.121), channel_id=1, source_target_pairs={{0,2},{1,3},{2,0},{3,1},{4,6},{5,7},{6,4},{7,5},{8,10},{9,11},{10,... | collective-permute-start | bytes 958472 | tf_op jit(solution)/shard_map/ppermute | solution.py:718
  264.4 11.1 %collective-permute-start.17 = (bf16[160,768]{1,0:T(8,128)(2,1)}, bf16[160,768]{1,0:T(8,128)(2,1)S(1)}, u32[]{:S(2)}, u32[]{:S(2)}) collective-permute-start(bf16[160,768]{1,0:T(8,128)(2,1)} %get-tuple-element.118), channel_id=1, source_target_pairs={{0,8},{1,9},{2,10},{3,11},{4,12},{5,13},{6,14},{7,15},{8,0},{9,1},... | collective-permute-start | bytes 737288 | tf_op jit(solution)/shard_map/ppermute | solution.py:718
  278.6 9.1 %collective-permute-start.27 = (bf16[192,384]{1,0:T(8,128)(2,1)}, bf16[192,384]{1,0:T(8,128)(2,1)S(1)}, u32[]{:S(2)}, u32[]{:S(2)}) collective-permute-start(bf16[192,384]{1,0:T(8,128)(2,1)} %get-tuple-element.136), channel_id=1, source_target_pairs={{0,16},{16,0},{1,17},{17,1},{2,18},{18,2},{3,19},{19,3},{4,20},{20... | collective-permute-start | bytes 442376 | tf_op jit(solution)/shard_map/ppermute | solution.py:722
  279.7 10.8 %collective-permute-start.20 = (bf16[64,768]{1,0:T(8,128)(2,1)}, bf16[64,768]{1,0:T(8,128)(2,1)S(1)}, u32[]{:S(2)}, u32[]{:S(2)}) collective-permute-start(bf16[64,768]{1,0:T(8,128)(2,1)} %get-tuple-element.127), channel_id=1, source_target_pairs={{0,4},{1,5},{2,6},{3,7},{4,0},{5,1},{6,2},{7,3},{8,12},{9,13},{10,... | collective-permute-start | bytes 294920 | tf_op jit(solution)/shard_map/ppermute | solution.py:718
  283.3 7.2 %collective-permute-start.21 = (bf16[64,768]{1,0:T(8,128)(2,1)}, bf16[64,768]{1,0:T(8,128)(2,1)S(1)}, u32[]{:S(2)}, u32[]{:S(2)}) collective-permute-start(bf16[64,768]{1,0:T(8,128)(2,1)} %get-tuple-element.128), channel_id=1, source_target_pairs={{0,8},{1,9},{2,10},{3,11},{4,12},{5,13},{6,14},{7,15},{8,0},{9,1},... | collective-permute-start | bytes 294920 | tf_op jit(solution)/shard_map/ppermute | solution.py:718
  283.3 9.4 %collective-permute-start.22 = (bf16[64,768]{1,0:T(8,128)(2,1)}, bf16[64,768]{1,0:T(8,128)(2,1)S(1)}, u32[]{:S(2)}, u32[]{:S(2)}) collective-permute-start(bf16[64,768]{1,0:T(8,128)(2,1)} %get-tuple-element.129), channel_id=1, source_target_pairs={{0,12},{1,13},{2,14},{3,15},{4,8},{5,9},{6,10},{7,11},{8,4},{9,5},... | collective-permute-start | bytes 294920 | tf_op jit(solution)/shard_map/ppermute | solution.py:718
  284.9 11.3 %collective-permute-start.19 = (bf16[176,768]{1,0:T(8,128)(2,1)}, bf16[176,768]{1,0:T(8,128)(2,1)S(1)}, u32[]{:S(2)}, u32[]{:S(2)}) collective-permute-start(bf16[176,768]{1,0:T(8,128)(2,1)} %get-tuple-element.124), channel_id=1, source_target_pairs={{0,4},{1,5},{2,6},{3,7},{4,0},{5,1},{6,2},{7,3},{8,12},{9,13},{10,... | collective-permute-start | bytes 811016 | tf_op jit(solution)/shard_map/ppermute | solution.py:718
  287.7 8.5 %collective-permute-start.23 = (bf16[240,768]{1,0:T(8,128)(2,1)}, bf16[240,768]{1,0:T(8,128)(2,1)S(1)}, u32[]{:S(2)}, u32[]{:S(2)}) collective-permute-start(bf16[240,768]{1,0:T(8,128)(2,1)} %reduce-scatter.2.cloned.1.call-done), channel_id=1, source_target_pairs={{0,16},{16,0},{1,17},{17,1},{2,18},{18,2},{3,19},{19,3},{4,20},{20... | collective-permute-start | bytes 1105928 | tf_op jit(solution)/shard_map/ppermute | solution.py:722
  303.9 7.0 %collective-permute-start.24 = (bf16[2,2,2,2,2,8,768]{6,5,4,2,0,1,3:T(8,128)(2,1)S(1)}, bf16[2,2,2,2,2,8,768]{6,5,4,2,0,1,3:T(8,128)(2,1)S(1)}, u32[]{:S(2)}, u32[]{:S(2)}) collective-permute-start(bf16[2,2,2,2,2,8,768]{6,5,4,2,0,1,3:T(8,128)(2,1)S(1)} %copy.62), channel_id=1, source_target_pairs={{0,1},{1,0},{2,3},{3,2},{4,5},{5,4},{6,7},{7,6},{8,9},{9,8},{10,11... | collective-permute-start | bytes 1179656 | tf_op jit(solution)/shard_map/ppermute | solution.py:718
  (40 other events, 145.6 us)
Sparse Core Ops, SparseCore 0:
  12.0 89.7 all-gather.1
  162.0 86.6 reduce-scatter.1

commit v6 on v5

--- a/solution.py
+++ b/solution.py
@@ -1015,11 +1015,15 @@
     grad_w_qkv = jnp.concatenate(
         [p[:, i * GW : (i + 1) * GW] for i in range(3) for p in parts], axis=1
     )
+    by_owner, start = [], 0
+    for size in SMALL_SIZES:
+        by_owner.append(lines[start // D : (start + size) // D].reshape(ranks, -1))
+        start += size
+    mine = lax.dynamic_index_in_dim(jnp.concatenate(by_owner, axis=1), me, keepdims=False)
     small_grads, start = {}, 0
     for name, size in zip(SMALL, SMALL_SIZES):
-        values = lines[start // D : (start + size) // D].reshape(ranks, -1)
-        small_grads[name] = lax.dynamic_index_in_dim(values, me, keepdims=False)
-        start += size
+        small_grads[name] = mine[start : start + size // ranks]
+        start += size // ranks
     return (
         layer_out,
         input_grad,

time: 325 us -> 325 us (level)
  transfers between devices with their start and end apart: 30 -> 30, of which waited for: 15 -> 14; matrix products, arithmetic and copies ran while one was open for 4% -> 4% of each run, Pallas kernels for 35% -> 35%
where the time goes in v6:
time: 325 us; the launch traced here: 320 us
  Pallas kernels  176 us (54%)
  waiting for transfers between devices  73.7 us (23%)
  starting transfers between devices  30.1 us (9%)
  local copies, waits for them, and re-layouts  18.9 us (6%)
  between operations  14.7 us (5%)
  other arithmetic  6.82 us (2%)
    pallas_call x16, Pallas kernels, call(): pl.pallas_call(run, grid_spec=pltpu.PrefetchScalarGridSpec(num_scalar_pre...  176 us
    ppermute x21, waiting for transfers between devices, swap(): return lax.ppermute(x, 'fsdp', [(i, i ^ mask) for i in range(RANKS)])  48.1 us
    ppermute x7, waiting for transfers between devices, swap_replica(): return lax.ppermute(x, 'replica', [(0, 1), (1, 0)])  25.5 us
    ppermute x21, starting transfers between devices, swap(): return lax.ppermute(x, 'fsdp', [(i, i ^ mask) for i in range(RANKS)])  21.4 us
    ppermute x7, starting transfers between devices, swap_replica(): return lax.ppermute(x, 'replica', [(0, 1), (1, 0)])  8.64 us
    unnamed x76, local copies, waits for them, and re-layouts  7.95 us
  transfers between devices with their start and end apart: 30, of which 14 were waited for; matrix products, arithmetic and copies ran while one was open for 4% of the time, Pallas kernels for 35%

profile of v6, /device:TPU:20, one launch (start us, length us, event | category | flops | bytes accessed | tf_op | source)
XLA Modules:
  0.0 320.2 jit_solution(195531921168381412)
XLA Ops:
  9.0 2.8 shard_map.262
  12.5 3.5 %collective-permute-start.1 = (bf16[48,1280]{1,0:T(8,128)(2,1)}, bf16[48,1280]{1,0:T(8,128)(2,1)S(1)}, u32[]{:S(2)}, u32[]{:S(2)}) collective-permute-start(bf16[48,1280]{1,0:T(8,128)(2,1)} %get-tuple-element.76), channel_id=1, source_target_pairs={{0,8},{1,9},{2,10},{3,11},{4,12},{5,13},{6,14},{7,15},{8,0},{9,1},... | collective-permute-start | bytes 368648 | tf_op jit(solution)/shard_map/ppermute | solution.py:718
  16.0 8.6 %collective-permute-done.2 = bf16[48,1280]{1,0:T(8,128)(2,1)S(1)} collective-permute-done((bf16[48,1280]{1,0:T(8,128)(2,1)}, bf16[48,1280]{1,0:T(8,128)(2,1)S(1)}, u32[]{:S(2)}, u32[]{:S(2)}) %collective-permute-start.2) | collective-permute-done | bytes 122912 | tf_op jit(solution)/shard_map/ppermute | solution.py:718
  26.6 14.1 %collective-permute-done.3 = bf16[4,48,1280]{2,1,0:T(8,128)(2,1)S(1)} collective-permute-done((bf16[4,48,1280]{2,1,0:T(8,128)(2,1)S(1)}, bf16[4,48,1280]{2,1,0:T(8,128)(2,1)S(1)}, u32[]{:S(2)}, u32[]{:S(2)}) %collective-permute-start.3) | collective-permute-done | bytes 491552 | tf_op jit(solution)/shard_map/ppermute | solution.py:718
  42.3 21.2 %collective-permute-done.4.refs_2_ = bf16[2,4,48,1280]{3,2,1,0:T(8,128)(2,1)S(1)} collective-permute-done((bf16[2,4,48,1280]{3,2,1,0:T(8,128)(2,1)S(1)}, bf16[2,4,48,1280]{3,2,1,0:T(8,128)(2,1)S(1)}, u32[]{:S(2)}, u32[]{:S(2)}) %collective-permute-start.4) | collective-permute-done | bytes 983072 | tf_op jit(solution)/shard_map/ppermute | solution.py:722
  67.0 5.0 %shard_map.263.refs_2_.refs_3_.refs_4_ = bf16[768,2560]{1,0:T(8,128)(2,1)} custom-call(s32[2]{0:T(128)} %pad_add_fusion.refs_0_, bf16[2,4,48,1280]{3,2,1,0:T(8,128)(2,1)} %copy-done.1, bf16[2,4,48,1280]{3,2,1,0:T(8,128)(2,1)} %copy-done.16, bf16[2,4,48,1280]{3,2,1,0:T(8,128)(2,1)} %copy-done.17, bf16[2,4,48,1280]{3,2,1,0:T(8,128)(2,1)} %copy-done.18), custom_call_target="tpu_custom_call" | custom-call | flops 4600000000 | bytes 14400000 | tf_op jit(solution)/shard_map/pallas_call | solution.py:58
  75.9 27.8 %shard_map.264 = (bf16[1024,768]{1,0:T(8,128)(2,1)}, bf16[1024,768]{1,0:T(8,128)(2,1)}, bf16[1024,768]{1,0:T(8,128)(2,1)}, bf16[6,2,4,384,256]{4,3,2,1,0:T(8,128)(2,1)}, bf16[1024,768]{1,0:T(8,128)(2,1)}) custom-call(s32[2,8]{1,0:T(2,128)} %refs_0_.3, bf16[1024,768]{1,0:T(8,128)(2,1)} %refs_2_.5, bf16[768,2560]{1,0:T(8,128)(2,1)} %shard_map.263.refs_2_.refs_3_.refs_4_, ...), custom_call_target="tpu_custom_call" | custom-call | flops 32199999488 | bytes 100800000 | tf_op jit(solution)/shard_map/pallas_call | solution.py:58
  103.7 46.1 %shard_map.265 = (bf16[1024,768]{1,0:T(8,128)(2,1)}, bf16[1024,768]{1,0:T(8,128)(2,1)}, bf16[1024,3072]{1,0:T(8,128)(2,1)}, bf16[1024,768]{1,0:T(8,128)(2,1)}, b...) custom-call(s32[2,8]{1,0:T(2,128)} %refs_0_.3, ...), custom_call_target="tpu_custom_call" | custom-call | flops 51749998592 | bytes 162000000 | tf_op jit(solution)/shard_map/pallas_call | solution.py:58
  149.8 12.2 %shard_map.266.refs_3_ = bf16[16,240,768]{2,1,0:T(8,128)(2,1)} custom-call(bf16[1024,3072]{1,0:T(8,128)(2,1)} %get-tuple-element.88.refs_0_, bf16[1024,768]{1,0:T(8,128)(2,1)} %get-tuple-element.89.refs_1_, bf16[1024,768]{1,0:T(8,128)(2,1)} %get-tuple-element.77.refs_2_.refs_3_, bf16[1024,768]{1,0:T(8,128)(2,1)} %get-tuple-element.81.refs_3_.refs_1_), custom_call_target="tpu_custom_call" | custom-call | flops 12650000384 | bytes 39600000 | tf_op jit(solution)/shard_map/pallas_call | solution.py:58
  162.0 10.9 %shard_map.267 = (bf16[2,2,4,192,384]{4,3,2,1,0:T(8,128)(2,1)}, bf16[2,2,4,192,384]{4,3,2,1,0:T(8,128)(2,1)}) custom-call(s32[2]{0:T(128)} %pad_add_fusion.refs_0_, bf16[1024,768]{1,0:T(8,128)(2,1)} %get-tuple-element.86.refs_1_, bf16[1024,3072]{1,0:T(8,128)(2,1)} %get-tuple-element.87.refs_2_, bf16[16,240,768]{2,1,0:T(8,128)(2,1)} %shard_map.266.refs_3_), custom_call_target="tpu_custom_call" | custom-call | flops 12650000384 | bytes 39600000 | tf_op jit(solution)/shard_map/pallas_call | solution.py:58
  173.2 4.6 %collective-permute-done.7.refs_1_ = bf16[3072,384]{1,0:T(8,128)(2,1)S(1)} collective-permute-done((bf16[3072,384]{1,0:T(8,128)(2,1)}, bf16[3072,384]{1,0:T(8,128)(2,1)S(1)}, u32[]{:S(2)}, u32[]{:S(2)}) %collective-permute-start.7) | collective-permute-done | bytes 2359328 | tf_op jit(solution)/shard_map/ppermute | solution.py:718
  179.2 4.4 %shard_map.268 = (bf16[1536,384]{1,0:T(8,128)(2,1)}, bf16[1536,384]{1,0:T(8,128)(2,1)}) custom-call(bf16[3072,384]{1,0:T(8,128)(2,1)} %bitcast.107, bf16[3072,384]{1,0:T(8,128)(2,1)} %copy-done.13), custom_call_target="tpu_custom_call" | custom-call | flops 2300000000 | bytes 7200000 | tf_op jit(solution)/shard_map/pallas_call | solution.py:58
  185.0 25.8 %shard_map.269 = (bf16[1024,1536]{1,0:T(8,128)(2,1)}, f32[2,512]{1,0:T(2,128)}, bf16[2,2,4,48,768]{4,3,2,1,0:T(8,128)(2,1)}, bf16[2,2,4,48,768]{4,3,2,1,0:T(8,128)(2,1)}) custom-call(s32[2]{0:T(128)} %pad_add_fusion.refs_0_, bf16[1024,768]{1,0:T(8,128)(2,1)} %get-tuple-element.81.refs_3_.refs_1_, bf16[1024,768]{1,0:T(8,128)(2,1)} %refs_2_.5, ...), custom_call_target="tpu_custom_call" | custom-call | flops 1150000000 | bytes 3600000 | tf_op jit(solution)/shard_map/pallas_call | solution.py:58
  212.9 2.9 shard_map.270
  220.0 3.0 shard_map.271
  226.3 15.9 %shard_map.272 = (bf16[1024,768]{1,0:T(8,128)(2,1)}, f32[2,256]{1,0:T(2,128)}, bf16[2,4,48,768]{3,2,1,0:T(8,128)(2,1)}, bf16[2,4,48,768]{3,2,1,0:T(8,128)(2,1)}) custom-call(s32[2]{0:T(128)} %pad_add_fusion.refs_0_, bf16[1024,768]{1,0:T(8,128)(2,1)} %get-tuple-element.81.refs_3_.refs_1_, bf16[1024,768]{1,0:T(8,128)(2,1)} %refs_2_.5, ...), custom_call_target="tpu_custom_call" | custom-call | flops 1150000000 | bytes 3600000 | tf_op jit(solution)/shard_map/pallas_call | solution.py:58
  249.0 9.0 %shard_map.274.refs_9_ = f32[1024,768]{1,0:T(8,128)} custom-call(f32[1024,768]{1,0:T(8,128)} %get-tuple-element.80.refs_0_, bf16[1024,1536]{1,0:T(8,128)(2,1)} %get-tuple-element.93.refs_1_, bf16[1024,768]{1,0:T(8,128)(2,1)} %get-tuple-element.101.refs_2_, bf16[768,2560]{1,0:T(8,128)(2,1)} %shard_map.263.refs_2_.refs_3_.refs_4_, ...), custom_call_target="tpu_custom_call" | custom-call | flops 10350000128 | bytes 32400000 | tf_op jit(solution)/shard_map/pallas_call | solution.py:58
  260.4 2.8 shard_map.275
  264.4 3.3 %collective-permute-start.17 = (bf16[160,768]{1,0:T(8,128)(2,1)}, bf16[160,768]{1,0:T(8,128)(2,1)S(1)}, u32[]{:S(2)}, u32[]{:S(2)}) collective-permute-start(bf16[160,768]{1,0:T(8,128)(2,1)} %get-tuple-element.118), channel_id=1, source_target_pairs={{0,8},{1,9},{2,10},{3,11},{4,12},{5,13},{6,14},{7,15},{8,0},{9,1},... | collective-permute-start | bytes 737288 | tf_op jit(solution)/shard_map/ppermute | solution.py:718
  267.7 7.0 %collective-permute-done.16.refs_1_ = bf16[192,384]{1,0:T(8,128)(2,1)S(1)} collective-permute-done((bf16[192,384]{1,0:T(8,128)(2,1)}, bf16[192,384]{1,0:T(8,128)(2,1)S(1)}, u32[]{:S(2)}, u32[]{:S(2)}) %collective-permute-start.16) | collective-permute-done | bytes 147488 | tf_op jit(solution)/shard_map/ppermute | solution.py:718
  280.2 3.6 %collective-permute-start.20 = (bf16[64,768]{1,0:T(8,128)(2,1)}, bf16[64,768]{1,0:T(8,128)(2,1)S(1)}, u32[]{:S(2)}, u32[]{:S(2)}) collective-permute-start(bf16[64,768]{1,0:T(8,128)(2,1)} %get-tuple-element.127), channel_id=1, source_target_pairs={{0,4},{1,5},{2,6},{3,7},{4,0},{5,1},{6,2},{7,3},{8,12},{9,13},{10,... | collective-permute-start | bytes 294920 | tf_op jit(solution)/shard_map/ppermute | solution.py:718
  285.3 2.8 collective-permute-start.19
  293.2 3.4 %collective-permute-done.19.refs_1_ = bf16[176,768]{1,0:T(8,128)(2,1)S(1)} collective-permute-done((bf16[176,768]{1,0:T(8,128)(2,1)}, bf16[176,768]{1,0:T(8,128)(2,1)S(1)}, u32[]{:S(2)}, u32[]{:S(2)}) %collective-permute-start.19) | collective-permute-done | bytes 270368 | tf_op jit(solution)/shard_map/ppermute | solution.py:718
  304.6 3.2 %collective-permute-done.26 = bf16[64,768]{1,0:T(8,128)(2,1)S(1)} collective-permute-done((bf16[64,768]{1,0:T(8,128)(2,1)S(1)}, bf16[64,768]{1,0:T(8,128)(2,1)S(1)}, u32[]{:S(2)}, u32[]{:S(2)}) %collective-permute-start.26) | collective-permute-done | bytes 98336 | tf_op jit(solution)/shard_map/ppermute | solution.py:722
  (197 shorter events, 61.6 us)
Async XLA Ops:
  7.2 96.5 %all-gather.2.cloned.1.call-start = ((), (), s32[]{:S(2)}) async-start(), calls=%async_computation.1 | async-start | bytes 11280384 | tf_op jit(solution)/shard_map/all_gather | solution.py:908
  11.9 276.3 %reduce-scatter.2.cloned.1.call-start = ((), (), s32[]{:S(2)}) async-start(), calls=%async_computation.2 | async-start | bytes 6266880 | tf_op jit(solution)/shard_map/reduce_scatter | solution.py:940
  12.0 12.6 %collective-permute-start.2 = (bf16[48,1280]{1,0:T(8,128)(2,1)}, bf16[48,1280]{1,0:T(8,128)(2,1)S(1)}, u32[]{:S(2)}, u32[]{:S(2)}) collective-permute-start(bf16[48,1280]{1,0:T(8,128)(2,1)} %get-tuple-element.76), channel_id=1, source_target_pairs={{0,12},{1,13},{2,14},{3,15},{4,8},{5,9},{6,10},{7,11},{8,4},{9,5},... | collective-permute-start | bytes 368648 | tf_op jit(solution)/shard_map/ppermute | solution.py:718
  12.5 12.6 %collective-permute-start.1 = (bf16[48,1280]{1,0:T(8,128)(2,1)}, bf16[48,1280]{1,0:T(8,128)(2,1)S(1)}, u32[]{:S(2)}, u32[]{:S(2)}) collective-permute-start(bf16[48,1280]{1,0:T(8,128)(2,1)} %get-tuple-element.76), channel_id=1, source_target_pairs={{0,8},{1,9},{2,10},{3,11},{4,12},{5,13},{6,14},{7,15},{8,0},{9,1},... | collective-permute-start | bytes 368648 | tf_op jit(solution)/shard_map/ppermute | solution.py:718
  16.0 9.2 %collective-permute-start = (bf16[48,1280]{1,0:T(8,128)(2,1)}, bf16[48,1280]{1,0:T(8,128)(2,1)S(1)}, u32[]{:S(2)}, u32[]{:S(2)}) collective-permute-start(bf16[48,1280]{1,0:T(8,128)(2,1)} %get-tuple-element.76), channel_id=1, source_target_pairs={{0,4},{1,5},{2,6},{3,7},{4,0},{5,1},{6,2},{7,3},{8,12},{9,13},{10,... | collective-permute-start | bytes 368648 | tf_op jit(solution)/shard_map/ppermute | solution.py:718
  26.1 14.6 %collective-permute-start.3 = (bf16[4,48,1280]{2,1,0:T(8,128)(2,1)S(1)}, bf16[4,48,1280]{2,1,0:T(8,128)(2,1)S(1)}, u32[]{:S(2)}, u32[]{:S(2)}) collective-permute-start(bf16[4,48,1280]{2,1,0:T(8,128)(2,1)S(1)} %get-tuple-element.150), channel_id=1, source_target_pairs={{0,2},{1,3},{2,0},{3,1},{4,6},{5,7},{6,4},{7,5},{8,10},{9,11},{10,... | collective-permute-start | bytes 1474568 | tf_op jit(solution)/shard_map/ppermute | solution.py:718
  40.8 22.7 %collective-permute-start.4 = (bf16[2,4,48,1280]{3,2,1,0:T(8,128)(2,1)S(1)}, bf16[2,4,48,1280]{3,2,1,0:T(8,128)(2,1)S(1)}, u32[]{:S(2)}, u32[]{:S(2)}) collective-permute-start(bf16[2,4,48,1280]{3,2,1,0:T(8,128)(2,1)S(1)} %pad_maximum_fusion.refs_1_), channel_id=1, source_target_pairs={{0,16},{16,0},{1,17},{17,1},{2,18},{18,2},{3,19},{19,3},{4,20},{20... | collective-permute-start | bytes 2949128 | tf_op jit(solution)/shard_map/ppermute | solution.py:722
  42.3 21.2 %collective-permute-start.5 = (bf16[2,4,48,1280]{3,2,1,0:T(8,128)(2,1)S(1)}, bf16[2,4,48,1280]{3,2,1,0:T(8,128)(2,1)S(1)}, u32[]{:S(2)}, u32[]{:S(2)}) collective-permute-start(bf16[2,4,48,1280]{3,2,1,0:T(8,128)(2,1)S(1)} %pad_maximum_fusion.refs_1_), channel_id=1, source_target_pairs={{0,1},{1,0},{2,3},{3,2},{4,5},{5,4},{6,7},{7,6},{8,9},{9,8},{10,11... | collective-permute-start | bytes 2949128 | tf_op jit(solution)/shard_map/ppermute | solution.py:718
  183.5 28.4 %collective-permute-start.8 = (bf16[1536,384]{1,0:T(8,128)(2,1)}, bf16[1536,384]{1,0:T(8,128)(2,1)S(1)}, u32[]{:S(2)}, u32[]{:S(2)}) collective-permute-start(bf16[1536,384]{1,0:T(8,128)(2,1)} %get-tuple-element.92.refs_9_), channel_id=1, source_target_pairs={{0,16},{16,0},{1,17},{17,1},{2,18},{18,2},{3,19},{19,3},{4,20},{20... | collective-permute-start | bytes 3538952 | tf_op jit(solution)/shard_map/ppermute | solution.py:722
  222.9 20.6 %collective-permute-start.11 = (bf16[400,768]{1,0:T(8,128)(2,1)}, bf16[400,768]{1,0:T(8,128)(2,1)S(1)}, u32[]{:S(2)}, u32[]{:S(2)}) collective-permute-start(bf16[400,768]{1,0:T(8,128)(2,1)} %get-tuple-element.100.refs_9_), channel_id=1, source_target_pairs={{0,16},{16,0},{1,17},{17,1},{2,18},{18,2},{3,19},{19,3},{4,20},{20... | collective-permute-start | bytes 1843208 | tf_op jit(solution)/shard_map/ppermute | solution.py:722
  224.4 19.0 %collective-permute-start.10 = (bf16[768,384]{1,0:T(8,128)(2,1)S(1)}, bf16[768,384]{1,0:T(8,128)(2,1)S(1)}, u32[]{:S(2)}, u32[]{:S(2)}) collective-permute-start(bf16[768,384]{1,0:T(8,128)(2,1)S(1)} %copy-done.20), channel_id=1, source_target_pairs={{0,2},{1,3},{2,0},{3,1},{4,6},{5,7},{6,4},{7,5},{8,10},{9,11},{10,... | collective-permute-start | bytes 1769480 | tf_op jit(solution)/shard_map/ppermute | solution.py:718
  242.9 15.2 %collective-permute-start.15 = (bf16[16,768]{1,0:T(8,128)(2,1)S(1)}, bf16[16,768]{1,0:T(8,128)(2,1)S(1)}, u32[]{:S(2)}, u32[]{:S(2)}) collective-permute-start(bf16[16,768]{1,0:T(8,128)(2,1)S(1)} %fusion.8.refs_8_), channel_id=1, source_target_pairs={{0,1},{1,0},{2,3},{3,2},{4,5},{5,4},{6,7},{7,6},{8,9},{9,8},{10,11... | collective-permute-start | bytes 73736 | tf_op jit(solution)/shard_map/ppermute | solution.py:718
  243.0 15.1 %collective-permute-start.14 = (bf16[384,768]{1,0:T(8,128)(2,1)}, bf16[384,768]{1,0:T(8,128)(2,1)S(1)}, u32[]{:S(2)}, u32[]{:S(2)}) collective-permute-start(bf16[384,768]{1,0:T(8,128)(2,1)} %bitcast.99), channel_id=1, source_target_pairs={{0,1},{1,0},{2,3},{3,2},{4,5},{5,4},{6,7},{7,6},{8,9},{9,8},{10,11... | collective-permute-start | bytes 1769480 | tf_op jit(solution)/shard_map/ppermute | solution.py:718
  247.3 12.3 %collective-permute-start.12 = (bf16[384,384]{1,0:T(8,128)(2,1)}, bf16[384,384]{1,0:T(8,128)(2,1)S(1)}, u32[]{:S(2)}, u32[]{:S(2)}) collective-permute-start(bf16[384,384]{1,0:T(8,128)(2,1)} %get-tuple-element.108), channel_id=1, source_target_pairs={{0,8},{1,9},{2,10},{3,11},{4,12},{5,13},{6,14},{7,15},{8,0},{9,1},... | collective-permute-start | bytes 884744 | tf_op jit(solution)/shard_map/ppermute | solution.py:718
  247.3 12.3 %collective-permute-start.13 = (bf16[224,768]{1,0:T(8,128)(2,1)}, bf16[224,768]{1,0:T(8,128)(2,1)S(1)}, u32[]{:S(2)}, u32[]{:S(2)}) collective-permute-start(bf16[224,768]{1,0:T(8,128)(2,1)} %get-tuple-element.106.refs_4_), channel_id=1, source_target_pairs={{0,2},{1,3},{2,0},{3,1},{4,6},{5,7},{6,4},{7,5},{8,10},{9,11},{10,... | collective-permute-start | bytes 1032200 | tf_op jit(solution)/shard_map/ppermute | solution.py:718
  263.2 12.7 %collective-permute-start.18 = (bf16[208,768]{1,0:T(8,128)(2,1)}, bf16[208,768]{1,0:T(8,128)(2,1)S(1)}, u32[]{:S(2)}, u32[]{:S(2)}) collective-permute-start(bf16[208,768]{1,0:T(8,128)(2,1)} %get-tuple-element.121), channel_id=1, source_target_pairs={{0,2},{1,3},{2,0},{3,1},{4,6},{5,7},{6,4},{7,5},{8,10},{9,11},{10,... | collective-permute-start | bytes 958472 | tf_op jit(solution)/shard_map/ppermute | solution.py:718
  264.4 11.4 %collective-permute-start.17 = (bf16[160,768]{1,0:T(8,128)(2,1)}, bf16[160,768]{1,0:T(8,128)(2,1)S(1)}, u32[]{:S(2)}, u32[]{:S(2)}) collective-permute-start(bf16[160,768]{1,0:T(8,128)(2,1)} %get-tuple-element.118), channel_id=1, source_target_pairs={{0,8},{1,9},{2,10},{3,11},{4,12},{5,13},{6,14},{7,15},{8,0},{9,1},... | collective-permute-start | bytes 737288 | tf_op jit(solution)/shard_map/ppermute | solution.py:718
  267.7 7.0 %collective-permute-start.16 = (bf16[192,384]{1,0:T(8,128)(2,1)}, bf16[192,384]{1,0:T(8,128)(2,1)S(1)}, u32[]{:S(2)}, u32[]{:S(2)}) collective-permute-start(bf16[192,384]{1,0:T(8,128)(2,1)} %get-tuple-element.116), channel_id=1, source_target_pairs={{0,4},{1,5},{2,6},{3,7},{4,0},{5,1},{6,2},{7,3},{8,12},{9,13},{10,... | collective-permute-start | bytes 442376 | tf_op jit(solution)/shard_map/ppermute | solution.py:718
  279.0 9.2 %collective-permute-start.27 = (bf16[192,384]{1,0:T(8,128)(2,1)}, bf16[192,384]{1,0:T(8,128)(2,1)S(1)}, u32[]{:S(2)}, u32[]{:S(2)}) collective-permute-start(bf16[192,384]{1,0:T(8,128)(2,1)} %get-tuple-element.136), channel_id=1, source_target_pairs={{0,16},{16,0},{1,17},{17,1},{2,18},{18,2},{3,19},{19,3},{4,20},{20... | collective-permute-start | bytes 442376 | tf_op jit(solution)/shard_map/ppermute | solution.py:722
  280.2 10.7 %collective-permute-start.20 = (bf16[64,768]{1,0:T(8,128)(2,1)}, bf16[64,768]{1,0:T(8,128)(2,1)S(1)}, u32[]{:S(2)}, u32[]{:S(2)}) collective-permute-start(bf16[64,768]{1,0:T(8,128)(2,1)} %get-tuple-element.127), channel_id=1, source_target_pairs={{0,4},{1,5},{2,6},{3,7},{4,0},{5,1},{6,2},{7,3},{8,12},{9,13},{10,... | collective-permute-start | bytes 294920 | tf_op jit(solution)/shard_map/ppermute | solution.py:718
  283.8 7.2 %collective-permute-start.21 = (bf16[64,768]{1,0:T(8,128)(2,1)}, bf16[64,768]{1,0:T(8,128)(2,1)S(1)}, u32[]{:S(2)}, u32[]{:S(2)}) collective-permute-start(bf16[64,768]{1,0:T(8,128)(2,1)} %get-tuple-element.128), channel_id=1, source_target_pairs={{0,8},{1,9},{2,10},{3,11},{4,12},{5,13},{6,14},{7,15},{8,0},{9,1},... | collective-permute-start | bytes 294920 | tf_op jit(solution)/shard_map/ppermute | solution.py:718
  283.8 9.4 %collective-permute-start.22 = (bf16[64,768]{1,0:T(8,128)(2,1)}, bf16[64,768]{1,0:T(8,128)(2,1)S(1)}, u32[]{:S(2)}, u32[]{:S(2)}) collective-permute-start(bf16[64,768]{1,0:T(8,128)(2,1)} %get-tuple-element.129), channel_id=1, source_target_pairs={{0,12},{1,13},{2,14},{3,15},{4,8},{5,9},{6,10},{7,11},{8,4},{9,5},... | collective-permute-start | bytes 294920 | tf_op jit(solution)/shard_map/ppermute | solution.py:718
  285.3 11.3 %collective-permute-start.19 = (bf16[176,768]{1,0:T(8,128)(2,1)}, bf16[176,768]{1,0:T(8,128)(2,1)S(1)}, u32[]{:S(2)}, u32[]{:S(2)}) collective-permute-start(bf16[176,768]{1,0:T(8,128)(2,1)} %get-tuple-element.124), channel_id=1, source_target_pairs={{0,4},{1,5},{2,6},{3,7},{4,0},{5,1},{6,2},{7,3},{8,12},{9,13},{10,... | collective-permute-start | bytes 811016 | tf_op jit(solution)/shard_map/ppermute | solution.py:718
  288.2 8.5 %collective-permute-start.23 = (bf16[240,768]{1,0:T(8,128)(2,1)}, bf16[240,768]{1,0:T(8,128)(2,1)S(1)}, u32[]{:S(2)}, u32[]{:S(2)}) collective-permute-start(bf16[240,768]{1,0:T(8,128)(2,1)} %reduce-scatter.2.cloned.1.call-done), channel_id=1, source_target_pairs={{0,16},{16,0},{1,17},{17,1},{2,18},{18,2},{3,19},{19,3},{4,20},{20... | collective-permute-start | bytes 1105928 | tf_op jit(solution)/shard_map/ppermute | solution.py:722
  (40 other events, 145.6 us)
Sparse Core Ops, SparseCore 0:
  12.0 89.7 all-gather.1
  162.1 87.3 reduce-scatter.1
